TPU v7x, 32 devices: a whole 2x2x4 slice. The times are simulated.
32 devices in a mesh: dp: 4 (over y, x), tok: 8 (over z, core).
Axes of the slice: x: 2, y: 2, z: 4, core: 2. Of those that a mesh axis runs over, the one named last changes fastest.
Arguments:
- encoder_input: bfloat16 [32, 512, 768], P(('dp', 'tok')), may hold values from -6 to 6
- decoder_input: bfloat16 [64, 768], P(('dp', 'tok')), may hold values from -6 to 6
- output_cotangent: bfloat16 [64, 768], P(('dp', 'tok')), may hold values from -6 to 6
- pair_lengths: int32 [32, 8], P(('dp', 'tok')), may hold values from 1 to 128, 512 in all within a row
- pair_offset: int32 [4, 8], P('dp'), may hold values from 0 to 7, as said below
- pair_query: int32 [4, 8], P('dp'), may hold values from 0 to 1, as said below
- attention_master: float32 [6, 768, 768], P(None, ('dp', 'tok')), may hold values from -0.21875 to 0.21875
- attention_moment: float32 [6, 768, 768], P(None, ('dp', 'tok')), may hold values from -24 to 24
- attention_average: float32 [6, 768, 768], P(None, ('dp', 'tok')), may hold values from -0.21875 to 0.21875
- feedforward_master: float32 [2, 768, 3072], P(None, ('dp', 'tok')), may hold values from -0.21875 to 0.21875
- feedforward_moment: float32 [2, 768, 3072], P(None, ('dp', 'tok')), may hold values from -24 to 24
- feedforward_average: float32 [2, 768, 3072], P(None, ('dp', 'tok')), may hold values from -0.21875 to 0.21875
- decoder_master: float32 [4, 768, 768], P(None, ('dp', 'tok')), may hold values from -0.21875 to 0.21875
- decoder_moment: float32 [4, 768, 768], P(None, ('dp', 'tok')), may hold values from -6 to 6
- decoder_average: float32 [4, 768, 768], P(None, ('dp', 'tok')), may hold values from -0.21875 to 0.21875
- expansion_master: float32 [2, 768, 3072], P(None, ('dp', 'tok')), may hold values from -0.21875 to 0.21875
- expansion_moment: float32 [2, 768, 3072], P(None, ('dp', 'tok')), may hold values from -6 to 6
- expansion_average: float32 [2, 768, 3072], P(None, ('dp', 'tok')), may hold values from -0.21875 to 0.21875
- gain_master: float32 [5, 768], replicated, may hold values from 0.5 to 1.5
- gain_moment: float32 [5, 768], replicated, may hold values from -40 to 40
- gain_average: float32 [5, 768], replicated, may hold values from 0.5 to 1.5
- bias_master: float32 [32, 12], replicated, may hold values from -4 to 4
- bias_moment: float32 [32, 12], replicated, may hold values from -16 to 16
- bias_average: float32 [32, 12], replicated, may hold values from -4 to 4
Outputs:
- decoder_output: float32 [64, 768], P(('dp', 'tok'))
- encoder_gradient: float32 [32, 512, 768], P(('dp', 'tok'))
- decoder_gradient: float32 [64, 768], P(('dp', 'tok'))
- attention_momentum: float32 [6, 768, 768], P(None, ('dp', 'tok'))
- attention_averaged: float32 [6, 768, 768], P(None, ('dp', 'tok'))
- attention_updated: float32 [6, 768, 768], P(None, ('dp', 'tok'))
- attention_copy: bfloat16 [6, 768, 768], P(None, ('dp', 'tok'))
- feedforward_momentum: float32 [2, 768, 3072], P(None, ('dp', 'tok'))
- feedforward_averaged: float32 [2, 768, 3072], P(None, ('dp', 'tok'))
- feedforward_updated: float32 [2, 768, 3072], P(None, ('dp', 'tok'))
- feedforward_copy: bfloat16 [2, 768, 3072], P(None, ('dp', 'tok'))
- decoder_momentum: float32 [4, 768, 768], P(None, ('dp', 'tok'))
- decoder_averaged: float32 [4, 768, 768], P(None, ('dp', 'tok'))
- decoder_updated: float32 [4, 768, 768], P(None, ('dp', 'tok'))
- decoder_copy: bfloat16 [4, 768, 768], P(None, ('dp', 'tok'))
- expansion_momentum: float32 [2, 768, 3072], P(None, ('dp', 'tok'))
- expansion_averaged: float32 [2, 768, 3072], P(None, ('dp', 'tok'))
- expansion_updated: float32 [2, 768, 3072], P(None, ('dp', 'tok'))
- expansion_copy: bfloat16 [2, 768, 3072], P(None, ('dp', 'tok'))
- gain_momentum: float32 [5, 768], replicated
- gain_averaged: float32 [5, 768], replicated
- gain_updated: float32 [5, 768], replicated
- gain_copy: bfloat16 [5, 768], replicated
- bias_momentum: float32 [32, 12], replicated
- bias_averaged: float32 [32, 12], replicated
- bias_updated: float32 [32, 12], replicated
- bias_copy: bfloat16 [32, 12], replicated
Inputs may be any that keep to these rules, and one draw needn't show every extreme that they name: Each row is a permutation of the 8 values i and 4 + i for i below 4; pair k of the row on tok index t goes to tok index (t + pair_offset[n, k]) mod 8 of the same dp index n, so every device receives exactly 8 pairs, one from each of 8 devices. `pair_query`: each value appears exactly 4 times in a row. `pair_lengths`: each row's lengths sum to 512.
All inputs are finite; a program needn't handle non-finite values.
Results may differ from a plain program's by a relative error of at most 0.025.
The roundings to bfloat16 on the way count: a program that leaves them out, or rounds other values in their place, can miss the bound.
Values may be sent and summed in bfloat16 or wider, within the bound.
No kernel may reach another device: no remote copies, remote signals or barrier semaphores. Data moves between devices by JAX's collectives and lax.ppermute only.
A program may use at most 320 MiB of HBM per device.

v0:
```python
import jax
import jax.numpy as jnp
from jax import lax
from jax.sharding import PartitionSpec as P

EPSILON = 1e-06
SCALING = 0.125
NEGATIVE = -1e30
MOMENTUM = 0.5
AVERAGING = 0.5
RATE = 0.02
THRESHOLDS = (12, 16, 23, 32, 46, 64, 91)


def bucket_ids(relative):
    magnitude = jnp.abs(relative)
    bucket = jnp.minimum(magnitude, 8)
    for limit in THRESHOLDS:
        bucket = bucket + (magnitude >= limit).astype(jnp.int32)
    return bucket + 16 * (relative > 0).astype(jnp.int32)


def rms_norm(values, gain):
    return values * lax.rsqrt(jnp.mean(values * values, axis=-1, keepdims=True) + EPSILON) * gain


def matmul(left, right):
    return jnp.dot(left, right, preferred_element_type=jnp.float32)


def right_transposed(left, right):
    return jnp.einsum("ik,jk->ij", left, right, preferred_element_type=jnp.float32)


def left_transposed(left, right):
    return jnp.einsum("ki,kj->ij", left, right, preferred_element_type=jnp.float32)


def norm_back(values, gain, upstream):
    result, pullback = jax.vjp(rms_norm, values, gain)
    return pullback(upstream)


def gelu_back(values, upstream):
    result, pullback = jax.vjp(jax.nn.gelu, values)
    return pullback(upstream)[0]


def softmax_back(probs, upstream):
    return probs * (upstream - jnp.sum(probs * upstream, axis=-1, keepdims=True))


def diagonal_sums(grid):
    heads, rows, cols = grid.shape
    flipped = grid[:, :, ::-1]
    padded = jnp.pad(flipped, ((0, 0), (0, 0), (0, rows)))
    skewed = padded.reshape(heads, rows * (cols + rows))[:, : rows * (cols + rows - 1)]
    return jnp.sum(skewed.reshape(heads, rows, cols + rows - 1), axis=1)


def update(weight, moment, average, gradient):
    new_moment = MOMENTUM * moment + gradient
    new_weight = weight - RATE * (gradient + MOMENTUM * new_moment)
    new_average = AVERAGING * average + (1.0 - AVERAGING) * new_weight
    return (new_moment, new_average, new_weight, new_weight.astype(jnp.bfloat16))


def per_device(
    encoder_input,
    decoder_input,
    output_cotangent,
    pair_lengths,
    pair_offset,
    pair_query,
    attention_master,
    attention_moment,
    attention_average,
    feedforward_master,
    feedforward_moment,
    feedforward_average,
    decoder_master,
    decoder_moment,
    decoder_average,
    expansion_master,
    expansion_moment,
    expansion_average,
    gain_master,
    gain_moment,
    gain_average,
    bias_master,
    bias_moment,
    bias_average,
):
    attention, feedforward, decoder, expansion = (
        lax.all_gather(attention_master.astype(jnp.bfloat16), ("dp", "tok"), axis=1, tiled=True),
        lax.all_gather(feedforward_master.astype(jnp.bfloat16), ("dp", "tok"), axis=1, tiled=True),
        lax.all_gather(decoder_master.astype(jnp.bfloat16), ("dp", "tok"), axis=1, tiled=True),
        lax.all_gather(expansion_master.astype(jnp.bfloat16), ("dp", "tok"), axis=1, tiled=True),
    )
    length = encoder_input.shape[1]
    width = encoder_input.shape[2]
    heads = bias_master.shape[1]
    head_size = width // heads
    pairs = pair_lengths.shape[1]
    slot_size = length // 4
    block = min(512, length)
    hidden = encoder_input[0].astype(jnp.float32)
    lengths = pair_lengths[0]
    ends = jnp.cumsum(lengths)
    starts = ends - lengths
    position = jnp.arange(length, dtype=jnp.int32)
    segment = jnp.sum((position[:, None] >= ends[None, :]).astype(jnp.int32), axis=1)
    normed = rms_norm(hidden, gain_master[0]).astype(jnp.bfloat16)
    queries = matmul(normed, attention[0]).astype(jnp.bfloat16).reshape(length, heads, head_size)
    keys = matmul(normed, attention[1]).astype(jnp.bfloat16).reshape(length, heads, head_size)
    values = matmul(normed, attention[2]).astype(jnp.bfloat16).reshape(length, heads, head_size)

    def scores_of():
        buckets = bucket_ids(position[None, :] - position[:, None])
        bias = jnp.transpose(jnp.take(bias_master, buckets, axis=0), (2, 0, 1))
        raw = jnp.einsum("ihd,jhd->hij", queries, keys, preferred_element_type=jnp.float32)
        same = segment[:, None] == segment[None, :]
        return (jnp.where(same[None], raw * SCALING + bias, NEGATIVE), queries)

    start = 0
    scores, rows_query = scores_of()
    peak = jnp.max(scores, axis=-1, keepdims=True)
    expo = jnp.exp(scores - peak)
    total = jnp.sum(expo, axis=-1, keepdims=True)
    probs = expo / total
    logsums = [peak + jnp.log(total)]
    outputs = jnp.einsum(
        "hij,jhd->ihd", probs.astype(jnp.bfloat16), values, preferred_element_type=jnp.float32
    )
    attended = outputs.reshape(length, width).astype(jnp.bfloat16)
    residual = hidden + matmul(attended, attention[3])
    normed_two = rms_norm(residual, gain_master[1]).astype(jnp.bfloat16)
    inner = matmul(normed_two, feedforward[0])
    activated = jax.nn.gelu(inner).astype(jnp.bfloat16)
    encoded = (residual + right_transposed(activated, feedforward[1])).astype(jnp.bfloat16)
    devices = lax.axis_size("tok")
    rank_self = lax.axis_index("tok")
    offsets = pair_offset[0]
    owners = pair_query[0]
    counter = jnp.arange(pairs, dtype=jnp.int32)
    all_lengths = lax.all_gather(pair_lengths, "tok", axis=0, tiled=True)
    sources = (rank_self - offsets) % devices
    targets = (rank_self + offsets) % devices
    context_lengths = all_lengths[sources, counter]
    inside = jnp.arange(slot_size, dtype=jnp.int32)
    token_index = jnp.minimum(starts[:, None] + inside[None, :], length - 1)
    valid = inside[None, :] < lengths[:, None]
    packed = jnp.where(valid[:, :, None], encoded[token_index], jnp.zeros((), jnp.bfloat16))
    half = pairs // 2
    shift_values = [index for index in range(half)] + [
        devices // 2 + index for index in range(half)
    ]
    place_of = jnp.zeros((pairs,), jnp.int32)
    for place, value in enumerate(shift_values):
        place_of = place_of + place * (offsets == value).astype(jnp.int32)
    outgoing = jnp.zeros((devices, slot_size, width), jnp.bfloat16).at[targets].set(packed)
    arrived = lax.all_to_all(outgoing, "tok", split_axis=0, concat_axis=0, tiled=True)
    context = arrived[sources]
    state = decoder_input.astype(jnp.float32)
    nquery = state.shape[0]
    self_in = rms_norm(state, gain_master[2]).astype(jnp.bfloat16)
    self_values = matmul(self_in, decoder[0]).astype(jnp.bfloat16)
    after_self = state + matmul(self_values, decoder[1])
    cross_in = rms_norm(after_self, gain_master[3]).astype(jnp.bfloat16)
    cross_query = (
        matmul(cross_in, decoder[2]).astype(jnp.bfloat16).reshape(nquery, heads, head_size)
    )
    flat_context = context.reshape(pairs * slot_size, width)
    cross_keys = (
        matmul(flat_context, attention[4])
        .astype(jnp.bfloat16)
        .reshape(pairs * slot_size, heads, head_size)
    )
    cross_values = (
        matmul(flat_context, attention[5])
        .astype(jnp.bfloat16)
        .reshape(pairs * slot_size, heads, head_size)
    )
    allowed = (owners[None, :, None] == jnp.arange(nquery, dtype=jnp.int32)[:, None, None]) & (
        inside[None, None, :] < context_lengths[None, :, None]
    )
    allowed = allowed.reshape(nquery, pairs * slot_size)
    cross_raw = jnp.einsum(
        "qhd,jhd->qhj", cross_query, cross_keys, preferred_element_type=jnp.float32
    )
    cross_scores = jnp.where(allowed[:, None, :], cross_raw * SCALING, NEGATIVE)
    cross_peak = jnp.max(cross_scores, axis=-1, keepdims=True)
    cross_expo = jnp.exp(cross_scores - cross_peak)
    cross_probs = cross_expo / jnp.sum(cross_expo, axis=-1, keepdims=True)
    cross_low = cross_probs.astype(jnp.bfloat16)
    cross_out = (
        jnp.einsum("qhj,jhd->qhd", cross_low, cross_values, preferred_element_type=jnp.float32)
        .reshape(nquery, width)
        .astype(jnp.bfloat16)
    )
    after_cross = after_self + matmul(cross_out, decoder[3])
    final_in = rms_norm(after_cross, gain_master[4]).astype(jnp.bfloat16)
    final_inner = matmul(final_in, expansion[0])
    final_act = jax.nn.gelu(final_inner).astype(jnp.bfloat16)
    decoder_output = after_cross + right_transposed(final_act, expansion[1])
    upstream = output_cotangent.astype(jnp.float32)
    up_low = upstream.astype(jnp.bfloat16)
    grad_act = matmul(up_low, expansion[1])
    grad_inner = gelu_back(final_inner, grad_act).astype(jnp.bfloat16)
    grad_final_in = right_transposed(grad_inner, expansion[0])
    grad_state_four, grad_gain_four = norm_back(after_cross, gain_master[4], grad_final_in)
    grad_cross_total = upstream + grad_state_four
    cross_grad_low = grad_cross_total.astype(jnp.bfloat16)
    grad_cross_out = (
        right_transposed(cross_grad_low, decoder[3])
        .astype(jnp.bfloat16)
        .reshape(nquery, heads, head_size)
    )
    grad_cross_probs = jnp.einsum(
        "qhd,jhd->qhj", grad_cross_out, cross_values, preferred_element_type=jnp.float32
    )
    grad_values_cross = (
        jnp.einsum("qhj,qhd->jhd", cross_low, grad_cross_out, preferred_element_type=jnp.float32)
        .astype(jnp.bfloat16)
        .reshape(pairs * slot_size, width)
    )
    grad_cross_scores = softmax_back(cross_probs, grad_cross_probs).astype(jnp.bfloat16)
    grad_query_cross = (
        (
            jnp.einsum(
                "qhj,jhd->qhd", grad_cross_scores, cross_keys, preferred_element_type=jnp.float32
            )
            * SCALING
        )
        .astype(jnp.bfloat16)
        .reshape(nquery, width)
    )
    grad_keys_cross = (
        (
            jnp.einsum(
                "qhj,qhd->jhd", grad_cross_scores, cross_query, preferred_element_type=jnp.float32
            )
            * SCALING
        )
        .astype(jnp.bfloat16)
        .reshape(pairs * slot_size, width)
    )
    grad_key_proj = left_transposed(flat_context, grad_keys_cross)
    grad_value_proj = left_transposed(flat_context, grad_values_cross)
    grad_context = (
        right_transposed(grad_keys_cross, attention[4])
        + right_transposed(grad_values_cross, attention[5])
    ).astype(jnp.bfloat16)
    grad_context = grad_context.reshape(pairs, slot_size, width)
    grad_cross_in = right_transposed(grad_query_cross, decoder[2])
    grad_state_three, grad_gain_three = norm_back(after_self, gain_master[3], grad_cross_in)
    grad_self_total = grad_cross_total + grad_state_three
    self_grad_low = grad_self_total.astype(jnp.bfloat16)
    grad_self_values = right_transposed(self_grad_low, decoder[1]).astype(jnp.bfloat16)
    grad_self_in = right_transposed(grad_self_values, decoder[0])
    grad_state_two, grad_gain_two = norm_back(state, gain_master[2], grad_self_in)
    decoder_gradient = grad_self_total + grad_state_two
    returning = jnp.zeros((devices, slot_size, width), jnp.bfloat16).at[sources].set(grad_context)
    returned = lax.all_to_all(returning, "tok", split_axis=0, concat_axis=0, tiled=True)
    grad_pairs = returned[targets]
    grad_encoded = grad_pairs[segment, position - starts[segment]]
    grad_enc_down = left_transposed(grad_encoded, activated)
    grad_activated = matmul(grad_encoded, feedforward[1])
    grad_inner_enc = gelu_back(inner, grad_activated).astype(jnp.bfloat16)
    grad_enc_up = left_transposed(normed_two, grad_inner_enc)
    grad_normed_two = right_transposed(grad_inner_enc, feedforward[0])
    grad_resid, grad_gain_one = norm_back(residual, gain_master[1], grad_normed_two)
    grad_residual = grad_encoded.astype(jnp.float32) + grad_resid
    attn_low = grad_residual.astype(jnp.bfloat16)
    grad_enc_out = left_transposed(attended, attn_low)
    grad_attended = (
        right_transposed(attn_low, attention[3])
        .astype(jnp.bfloat16)
        .reshape(length, heads, head_size)
    )
    grad_keys = jnp.zeros((length, heads, head_size), jnp.float32)
    grad_values = jnp.zeros((length, heads, head_size), jnp.float32)
    grad_table = jnp.zeros(bias_master.shape, jnp.float32)
    bucket_range = jnp.arange(bias_master.shape[0], dtype=jnp.int32)
    diagonal_index = jnp.arange(length + block - 1, dtype=jnp.int32)
    query_grads = []
    for index, start in enumerate(range(0, length, block)):
        scores, rows_query = scores_of()
        probs = jnp.exp(scores - logsums[index])
        grad_probs = jnp.einsum(
            "ihd,jhd->hij", grad_attended, values, preferred_element_type=jnp.float32
        )
        grad_values = jnp.einsum(
            "hij,ihd->jhd",
            probs.astype(jnp.bfloat16),
            grad_attended,
            preferred_element_type=jnp.float32,
        )
        grad_scores = softmax_back(probs, grad_probs).astype(jnp.bfloat16)
        query_grads.append(
            (
                jnp.einsum("hij,jhd->ihd", grad_scores, keys, preferred_element_type=jnp.float32)
                * SCALING
            ).astype(jnp.bfloat16)
        )
        grad_keys = (
            jnp.einsum("hij,ihd->jhd", grad_scores, rows_query, preferred_element_type=jnp.float32)
            * SCALING
        )
        sums = diagonal_sums(grad_scores.astype(jnp.float32))
        relative = length - 1 - diagonal_index - start
        onehot = (bucket_ids(relative)[:, None] == bucket_range[None, :]).astype(jnp.float32)
        grad_table = jnp.dot(
            sums, onehot, precision=lax.Precision.HIGHEST, preferred_element_type=jnp.float32
        ).T
    grad_queries = query_grads[0].reshape(length, width)
    grad_keys_low = grad_keys.astype(jnp.bfloat16).reshape(length, width)
    grad_values_low = grad_values.astype(jnp.bfloat16).reshape(length, width)
    grad_query_proj = left_transposed(normed, grad_queries)
    grad_keys_proj = left_transposed(normed, grad_keys_low)
    grad_values_proj = left_transposed(normed, grad_values_low)
    grad_normed = (
        right_transposed(grad_queries, attention[0])
        + right_transposed(grad_keys_low, attention[1])
        + right_transposed(grad_values_low, attention[2])
    )
    grad_input_part, grad_gain_zero = norm_back(hidden, gain_master[0], grad_normed)
    encoder_gradient = (grad_residual + grad_input_part)[None]
    attention_grad = jnp.stack(
        [
            grad_query_proj,
            grad_keys_proj,
            grad_values_proj,
            grad_enc_out,
            grad_key_proj,
            grad_value_proj,
        ]
    )
    feedforward_grad = jnp.stack([grad_enc_up, grad_enc_down])
    grad_value_self = left_transposed(self_in, grad_self_values)
    grad_output_self = left_transposed(self_values, self_grad_low)
    grad_query_decoder = left_transposed(cross_in, grad_query_cross)
    grad_cross_proj = left_transposed(cross_out, cross_grad_low)
    grad_up = left_transposed(final_in, grad_inner)
    grad_down = left_transposed(up_low, final_act)
    decoder_grad = jnp.stack(
        [grad_value_self, grad_output_self, grad_query_decoder, grad_cross_proj]
    )
    expansion_grad = jnp.stack([grad_up, grad_down])
    attention_sum, feedforward_sum, decoder_sum, expansion_sum = (
        lax.psum_scatter(attention_grad, ("dp", "tok"), scatter_dimension=1, tiled=True),
        lax.psum_scatter(feedforward_grad, ("dp", "tok"), scatter_dimension=1, tiled=True),
        lax.psum_scatter(decoder_grad, ("dp", "tok"), scatter_dimension=1, tiled=True),
        lax.psum_scatter(expansion_grad, ("dp", "tok"), scatter_dimension=1, tiled=True),
    )
    gain_grad = jnp.stack(
        [grad_gain_zero, grad_gain_one, grad_gain_two, grad_gain_three, grad_gain_four]
    )
    gain_sum, bias_sum = lax.psum((gain_grad, grad_table), ("dp", "tok"))
    results = [decoder_output, encoder_gradient, decoder_gradient]
    groups = (
        (attention_master, attention_moment, attention_average, attention_sum),
        (feedforward_master, feedforward_moment, feedforward_average, feedforward_sum),
        (decoder_master, decoder_moment, decoder_average, decoder_sum),
        (expansion_master, expansion_moment, expansion_average, expansion_sum),
        (gain_master, gain_moment, gain_average, gain_sum),
        (bias_master, bias_moment, bias_average, bias_sum),
    )
    for weight, moment, average, gradient in groups:
        results.extend(update(weight, moment, average, gradient))
    return tuple(results)


def solution(mesh):
    in_specs = (
        P(("dp", "tok"), None, None),
        P(("dp", "tok"), None),
        P(("dp", "tok"), None),
        P(("dp", "tok"), None),
        P("dp", None),
        P("dp", None),
        P(None, ("dp", "tok"), None),
        P(None, ("dp", "tok"), None),
        P(None, ("dp", "tok"), None),
        P(None, ("dp", "tok"), None),
        P(None, ("dp", "tok"), None),
        P(None, ("dp", "tok"), None),
        P(None, ("dp", "tok"), None),
        P(None, ("dp", "tok"), None),
        P(None, ("dp", "tok"), None),
        P(None, ("dp", "tok"), None),
        P(None, ("dp", "tok"), None),
        P(None, ("dp", "tok"), None),
        P(),
        P(),
        P(),
        P(),
        P(),
        P(),
    )
    out_specs = (
        P(("dp", "tok"), None),
        P(("dp", "tok"), None, None),
        P(("dp", "tok"), None),
        P(None, ("dp", "tok"), None),
        P(None, ("dp", "tok"), None),
        P(None, ("dp", "tok"), None),
        P(None, ("dp", "tok"), None),
        P(None, ("dp", "tok"), None),
        P(None, ("dp", "tok"), None),
        P(None, ("dp", "tok"), None),
        P(None, ("dp", "tok"), None),
        P(None, ("dp", "tok"), None),
        P(None, ("dp", "tok"), None),
        P(None, ("dp", "tok"), None),
        P(None, ("dp", "tok"), None),
        P(None, ("dp", "tok"), None),
        P(None, ("dp", "tok"), None),
        P(None, ("dp", "tok"), None),
        P(None, ("dp", "tok"), None),
        P(),
        P(),
        P(),
        P(),
        P(),
        P(),
        P(),
        P(),
    )
    return jax.shard_map(
        per_device, mesh=mesh, in_specs=in_specs, out_specs=out_specs, check_vma=False
    )
```

profile of v0, /device:TPU:0, one launch (start us, length us, event | category | flops | bytes accessed | tf_op | source)
XLA Modules:
  0.0 1855.5 jit_solution(18096413515725142426)
XLA Ops:
  15.5 865.9 %gather_fusion.5 = f32[262144,12]{1,0:T(8,128)} fusion(f32[32,12]{1,0:T(8,128)S(1)} %copy.113, s32[262144]{0:T(1024)S(1)} %broadcast_clamp_fusion), kind=kCustom, calls=%fused_computation.clone | custom fusion | bytes 26214400 | tf_op jit(solution)/shard_map/jit(_take)/gather | solution.py:120
  881.4 73.5 %copy.115 = f32[512,512,12]{0,1,2:T(8,128)} copy(f32[512,512,12]{2,1,0:T(8,128)} %bitcast.15) | data formatting | bytes 25165824 | tf_op jit(solution)/shard_map/jit(_take)/gather | solution.py:120
  962.6 3.0 convolution_convert_fusion.6
  967.1 7.1 fusion.132
  976.1 2.6 copy-done
  985.5 5.0 fusion.16
  993.1 5.2 add_convert_fusion.1
  998.3 5.2 gather_fusion
  1006.4 4.8 scatter_fusion
  1011.3 6.3 all-to-all-start
  1017.6 33.0 %all-gather = s32[8,1,8]{2,1,0:T(1,128)S(1)} all-gather(s32[1,1,8]{2,1,0:T(1,128)S(1)} %bitcast.325), channel_id=1, replica_groups=mesh['dp'=4,'tok'=8] {'tok'}, dimensions={0}, use_global_device_ids=true | all-gather | bytes 288 | tf_op jit(solution)/shard_map/all_gather | solution.py:146
  1058.4 4.5 convolution_convert_fusion.1
  1065.3 2.7 convolution_convert_fusion.2
  1071.0 3.2 fusion.20
  1074.3 3.6 fusion.75
  1092.9 14.9 pad_maximum_fusion.2
  1109.3 3.3 fusion.61
  1112.6 2.8 add_convert_fusion
  1116.7 4.9 scatter_fusion.1
  1121.6 10.6 all-to-all-start.1
  1132.9 4.6 compare_select_fusion.4
  1138.2 34.1 %all-to-all-done.1 = bf16[8,128,768]{2,1,0:T(8,128)(2,1)} async-done(((bf16[8,128,768]{2,1,0:T(8,128)(2,1)}), bf16[8,128,768]{2,1,0:T(8,128)(2,1)}, u32[]{:S(2)}, u32[]{:S(2)}) %all-to-all-start.1) | async-done | bytes 1572896 | tf_op jit(solution)/shard_map/all_to_all | solution.py:264
  1174.3 7.3 gather_fusion.4
  1181.6 8.7 fusion.10
  1190.4 6.5 multiply_reduce_fusion.1
  1197.4 3.6 convolution_convert_fusion.3
  1203.2 12.6 multiply_reduce_fusion
  1215.8 7.3 multiply_convert_fusion
  1238.1 2.8 bitcast_dynamic-update-slice_fusion.1
  1240.9 2.8 bitcast_dynamic-update-slice_fusion
  1246.7 7.0 pad_maximum_fusion.1
  1255.1 4.7 convolution_bitcast_fusion.3
  1259.9 5.2 convolution_bitcast_fusion.2
  1265.1 7.4 pad_maximum_fusion
  1275.3 4.5 fusion.48
  1279.8 91.0 %rev.3 = f32[12,512,512]{1,2,0:T(8,128)} reverse(bf16[12,512,512]{1,2,0:T(8,128)(2,1)} %copy-done.1), dimensions={2} | reverse | bytes 18874368 | tf_op jit(solution)/shard_map/rev | solution.py:55
  1375.1 3.7 fusion.31
  1378.8 12.7 copy.136
  1391.5 14.6 pad.4.clone
  1406.1 11.0 pad.17
  1417.1 39.7 %copy.139 = f32[2,8,512,1024]{3,1,2,0:T(8,128)} copy(f32[2,8,512,1024]{3,2,1,0:T(8,128)S(1)} %bitcast.288) | data formatting | bytes 67108864
  1456.8 24.4 %slice.134 = f32[12,523776]{1,0:T(8,128)} slice(f32[12,524288]{1,0:T(8,128)} %bitcast.289), slice={[0:12], [0:523776]} | slice | bytes 50282496 | tf_op jit(solution)/shard_map/slice | solution.py:57
  1481.2 42.6 %reshape.698 = f32[12,512,1023]{2,1,0:T(8,128)} reshape(f32[12,523776]{1,0:T(8,128)} %slice.134) | data formatting | bytes 50282496 | tf_op jit(solution)/shard_map/reshape | solution.py:58
  1523.9 9.4 reduce_sum.224
  1533.7 38.2 %all-reduce.1 = (f32[5,768]{1,0:T(8,128)S(1)}, f32[32,12]{0,1:T(8,128)S(1)}) all-reduce(f32[5,768]{1,0:T(8,128)S(1)} %stack.80, f32[32,12]{0,1:T(8,128)S(1)} %fusion.65), channel_id=1, replica_groups=mesh['dp'=4,'tok'=8] {'dp','tok'}, use_global_device_ids=true, to_apply=%region_29.31 | all-reduce | flops 4224 | bytes 33792 | tf_op jit(solution)/shard_map/psum | solution.py:359
  1574.4 3.0 fusion.36
  1584.2 49.4 %reduce-scatter.11.cloned.1.call-done = f32[2,24,3072]{2,1,0:T(8,128)} async-done(((f32[2,768,3072]{2,1,0:T(8,128)}), f32[2,24,3072]{2,1,0:T(8,128)}) %reduce-scatter.11.cloned.1.call-update) | async-done | bytes 589840 | tf_op jit(solution)/shard_map/reduce_scatter | solution.py:354
  1638.1 207.1 %reduce-scatter.7.cloned.1.call-done = f32[2,24,3072]{2,1,0:T(8,128)} async-done(((f32[2,768,3072]{2,1,0:T(8,128)}), f32[2,24,3072]{2,1,0:T(8,128)}) %reduce-scatter.7.cloned.1.call-update) | async-done | bytes 589840 | tf_op jit(solution)/shard_map/reduce_scatter | solution.py:352
  (272 shorter events, 111.8 us)
Async XLA Ops:
  7.2 950.3 %all-gather.8.cloned.1.call-start = ((), (), s32[]{:S(2)}) async-start(), calls=%async_computation.7 | async-start | bytes 7299072 | tf_op jit(solution)/shard_map/all_gather | solution.py:95
  9.0 975.4 %all-gather.10.cloned.1.call-start = ((), (), s32[]{:S(2)}) async-start(), calls=%async_computation.8 | async-start | bytes 9732096 | tf_op jit(solution)/shard_map/all_gather | solution.py:96
  10.9 1040.7 %all-gather.6.cloned.1.call-start = ((), (), s32[]{:S(2)}) async-start(), calls=%async_computation.6 | async-start | bytes 4866048 | tf_op jit(solution)/shard_map/all_gather | solution.py:97
  12.6 1058.4 %all-gather.12.cloned.1.call-start = ((), (), s32[]{:S(2)}) async-start(), calls=%async_computation.9 | async-start | bytes 9732096 | tf_op jit(solution)/shard_map/all_gather | solution.py:98
  881.4 74.5 %copy-start.51 = (s32[1,8]{1,0:T(1,128)S(1)}, s32[1,8]{1,0:T(1,128)}, u32[]{:S(2)}) copy-start(s32[1,8]{1,0:T(1,128)} %param.29) | copy-start | bytes 100
  881.4 74.7 %copy-start.38 = (f32[5,768]{1,0:T(8,128)S(1)}, f32[5,768]{1,0:T(8,128)}, u32[]{:S(2)}) copy-start(f32[5,768]{1,0:T(8,128)} %param.44) | copy-start | bytes 46084
  881.4 74.8 %copy-start.2 = (bf16[1,512,768]{2,1,0:T(8,128)(2,1)S(1)}, bf16[1,512,768]{2,1,0:T(8,128)(2,1)}, u32[]{:S(2)}) copy-start(bf16[1,512,768]{2,1,0:T(8,128)(2,1)} %param.26) | copy-start | bytes 2359300
  881.4 75.1 %copy-start.50 = (s32[1,8]{1,0:T(1,128)S(1)}, s32[1,8]{1,0:T(1,128)}, u32[]{:S(2)}) copy-start(s32[1,8]{1,0:T(1,128)} %param.30) | copy-start | bytes 100
  959.9 7.1 copy-start.8
  967.0 9.1 copy-start.13
  985.5 7.6 copy-start.52
  1006.4 44.8 %copy-start.37 = (bf16[2,768]{1,0:T(2,128)(2,1)S(1)}, bf16[2,768]{1,0:T(2,128)(2,1)}, u32[]{:S(2)}) copy-start(bf16[2,768]{1,0:T(2,128)(2,1)} %param.27) | copy-start | bytes 9220
  1006.4 45.0 %copy-start.53 = (s32[1,8]{1,0:T(1,128)S(1)}, s32[1,8]{1,0:T(1,128)}, u32[]{:S(2)}) copy-start(s32[1,8]{1,0:T(1,128)} %param.31) | copy-start | bytes 100
  1011.3 45.3 %all-to-all-start = ((bf16[8,128,768]{2,1,0:T(8,128)(2,1)}), bf16[8,128,768]{2,1,0:T(8,128)(2,1)S(1)}, u32[]{:S(2)}, u32[]{:S(2)}) async-start(bf16[8,128,768]{2,1,0:T(8,128)(2,1)} %scatter_fusion), calls=%async_computation | async-start | bytes 3145728 | tf_op jit(solution)/shard_map/all_to_all | solution.py:162
  1017.6 559.9 %reduce-scatter.9.cloned.1.call-start = ((), (), s32[]{:S(2)}) async-start(), calls=%async_computation.12 | async-start | bytes 9732096 | tf_op jit(solution)/shard_map/reduce_scatter | solution.py:353
  1058.4 6.9 copy-start.27
  1071.0 6.9 copy-start.6
  1085.4 23.9 %copy-start.54 = (bf16[12,64,1024]{2,1,0:T(8,128)(2,1)}, bf16[12,64,1024]{2,1,0:T(8,128)(2,1)S(1)}, u32[]{:S(2)}) copy-start(bf16[12,64,1024]{2,1,0:T(8,128)(2,1)S(1)} %multiply_convert_fusion.2) | copy-start | bytes 4718596
  1121.6 50.6 %all-to-all-start.1 = ((bf16[8,128,768]{2,1,0:T(8,128)(2,1)}), bf16[8,128,768]{2,1,0:T(8,128)(2,1)}, u32[]{:S(2)}, u32[]{:S(2)}) async-start(bf16[8,128,768]{2,1,0:T(8,128)(2,1)} %scatter_fusion.1), calls=%async_computation.1 | async-start | bytes 3145728 | tf_op jit(solution)/shard_map/all_to_all | solution.py:264
  1132.2 449.0 %reduce-scatter.5.cloned.1.call-start = ((), (), s32[]{:S(2)}) async-start(), calls=%async_computation.10 | async-start | bytes 14598144 | tf_op jit(solution)/shard_map/reduce_scatter | solution.py:351
  1181.6 8.7 copy-start.11
  1190.3 6.6 copy-start.14
  1190.3 6.6 copy-start.15
  1197.3 38.3 %copy-start.3 = (f32[512,768]{1,0:T(8,128)}, f32[512,768]{1,0:T(8,128)S(1)}, u32[]{:S(2)}) copy-start(f32[512,768]{1,0:T(8,128)S(1)} %fusion.34) | copy-start | bytes 4718596
  1203.2 12.6 slice-start
  1203.2 12.6 slice-start.1
  1203.2 12.6 slice-start.2
  1243.8 389.8 %reduce-scatter.11.cloned.1.call-start = ((), (), s32[]{:S(2)}) async-start(), calls=%async_computation.13 | async-start | bytes 19464192 | tf_op jit(solution)/shard_map/reduce_scatter | solution.py:354
  1253.7 591.4 %reduce-scatter.7.cloned.1.call-start = ((), (), s32[]{:S(2)}) async-start(), calls=%async_computation.11 | async-start | bytes 19464192 | tf_op jit(solution)/shard_map/reduce_scatter | solution.py:352
  1279.8 91.0 %copy-start.18 = (bf16[12,64,512]{2,1,0:T(8,128)(2,1)S(1)}, bf16[12,64,512]{2,1,0:T(8,128)(2,1)}, u32[]{:S(2)}) copy-start(bf16[12,64,512]{2,1,0:T(8,128)(2,1)} %copy-done.17) | copy-start | bytes 2359300
  1523.8 48.1 %copy-start.46 = (f32[512]{0:T(512)S(1)}, f32[512]{0:T(512)}, u32[]{:S(2)}) copy-start(f32[512]{0:T(512)} %copy-done.45) | copy-start | bytes 6148
  1523.8 48.1 %copy-start.41 = (f32[32,12]{0,1:T(8,128)S(1)}, f32[32,12]{0,1:T(8,128)}, u32[]{:S(2)}) copy-start(f32[32,12]{0,1:T(8,128)} %param.47) | copy-start | bytes 4612
  1523.8 48.1 %copy-start.49 = (f32[32,12]{0,1:T(8,128)S(1)}, f32[32,12]{0,1:T(8,128)}, u32[]{:S(2)}) copy-start(f32[32,12]{0,1:T(8,128)} %param.48) | copy-start | bytes 4612
  1523.8 48.7 %copy-start.48 = (f32[32,12]{0,1:T(8,128)S(1)}, f32[32,12]{0,1:T(8,128)}, u32[]{:S(2)}) copy-start(f32[32,12]{0,1:T(8,128)} %param.49) | copy-start | bytes 4612
  1523.8 49.3 %copy-start.39 = (f32[5,768]{1,0:T(8,128)S(1)}, f32[5,768]{1,0:T(8,128)}, u32[]{:S(2)}) copy-start(f32[5,768]{1,0:T(8,128)} %param.44) | copy-start | bytes 46084
  1523.8 49.3 %copy-start.44 = (f32[5,768]{1,0:T(8,128)S(1)}, f32[5,768]{1,0:T(8,128)}, u32[]{:S(2)}) copy-start(f32[5,768]{1,0:T(8,128)} %param.45) | copy-start | bytes 46084
  1523.8 49.9 %copy-start.43 = (f32[5,768]{1,0:T(8,128)S(1)}, f32[5,768]{1,0:T(8,128)}, u32[]{:S(2)}) copy-start(f32[5,768]{1,0:T(8,128)} %param.46) | copy-start | bytes 46084
  1523.8 50.5 %copy-start.4 = (f32[512,768]{1,0:T(8,128)S(1)}, f32[512,768]{1,0:T(8,128)}, u32[]{:S(2)}) copy-start(f32[512,768]{1,0:T(8,128)} %copy-done.3) | copy-start | bytes 4718596
  1533.3 44.2 %copy-start.30 = (f32[4,24,768]{2,1,0:T(8,128)S(1)}, f32[4,24,768]{2,1,0:T(8,128)}, u32[]{:S(2)}) copy-start(f32[4,24,768]{2,1,0:T(8,128)} %param.38) | copy-start | bytes 884740
  1572.5 6.9 copy-start.42
  1574.4 6.9 copy-start.25
  1577.4 56.2 %copy-start.23 = (f32[2,24,3072]{2,1,0:T(8,128)S(1)}, f32[2,24,3072]{2,1,0:T(8,128)}, u32[]{:S(2)}) copy-start(f32[2,24,3072]{2,1,0:T(8,128)} %param.41) | copy-start | bytes 1769476
  1579.4 56.5 %copy-start.29 = (f32[4,24,768]{2,1,0:T(8,128)}, f32[4,24,768]{2,1,0:T(8,128)S(1)}, u32[]{:S(2)}) copy-start(f32[4,24,768]{2,1,0:T(8,128)S(1)} %get-tuple-element.55) | copy-start | bytes 884740
  1583.3 54.7 %copy-start.26 = (f32[6,24,768]{2,1,0:T(8,128)}, f32[6,24,768]{2,1,0:T(8,128)S(1)}, u32[]{:S(2)}) copy-start(f32[6,24,768]{2,1,0:T(8,128)S(1)} %get-tuple-element.61) | copy-start | bytes 1327108
  1583.3 261.8 %copy-start.24 = (f32[2,24,3072]{2,1,0:T(8,128)S(1)}, f32[2,24,3072]{2,1,0:T(8,128)}, u32[]{:S(2)}) copy-start(f32[2,24,3072]{2,1,0:T(8,128)} %param.35) | copy-start | bytes 1769476
  1583.3 261.8 %copy-start.33 = (f32[2,24,3072]{2,1,0:T(8,128)S(1)}, f32[2,24,3072]{2,1,0:T(8,128)}, u32[]{:S(2)}) copy-start(f32[2,24,3072]{2,1,0:T(8,128)} %param.36) | copy-start | bytes 1769476
  1635.9 212.4 %copy-start.21 = (f32[2,24,3072]{2,1,0:T(8,128)}, f32[2,24,3072]{2,1,0:T(8,128)S(1)}, u32[]{:S(2)}) copy-start(f32[2,24,3072]{2,1,0:T(8,128)S(1)} %get-tuple-element.52) | copy-start | bytes 1769476
  1635.9 211.4 %copy-start.34 = (f32[2,24,3072]{2,1,0:T(8,128)S(1)}, f32[2,24,3072]{2,1,0:T(8,128)}, u32[]{:S(2)}) copy-start(f32[2,24,3072]{2,1,0:T(8,128)} %param.37) | copy-start | bytes 1769476
  (28 other events, 89.9 us)
Sparse Core Ops, SparseCore 0:
  11.8 75.3 all-gather.7
  91.0 80.6 all-gather.9
  175.4 62.2 all-gather.5
  241.4 80.9 all-gather.11
  1107.9 143.4 reduce-scatter.8
  1258.3 163.4 reduce-scatter.4
  1429.3 204.2 reduce-scatter.10
  1641.1 203.9 reduce-scatter.6
where the time goes:
time: 1880 us; the launch traced here: 1860 us
  local copies, waits for them, and re-layouts  1220 us (65%)
  waiting for transfers between devices  291 us (15%)
  matrix products  155 us (8%)
  other arithmetic  85.7 us (5%)
  blocking collectives  71.2 us (4%)
    gather x2, local copies, waits for them, and re-layouts, scores_of(): bias = jnp.transpose(jnp.take(bias_master, buckets, axis=0), (2, 0, 1))  939 us
    reduce_scatter x1, waiting for transfers between devices, per_device(): lax.psum_scatter(feedforward_grad, ('dp', 'tok'), scatter_dimension=1, ti...  207 us
    rev x1, local copies, waits for them, and re-layouts, diagonal_sums(): flipped = grid[:, :, ::-1]  91 us
    unnamed x138, local copies, waits for them, and re-layouts  73.4 us
    reduce_scatter x1, waiting for transfers between devices, per_device(): lax.psum_scatter(expansion_grad, ('dp', 'tok'), scatter_dimension=1, tile...  49.4 us
    dot_general x14, matrix products, matmul(): return jnp.dot(left, right, preferred_element_type=jnp.float32)  44 us
    dot_general x14, matrix products, right_transposed(): jnp.einsum('ik,jk->ij', left, right, preferred_element_type=jnp.float32)  42.7 us
    reshape x1, local copies, waits for them, and re-layouts, diagonal_sums(): return jnp.sum(skewed.reshape(heads, rows, cols + rows - 1), axis=1)  42.6 us
  transfers between devices with their start and end apart: 10, of which 3 were waited for; matrix products, arithmetic and copies ran while one was open for 76% of the time, Pallas kernels for 0%

commit v1 on v0

v1 whole, which is shorter than its diff:
```python
import jax
import jax.numpy as jnp
from jax import lax
from jax.experimental import pallas as pl
from jax.experimental.pallas import tpu as pltpu
from jax.sharding import PartitionSpec as P

EPSILON = 1e-06
SCALING = 0.125
NEGATIVE = -1e30
MOMENTUM = 0.5
AVERAGING = 0.5
RATE = 0.02
THRESHOLDS = (12, 16, 23, 32, 46, 64, 91)
BF = jnp.bfloat16
F32 = jnp.float32
QB = 128
DIAG = 512
SPAN = 3 * QB
VMEM = 48 * 2**20


def bucket_ids(relative):
    magnitude = jnp.abs(relative)
    bucket = jnp.minimum(magnitude, 8)
    for limit in THRESHOLDS:
        bucket = bucket + (magnitude >= limit).astype(jnp.int32)
    return bucket + 16 * (relative > 0).astype(jnp.int32)


def rms_norm(values, gain):
    return values * lax.rsqrt(jnp.mean(values * values, axis=-1, keepdims=True) + EPSILON) * gain


def dot_nn(left, right):
    return lax.dot_general(left, right, (((1,), (0,)), ((), ())), preferred_element_type=F32)


def dot_nt(left, right):
    return lax.dot_general(left, right, (((1,), (1,)), ((), ())), preferred_element_type=F32)


def dot_tn(left, right):
    return lax.dot_general(left, right, (((0,), (0,)), ((), ())), preferred_element_type=F32)


def norm_back(values, gain, upstream):
    result, pullback = jax.vjp(rms_norm, values, gain)
    return pullback(upstream)


def gelu_back(values, upstream):
    result, pullback = jax.vjp(jax.nn.gelu, values)
    return pullback(upstream)[0]


def update(weight, moment, average, gradient):
    new_moment = MOMENTUM * moment + gradient
    new_weight = weight - RATE * (gradient + MOMENTUM * new_moment)
    new_average = AVERAGING * average + (1.0 - AVERAGING) * new_weight
    return (new_moment, new_average, new_weight, new_weight.astype(BF))


def window(block, blocks):
    return max(0, block - 1) * QB, min(blocks, block + 2) * QB


def diagonal_onehot(buckets):
    place = jnp.arange(DIAG, dtype=jnp.int32)
    relative = jnp.where(place < SPAN, place, place - DIAG) - QB
    return (bucket_ids(relative)[:, None] == jnp.arange(buckets, dtype=jnp.int32)[None, :]).astype(
        F32
    )


def bias_tile(rows_ref, head):
    row = jnp.broadcast_to(rows_ref[0, head : head + 1, :], (QB, DIAG))
    return pltpu.roll(row, 0, 1, stride=1, stride_axis=0)[:, :SPAN]


def attention_kernel(q_ref, k_ref, v_ref, rows_ref, column_ref, line_ref, out_ref):
    blocks = q_ref.shape[0] // QB
    half = lax.broadcasted_iota(jnp.int32, (QB, QB), 1) < 64
    bias = [bias_tile(rows_ref, head) for head in range(2)]
    for block in range(blocks):
        low, high = window(block, blocks)
        off = low - (block - 1) * QB
        mine = pl.ds(block * QB, QB)
        query = q_ref[mine, :]
        same = column_ref[mine, :] == line_ref[:, low:high]
        outs = []
        for head in range(2):
            part = jnp.where(half if head == 0 else ~half, query, jnp.zeros((), BF))
            scores = dot_nt(part, k_ref[low:high, :]) * SCALING
            scores = jnp.where(same, scores + bias[head][:, off : off + high - low], NEGATIVE)
            expo = jnp.exp(scores - jnp.max(scores, axis=1, keepdims=True))
            probs = (expo * (1.0 / jnp.sum(expo, axis=1, keepdims=True))).astype(BF)
            outs.append(dot_nn(probs, v_ref[low:high, :]))
        out_ref[mine, :] = jnp.where(half, outs[0], outs[1]).astype(BF)


def attention_back_kernel(
    q_ref,
    k_ref,
    v_ref,
    up_ref,
    rows_ref,
    column_ref,
    line_ref,
    gq_ref,
    gk_ref,
    gv_ref,
    diag_ref,
    gk_sum,
    gv_sum,
    grid_sum,
):
    blocks = q_ref.shape[0] // QB
    lanes = lax.broadcasted_iota(jnp.int32, (QB, QB), 1)
    half = lanes < 64
    flip = (lax.broadcasted_iota(jnp.int32, (QB, QB), 0) + lanes == QB - 1).astype(BF)
    bias = [bias_tile(rows_ref, head) for head in range(2)]
    gk_sum[...] = jnp.zeros_like(gk_sum)
    gv_sum[...] = jnp.zeros_like(gv_sum)
    grid_sum[...] = jnp.zeros_like(grid_sum)
    for block in range(blocks):
        low, high = window(block, blocks)
        off = low - (block - 1) * QB
        span = high - low
        mine = pl.ds(block * QB, QB)
        query = q_ref[mine, :]
        up = up_ref[mine, :]
        same = column_ref[mine, :] == line_ref[:, low:high]
        outs = []
        gks = 0.0
        gvs = 0.0
        for head in range(2):
            keep = half if head == 0 else ~half
            query_part = jnp.where(keep, query, jnp.zeros((), BF))
            up_part = jnp.where(keep, up, jnp.zeros((), BF))
            scores = dot_nt(query_part, k_ref[low:high, :]) * SCALING
            scores = jnp.where(same, scores + bias[head][:, off : off + span], NEGATIVE)
            expo = jnp.exp(scores - jnp.max(scores, axis=1, keepdims=True))
            probs = expo * (1.0 / jnp.sum(expo, axis=1, keepdims=True))
            grad = dot_nt(up_part, v_ref[low:high, :])
            inner = jnp.sum(probs * grad, axis=1, keepdims=True)
            grad = (probs * (grad - inner)).astype(BF)
            outs.append(dot_nn(grad, k_ref[low:high, :]))
            gvs = gvs + dot_tn(probs.astype(BF), up_part)
            gks = gks + dot_tn(grad, query_part)
            grid_sum[head, :, off : off + span] += dot_nn(flip, grad)
        gk_sum[low:high, :] += gks
        gv_sum[low:high, :] += gvs
        gq_ref[mine, :] = (jnp.where(half, outs[0], outs[1]) * SCALING).astype(BF)
    gk_ref[...] = (gk_sum[...] * SCALING).astype(BF)
    gv_ref[...] = gv_sum[...].astype(BF)
    for head in range(2):
        rolled = pltpu.roll(grid_sum[head], DIAG - QB + 1, 1, stride=1, stride_axis=0)
        diag_ref[0, head : head + 1, :] = jnp.sum(rolled, axis=0, keepdims=True)


def attention_specs(length, slabs):
    slab = pl.BlockSpec((length, 128), lambda h: (0, h))
    rows = pl.BlockSpec((1, 2, DIAG), lambda h: (h, 0, 0))
    column = pl.BlockSpec((length, 1), lambda h: (0, 0))
    line = pl.BlockSpec((1, length), lambda h: (0, 0))
    return [slab] * slabs + [rows, column, line], slab, rows


def attention_forward(q, k, v, rows, segment):
    length, width = q.shape
    pairs = width // 128
    specs, slab, _ = attention_specs(length, 3)
    area = 24 * 164000
    return pl.pallas_call(
        attention_kernel,
        grid=(pairs,),
        in_specs=specs,
        out_specs=slab,
        out_shape=jax.ShapeDtypeStruct((length, width), BF),
        compiler_params=pltpu.CompilerParams(vmem_limit_bytes=VMEM),
        cost_estimate=pl.CostEstimate(
            flops=4 * area * 128, bytes_accessed=8 * length * width, transcendentals=area
        ),
    )(q, k, v, rows.reshape(pairs, 2, DIAG), segment[:, None], segment[None, :])


def attention_backward(q, k, v, up, rows, segment):
    length, width = q.shape
    pairs = width // 128
    specs, slab, rows_spec = attention_specs(length, 4)
    shape = jax.ShapeDtypeStruct((length, width), BF)
    area = 24 * 164000
    gq, gk, gv, diag = pl.pallas_call(
        attention_back_kernel,
        grid=(pairs,),
        in_specs=specs,
        out_specs=[slab] * 3 + [rows_spec],
        out_shape=[shape] * 3 + [jax.ShapeDtypeStruct((pairs, 2, DIAG), F32)],
        scratch_shapes=[
            pltpu.VMEM((length, 128), F32),
            pltpu.VMEM((length, 128), F32),
            pltpu.VMEM((2, QB, DIAG), F32),
        ],
        compiler_params=pltpu.CompilerParams(vmem_limit_bytes=VMEM),
        cost_estimate=pl.CostEstimate(
            flops=10 * area * 128, bytes_accessed=14 * length * width, transcendentals=area
        ),
    )(q, k, v, up, rows.reshape(pairs, 2, DIAG), segment[:, None], segment[None, :])
    return gq, gk, gv, diag.reshape(width // 64, DIAG)


class Net:
    def __init__(self):
        self.n_dp = lax.axis_size("dp")
        self.n_tok = lax.axis_size("tok")
        self.n_z = self.n_tok // 2
        self.tree = self.n_dp == 4 and self.n_z == 4
        dp, tok = lax.axis_index("dp"), lax.axis_index("tok")
        self.core, self.z = tok % 2, tok // 2
        self.x, self.y = dp % 2, dp // 2

    def tok_to(self, array, where):
        return lax.ppermute(array, "tok", [(t, where(t)) for t in range(self.n_tok)])

    def swap_core(self, array):
        return self.tok_to(array, lambda t: t ^ 1)

    def shift_z(self, array, by):
        return self.tok_to(array, lambda t: (t + 2 * by) % self.n_tok)

    def shift_tok(self, array, by):
        return self.tok_to(array, lambda t: (t + by) % self.n_tok) if by % self.n_tok else array

    def flip_dp(self, array, bit):
        return lax.ppermute(array, "dp", [(d, d ^ bit) for d in range(self.n_dp)])

    def swap_x(self, array):
        return self.flip_dp(array, 1)

    def swap_y(self, array):
        return self.flip_dp(array, 2)

    def own_first(self, array, axis=-1):
        low, high = jnp.split(array, 2, axis=axis)
        flipped = jnp.concatenate([high, low], axis=axis)
        return jnp.where(self.core == 0, array, flipped)


def place_kernel(meta_ref, *refs):
    pieces, out_ref, sems = refs[:8], refs[8], refs[9]
    half = out_ref.shape[2] // 2
    copies = []
    for index, piece in enumerate(pieces):
        for block in range(4):
            row = pl.multiple_of(meta_ref[(index % 4) * 4 + block], 48)
            column = pl.multiple_of(meta_ref[16 + index // 4], 128)
            copies.append(
                pltpu.make_async_copy(
                    piece.at[:, pl.ds(block * 48, 48), :],
                    out_ref.at[:, pl.ds(row, 48), pl.ds(column, half)],
                    sems.at[index * 4 + block],
                )
            )
            copies[-1].start()
    for copy in copies:
        copy.wait()


def place(net, mine, theirs, own_columns, own_rows):
    count, rows, half = mine[0].shape
    spots = []
    for dy in range(2):
        for dx in range(2):
            top = net.y ^ dy ^ (net.core if own_rows else 0)
            for block in range(4):
                spots.append((top * 2 + (net.x ^ dx)) * rows + (net.z + 1 + block) % 4 * 48)
    first = 0 if own_columns else net.core
    spots += [first * half, (1 - first) * half]
    meta = jnp.stack([jnp.asarray(spot, jnp.int32) for spot in spots])
    return pl.pallas_call(
        place_kernel,
        in_specs=[pl.BlockSpec(memory_space=pltpu.SMEM)] + [pl.BlockSpec(memory_space=pl.ANY)] * 8,
        out_specs=pl.BlockSpec(memory_space=pltpu.VMEM),
        out_shape=jax.ShapeDtypeStruct((count, 4 * rows, 2 * half), BF),
        scratch_shapes=[pltpu.SemaphoreType.DMA((32,))],
        compiler_params=pltpu.CompilerParams(vmem_limit_bytes=VMEM),
        cost_estimate=pl.CostEstimate(
            flops=0, bytes_accessed=count * rows * half * 32, transcendentals=0
        ),
    )(meta, *mine, *theirs)


def gather(net, shard, route, own_columns=True, own_rows=False):
    if not net.tree:
        whole = lax.all_gather(shard, ("dp", "tok"), axis=1, tiled=True)
        whole = net.own_first(whole, 2) if own_columns else whole
        return net.own_first(whole, 1) if own_rows else whole
    low, high = jnp.split(shard, 2, axis=2)
    keep = jnp.where(net.core == 0, low, high)
    got = net.swap_core(jnp.where(net.core == 0, high, low))
    chip = jnp.concatenate(
        [jnp.where(net.core == 0, keep, got), jnp.where(net.core == 0, got, keep)], axis=1
    )
    line = jnp.concatenate([net.shift_z(chip, by) for by in (3, 2, 1)] + [chip], axis=1)
    if route == 0:
        over_x = net.swap_x(line)
        mine = [line, over_x, net.swap_y(line), net.swap_y(over_x)]
    else:
        over_y = net.swap_y(line)
        mine = [line, net.swap_x(line), over_y, net.swap_x(over_y)]
    theirs = [net.swap_core(piece) for piece in mine]
    return place(net, mine, theirs, own_columns, own_rows)


def pick(array, index, axis):
    return lax.dynamic_index_in_dim(array, index, axis, keepdims=False)


def add(*parts):
    total = parts[0].astype(F32)
    for part in parts[1:]:
        total = total + part.astype(F32)
    return total


def scatter(net, grad, route):
    count, rows, columns = grad.shape
    if not net.tree:
        whole = net.own_first(grad, 2)
        total = lax.psum_scatter(whole, ("dp", "tok"), scatter_dimension=1, tiled=True)
        return total.astype(F32)
    half = columns // 2
    mine = grad[:, :, :half].reshape(count, 2, 2, rows // 4, half)
    got = net.swap_core(grad[:, :, half:]).reshape(count, 2, 2, rows // 4, half)
    steps = [(1, net.y, net.swap_y), (1, net.x, net.swap_x)]
    if route == 0:
        steps = [(2, net.x, net.swap_x), (1, net.y, net.swap_y)]
    for axis, index, swap in steps:
        sent = add(pick(mine, 1 - index, axis), pick(got, 1 - index, axis)).astype(BF)
        mine = add(pick(mine, index, axis), pick(got, index, axis)).astype(BF)
        got = swap(sent)
    mine = mine.reshape(count, 4, rows // 16, half)
    got = got.reshape(count, 4, rows // 16, half)
    parts = [pick(mine, net.z, 1), pick(got, net.z, 1)]
    for by in (1, 2, 3):
        to = (net.z + by) % 4
        parts.append(net.shift_z(add(pick(mine, to, 1), pick(got, to, 1)).astype(BF), by))
    total = add(*parts).reshape(count, 2, rows // 32, half)
    keep = pick(total, net.core, 1)
    other = net.swap_core(pick(total, 1 - net.core, 1))
    low = jnp.where(net.core == 0, keep, other)
    high = jnp.where(net.core == 0, other, keep)
    return jnp.concatenate([low, high], axis=2)


def gather_small(net, array):
    if not net.tree:
        return lax.all_gather(array, ("dp", "tok"), axis=0, tiled=True)
    array = jnp.concatenate([array] + [net.shift_z(array, by) for by in (1, 2, 3)], axis=0)
    array = jnp.concatenate([array, net.swap_x(array)], axis=0)
    array = jnp.concatenate([array, net.swap_y(array)], axis=0)
    return jnp.concatenate([array, net.swap_core(array)], axis=0)


def sum_small(net, array):
    bit = 1
    while bit < net.n_tok:
        array = array + net.tok_to(array, lambda t, bit=bit: t ^ bit)
        bit *= 2
    bit = 1
    while bit < net.n_dp:
        array = array + net.flip_dp(array, bit)
        bit *= 2
    return array


def per_device(
    encoder_input,
    decoder_input,
    output_cotangent,
    pair_lengths,
    pair_offset,
    pair_query,
    attention_master,
    attention_moment,
    attention_average,
    feedforward_master,
    feedforward_moment,
    feedforward_average,
    decoder_master,
    decoder_moment,
    decoder_average,
    expansion_master,
    expansion_moment,
    expansion_average,
    gain_master,
    gain_moment,
    gain_average,
    bias_master,
    bias_moment,
    bias_average,
):
    net = Net()
    attention_low = attention_master.astype(BF)
    feedforward_low = feedforward_master.astype(BF)
    decoder_low = decoder_master.astype(BF)
    expansion_low = expansion_master.astype(BF)
    w_qkv = gather(net, attention_low[:3], 0)
    w_out = gather(net, attention_low[3:4], 1, own_columns=False, own_rows=True)[0]
    w_up = gather(net, feedforward_low[:1], 1)[0]
    w_down = gather(net, feedforward_low[1:], 0)[0]
    w_cross = gather(net, attention_low[4:], 1)
    w_dec = gather(net, decoder_low, 0, own_columns=False)
    x_up = gather(net, expansion_low[:1], 1, own_columns=False)[0]
    x_down = gather(net, expansion_low[1:], 0, own_columns=False)[0]

    length = encoder_input.shape[1]
    width = encoder_input.shape[2]
    buckets, heads = bias_master.shape
    head_size = width // heads
    pairs = pair_lengths.shape[1]
    counter = jnp.arange(pairs, dtype=jnp.int32)
    hidden = encoder_input[0].astype(F32)
    lengths = pair_lengths[0]
    ends = jnp.sum(
        jnp.where(counter[:, None] <= counter[None, :], lengths[:, None], 0), axis=0
    )
    position = jnp.arange(length, dtype=jnp.int32)
    segment = jnp.sum((position[:, None] >= ends[None, :]).astype(jnp.int32), axis=1)
    onehot = diagonal_onehot(buckets)
    bias_rows = jnp.sum(bias_master.T[:, None, :] * onehot[None], axis=2)
    bias_rows = net.own_first(bias_rows, 0)

    normed = rms_norm(hidden, gain_master[0]).astype(BF)
    queries, keys, values = (dot_nn(normed, w_qkv[i]).astype(BF) for i in range(3))
    attended = attention_forward(queries, keys, values, bias_rows, segment)
    residual = hidden + dot_nn(attended, w_out)
    normed_two = rms_norm(residual, gain_master[1]).astype(BF)
    inner = dot_nn(normed_two, w_up)
    activated = jax.nn.gelu(inner).astype(BF)
    encoded = (residual + dot_nt(activated, w_down)).astype(BF)
    cross_keys = dot_nn(encoded, w_cross[0]).astype(BF)
    cross_values = dot_nn(encoded, w_cross[1]).astype(BF)

    offsets = pair_offset[0]
    owners = pair_query[0]
    half = pairs // 2
    shifts = list(range(half)) + [net.n_tok // 2 + index for index in range(half)]
    match = offsets[None, :] == jnp.asarray(shifts, jnp.int32)[:, None]
    slot_query = jnp.sum(jnp.where(match, owners[None, :], 0), axis=1)

    def to_owner(rows):
        ordered = jnp.sum(jnp.where(match[:, :, None], rows[None], 0.0), axis=1)
        return jnp.concatenate(
            [net.shift_tok(ordered[i : i + 1], shift) for i, shift in enumerate(shifts)], axis=0
        )

    def to_tokens(rows):
        got = jnp.concatenate(
            [
                net.shift_tok(rows[i : i + 1], net.n_tok - shift)
                for i, shift in enumerate(shifts)
            ],
            axis=0,
        )
        return jnp.sum(jnp.where(match[:, :, None], got[:, None], 0.0), axis=0)

    state = decoder_input.astype(F32)
    nquery = state.shape[0]
    of_slot = slot_query[:, None] == jnp.arange(nquery, dtype=jnp.int32)[None, :]

    def per_slot(rows):
        return jnp.sum(jnp.where(of_slot[:, :, None], rows[None], 0.0), axis=1)

    self_in = rms_norm(state, gain_master[2]).astype(BF)
    self_values = dot_nn(self_in, w_dec[0]).astype(BF)
    after_self = state + dot_nn(self_values, w_dec[1])
    cross_in = rms_norm(after_self, gain_master[3]).astype(BF)
    cross_query = dot_nn(cross_in, w_dec[2]).astype(BF)
    upstream = output_cotangent.astype(F32)
    up_low = output_cotangent.astype(BF)
    grad_act = dot_nn(up_low, x_down)

    head_mask = (
        jnp.arange(width, dtype=jnp.int32)[None, :] // head_size
        == jnp.arange(heads, dtype=jnp.int32)[:, None]
    )

    def by_head(rows):
        spread = jnp.where(head_mask[None], rows[:, None, :], 0.0)
        return spread.reshape(pairs * heads, width).astype(BF)

    def from_heads(rows):
        rows = rows.reshape(pairs, heads, width)
        return jnp.sum(jnp.where(head_mask[None], rows, 0.0), axis=1)

    token_query = net.own_first(to_tokens(per_slot(cross_query.astype(F32))))
    query_heads = by_head(token_query)
    inside = (segment[None, :] == counter[:, None])[:, None, :]
    scores = dot_nt(query_heads, cross_keys).reshape(pairs, heads, length) * SCALING
    scores = jnp.where(inside, scores, NEGATIVE)
    peak = jnp.max(scores, axis=2)
    expo = jnp.exp(scores - peak[:, :, None])
    total = jnp.sum(expo, axis=2)
    weighted = from_heads(
        lax.dot_general(
            expo.reshape(pairs * heads, length),
            cross_values.astype(F32),
            (((1,), (0,)), ((), ())),
            precision=lax.Precision.HIGHEST,
            preferred_element_type=F32,
        )
    )
    sent = jnp.concatenate(
        [net.own_first(weighted), net.own_first(peak), net.own_first(total)], axis=1
    )
    got = to_owner(sent)
    slot_peak, slot_total = got[:, width : width + heads], got[:, width + heads :]
    chosen = of_slot.T[:, :, None]
    row_peak = jnp.max(jnp.where(chosen, slot_peak[None], NEGATIVE), axis=1)
    factor = jnp.where(chosen, jnp.exp(slot_peak[None] - row_peak[:, None]), 0.0)
    row_total = jnp.sum(factor * slot_total[None], axis=1)
    factor = factor / row_total[:, None]
    wide = jnp.repeat(factor, head_size, axis=2)
    cross_wide = jnp.sum(wide * got[None, :, :width], axis=1)
    cross_out = cross_wide.astype(BF)
    row_log = row_peak + jnp.log(row_total)

    after_cross = after_self + dot_nn(cross_out, w_dec[3])
    final_in = rms_norm(after_cross, gain_master[4]).astype(BF)
    final_inner = dot_nn(final_in, x_up)
    grad_inner = gelu_back(final_inner, grad_act).astype(BF)
    grad_final_in = dot_nt(grad_inner, x_up)
    grad_state_four, grad_gain_four = norm_back(after_cross, gain_master[4], grad_final_in)
    grad_cross_total = upstream + grad_state_four
    cross_grad_low = grad_cross_total.astype(BF)
    grad_cross_out = dot_nt(cross_grad_low, w_dec[3]).astype(BF).astype(F32)
    row_inner = jnp.sum((grad_cross_out * cross_wide).reshape(nquery, heads, head_size), axis=2)
    back = to_tokens(per_slot(jnp.concatenate([grad_cross_out, row_log, row_inner], axis=1)))
    final_act = jax.nn.gelu(final_inner).astype(BF)
    decoder_output = after_cross + dot_nt(final_act, x_down)

    grad_heads = by_head(net.own_first(back[:, :width]))
    token_log = net.own_first(back[:, width : width + heads])
    token_inner = net.own_first(back[:, width + heads :])
    probs = jnp.exp(scores - token_log[:, :, None])
    grad_probs = dot_nt(grad_heads, cross_values).reshape(pairs, heads, length)
    grad_scores = (probs * (grad_probs - token_inner[:, :, None])).astype(BF)
    grad_scores = grad_scores.reshape(pairs * heads, length)
    probs_low = probs.reshape(pairs * heads, length).astype(BF)
    grad_values_cross = dot_tn(probs_low, grad_heads).astype(BF)
    grad_keys_cross = (dot_tn(grad_scores, query_heads) * SCALING).astype(BF)
    grad_query_part = from_heads(dot_nn(grad_scores, cross_keys))
    got_query = to_owner(net.own_first(grad_query_part))
    grad_query_cross = (
        jnp.sum(jnp.where(chosen, got_query[None], 0.0), axis=1) * SCALING
    ).astype(BF)
    grad_encoded = (
        dot_nt(grad_keys_cross, w_cross[0]) + dot_nt(grad_values_cross, w_cross[1])
    ).astype(BF)
    grad_cross_proj = jnp.stack(
        [dot_tn(encoded, grad_keys_cross).astype(BF), dot_tn(encoded, grad_values_cross).astype(BF)]
    )
    sum_cross = scatter(net, grad_cross_proj, 1)

    grad_cross_in = dot_nt(grad_query_cross, w_dec[2])
    grad_state_three, grad_gain_three = norm_back(after_self, gain_master[3], grad_cross_in)
    grad_self_total = grad_cross_total + grad_state_three
    self_grad_low = grad_self_total.astype(BF)
    grad_self_values = dot_nt(self_grad_low, w_dec[1]).astype(BF)
    grad_self_in = dot_nt(grad_self_values, w_dec[0])
    grad_state_two, grad_gain_two = norm_back(state, gain_master[2], grad_self_in)
    decoder_gradient = grad_self_total + grad_state_two
    packed = [
        self_in,
        self_values,
        cross_in,
        cross_out,
        final_in,
        up_low,
        grad_self_values,
        self_grad_low,
        grad_query_cross,
        cross_grad_low,
        grad_inner,
        final_act,
    ]
    spread = gather_small(net, jnp.concatenate(packed, axis=1))
    rank = lax.axis_index("dp") * net.n_tok + lax.axis_index("tok")
    own = decoder_master.shape[1]
    lefts = [
        lax.dynamic_slice_in_dim(spread, i * width + rank * own, own, axis=1) for i in range(6)
    ]
    rights = [spread[:, (6 + i) * width : (7 + i) * width] for i in range(4)]
    wide_size = final_act.shape[1]
    grad_dec = jnp.stack([dot_tn(lefts[i], rights[i]) for i in range(4)])
    grad_exp = jnp.stack(
        [
            dot_tn(lefts[4], spread[:, 10 * width : 10 * width + wide_size]),
            dot_tn(lefts[5], spread[:, 10 * width + wide_size :]),
        ]
    )

    grad_down = dot_tn(grad_encoded, activated).astype(BF)
    sum_down = scatter(net, grad_down[None], 0)
    grad_activated = dot_nn(grad_encoded, w_down)
    grad_inner_enc = gelu_back(inner, grad_activated).astype(BF)
    grad_up = dot_tn(normed_two, grad_inner_enc).astype(BF)
    sum_up = scatter(net, grad_up[None], 1)
    grad_normed_two = dot_nt(grad_inner_enc, w_up)
    grad_resid, grad_gain_one = norm_back(residual, gain_master[1], grad_normed_two)
    grad_residual = grad_encoded.astype(F32) + grad_resid
    attn_low = grad_residual.astype(BF)
    grad_out = dot_tn(net.own_first(attended), net.own_first(attn_low)).astype(BF)
    sum_out = scatter(net, grad_out[None], 0)
    grad_attended = dot_nt(attn_low, w_out).astype(BF)
    grad_queries, grad_keys, grad_values, diagonals = attention_backward(
        queries, keys, values, grad_attended, bias_rows, segment
    )
    grad_normed = (
        dot_nt(grad_queries, w_qkv[0])
        + dot_nt(grad_keys, w_qkv[1])
        + dot_nt(grad_values, w_qkv[2])
    )
    grad_qkv = jnp.stack(
        [dot_tn(normed, grad).astype(BF) for grad in (grad_queries, grad_keys, grad_values)]
    )
    sum_qkv = scatter(net, grad_qkv, 1)
    grad_input_part, grad_gain_zero = norm_back(hidden, gain_master[0], grad_normed)
    encoder_gradient = (grad_residual + grad_input_part)[None]

    grad_table = jnp.dot(
        net.own_first(diagonals, 0),
        onehot,
        precision=lax.Precision.HIGHEST,
        preferred_element_type=F32,
    ).T
    gain_grad = jnp.concatenate(
        [grad_gain_zero, grad_gain_one, grad_gain_two, grad_gain_three, grad_gain_four]
    )
    small = sum_small(net, jnp.concatenate([gain_grad, grad_table.reshape(-1)]))
    gain_sum = small[: 5 * width].reshape(5, width)
    bias_sum = small[5 * width :].reshape(buckets, heads)

    results = [decoder_output, encoder_gradient, decoder_gradient]
    groups = (
        (
            attention_master,
            attention_moment,
            attention_average,
            jnp.concatenate([sum_qkv, sum_out, sum_cross], axis=0),
        ),
        (
            feedforward_master,
            feedforward_moment,
            feedforward_average,
            jnp.concatenate([sum_up, sum_down], axis=0),
        ),
        (decoder_master, decoder_moment, decoder_average, grad_dec),
        (expansion_master, expansion_moment, expansion_average, grad_exp),
        (gain_master, gain_moment, gain_average, gain_sum),
        (bias_master, bias_moment, bias_average, bias_sum),
    )
    for weight, moment, average, gradient in groups:
        results.extend(update(weight, moment, average, gradient))
    return tuple(results)


def solution(mesh):
    spread = P(("dp", "tok"), None)
    weights = P(None, ("dp", "tok"), None)
    in_specs = (
        P(("dp", "tok"), None, None),
        spread,
        spread,
        spread,
        P("dp", None),
        P("dp", None),
        *[weights] * 12,
        *[P()] * 6,
    )
    out_specs = (spread, P(("dp", "tok"), None, None), spread, *[weights] * 16, *[P()] * 8)
    return jax.shard_map(
        per_device, mesh=mesh, in_specs=in_specs, out_specs=out_specs, check_vma=False
    )
```

time: 1880 us -> 713 us (0.38)
  local copies, waits for them, and re-layouts: 1220 us -> 78.9 us
  starting transfers between devices: 17.2 us -> 148 us
  Pallas kernels: 0 us -> 72 us
  blocking collectives: 71.2 us -> 0 us
  matrix products: 155 us -> 90 us
  other arithmetic: 85.7 us -> 51.7 us
  waiting for transfers between devices: 291 us -> 260 us
    gather x8 -> x0, local copies, waits for them, and re-layouts: 957 us -> none  [the longest x2 939 us: scores_of(): bias = jnp.transpose(jnp.take(bias_master, buckets, axis=0), (2, 0, 1))]
    ppermute x0 -> x162, waiting for transfers between devices: none -> 260 us  [the longest x38 154 us: flip_dp(): return lax.ppermute(array, 'dp', [(d, d ^ bit) for d in range(self.n_dp)])]
    reduce_scatter x4 -> x0, waiting for transfers between devices: 256 us -> none  [the longest x1 207 us: per_device(): lax.psum_scatter(feedforward_grad, ('dp', 'tok'), scatter_dimension=1, ti...]
    ppermute x0 -> x162, starting transfers between devices: none -> 148 us  [the longest x124 114 us: tok_to(): lax.ppermute(array, 'tok', [(t, where(t)) for t in range(self.n_tok)])]
    rev x1 -> x0, local copies, waits for them, and re-layouts: 91 us -> none  [diagonal_sums(): flipped = grid[:, :, ::-1]]
    pallas_call x0 -> x10, Pallas kernels: none -> 72 us  [the longest x8 28 us: place(): pl.pallas_call(place_kernel, in_specs=[pl.BlockSpec(memory_space=pltpu.SM...]
    dot_general x54 -> x49, matrix products: 152 us -> 90 us  [the longest x16 33.6 us: dot_nt(): lax.dot_general(left, right, (((1,), (1,)), ((), ())), preferred_element_...]
    unnamed x138 -> x442, local copies, waits for them, and re-layouts: 73.4 us -> 27.8 us
  transfers between devices with their start and end apart: 10 -> 162, of which waited for: 3 -> 58; matrix products, arithmetic and copies ran while one was open for 76% -> 18% of each run, Pallas kernels for 0% -> 6%
where the time goes in v1:
time: 713 us; the launch traced here: 706 us
  waiting for transfers between devices  260 us (36%)
  starting transfers between devices  148 us (21%)
  matrix products  90 us (13%)
  local copies, waits for them, and re-layouts  78.9 us (11%)
  Pallas kernels  72 us (10%)
  other arithmetic  51.7 us (7%)
    ppermute x38, waiting for transfers between devices, flip_dp(): return lax.ppermute(array, 'dp', [(d, d ^ bit) for d in range(self.n_dp)])  154 us
    ppermute x124, starting transfers between devices, tok_to(): lax.ppermute(array, 'tok', [(t, where(t)) for t in range(self.n_tok)])  114 us
    ppermute x124, waiting for transfers between devices, tok_to(): lax.ppermute(array, 'tok', [(t, where(t)) for t in range(self.n_tok)])  107 us
    ppermute x38, starting transfers between devices, flip_dp(): return lax.ppermute(array, 'dp', [(d, d ^ bit) for d in range(self.n_dp)])  34.1 us
    dot_general x16, matrix products, dot_nt(): lax.dot_general(left, right, (((1,), (1,)), ((), ())), preferred_element_...  33.6 us
    dot_general x15, matrix products, dot_nn(): lax.dot_general(left, right, (((1,), (0,)), ((), ())), preferred_element_...  31.8 us
    pallas_call x8, Pallas kernels, place(): pl.pallas_call(place_kernel, in_specs=[pl.BlockSpec(memory_space=pltpu.SM...  28 us
    unnamed x442, local copies, waits for them, and re-layouts  27.8 us
  transfers between devices with their start and end apart: 162, of which 58 were waited for; matrix products, arithmetic and copies ran while one was open for 18% of the time, Pallas kernels for 6%

profile of v1, /device:TPU:0, one launch (start us, length us, event | category | flops | bytes accessed | tf_op | source)
XLA Modules:
  0.0 705.6 jit_solution(16955889945554130951)
XLA Ops:
  15.9 5.1 collective-permute-start.30
  29.3 4.3 collective-permute-done.32
  56.3 5.2 collective-permute-done.81
  68.7 7.6 %collective-permute-done.82 = bf16[1,48,1536]{2,1,0:T(8,128)(2,1)S(1)} collective-permute-done((bf16[1,48,1536]{2,1,0:T(8,128)(2,1)S(1)}, bf16[1,48,1536]{2,1,0:T(8,128)(2,1)S(1)}, u32[]{:S(2)}, u32[]{:S(2)}) %collective-permute-start.82) | collective-permute-done | bytes 147488 | tf_op jit(solution)/shard_map/ppermute | solution.py:224
  77.9 6.8 collective-permute-done.83
  86.1 7.2 %collective-permute-done.42 = bf16[1,48,1536]{2,1,0:T(8,128)(2,1)S(1)} collective-permute-done((bf16[1,48,1536]{2,1,0:T(8,128)(2,1)S(1)}, bf16[1,48,1536]{2,1,0:T(8,128)(2,1)S(1)}, u32[]{:S(2)}, u32[]{:S(2)}) %collective-permute-start.42) | collective-permute-done | bytes 147488 | tf_op jit(solution)/shard_map/ppermute | solution.py:224
  94.0 4.1 collective-permute-start.1
  98.1 6.7 collective-permute-done.1
  107.9 5.3 collective-permute-done.3
  113.3 5.1 collective-permute-done.92
  118.5 4.3 collective-permute-start.52
  127.3 6.1 collective-permute-done.53
  135.5 6.2 collective-permute-done.35.refs_3_
  148.2 6.4 collective-permute-done.23.refs_2_
  157.4 17.6 %collective-permute-done.68.refs_3_ = bf16[2,192,384]{2,1,0:T(8,128)(2,1)S(1)} collective-permute-done((bf16[2,192,384]{2,1,0:T(8,128)(2,1)S(1)}, bf16[2,192,384]{2,1,0:T(8,128)(2,1)S(1)}, u32[]{:S(2)}, u32[]{:S(2)}) %collective-permute-start.68) | collective-permute-done | bytes 294944 | tf_op jit(solution)/shard_map/ppermute | solution.py:236
  181.8 9.5 %collective-permute-done.5.refs_2_ = bf16[4,192,384]{2,1,0:T(8,128)(2,1)S(1)} collective-permute-done((bf16[4,192,384]{2,1,0:T(8,128)(2,1)S(1)}, bf16[4,192,384]{2,1,0:T(8,128)(2,1)S(1)}, u32[]{:S(2)}, u32[]{:S(2)}) %collective-permute-start.5) | collective-permute-done | bytes 589856 | tf_op jit(solution)/shard_map/ppermute | solution.py:236
  191.9 12.0 %collective-permute-done.6.refs_3_ = bf16[4,192,384]{2,1,0:T(8,128)(2,1)S(1)} collective-permute-done((bf16[4,192,384]{2,1,0:T(8,128)(2,1)S(1)}, bf16[4,192,384]{2,1,0:T(8,128)(2,1)S(1)}, u32[]{:S(2)}, u32[]{:S(2)}) %collective-permute-start.6) | collective-permute-done | bytes 589856 | tf_op jit(solution)/shard_map/ppermute | solution.py:236
  213.9 17.3 %shard_map.450 = bf16[512,768]{1,0:T(8,128)(2,1)S(1)} custom-call(bf16[512,768]{1,0:T(8,128)(2,1)S(1)} %convolution_convert_fusion.13.q_ref, bf16[512,768]{1,0:T(8,128)(2,1)S(1)} %convolution_convert_fusion.12.k_ref, bf16[512,768]{1,0:T(8,128)(2,1)S(1)} %convolution_convert_fusion.11.v_ref, f32[6,2,512]{2,1,0:T(2,128)S(1)} %copy-done.9, ...), custom_call_target="tpu_custom_call" | custom-call | flops 2015232000 | bytes 3145728 | tf_op jit(solution)/shard_map/pallas_call | solution.py:175
  234.4 3.7 shard_map.448
  243.7 3.9 collective-permute-done.44.refs_1_
  247.6 12.7 %collective-permute-done.55.refs_1_ = bf16[1,192,1536]{2,1,0:T(8,128)(2,1)} collective-permute-done((bf16[1,192,1536]{2,1,0:T(8,128)(2,1)}, bf16[1,192,1536]{2,1,0:T(8,128)(2,1)}, u32[]{:S(2)}, u32[]{:S(2)}) %collective-permute-start.55) | collective-permute-done | bytes 589856 | tf_op jit(solution)/shard_map/ppermute | solution.py:236
  260.7 11.7 %collective-permute-done.46.refs_3_ = bf16[1,192,1536]{2,1,0:T(8,128)(2,1)S(1)} collective-permute-done((bf16[1,192,1536]{2,1,0:T(8,128)(2,1)S(1)}, bf16[1,192,1536]{2,1,0:T(8,128)(2,1)S(1)}, u32[]{:S(2)}, u32[]{:S(2)}) %collective-permute-start.46) | collective-permute-done | bytes 589856 | tf_op jit(solution)/shard_map/ppermute | solution.py:236
  281.1 4.2 shard_map.452
  287.3 7.1 %fusion.21 = f32[512,3072]{1,0:T(8,128)} fusion(bf16[1,768,3072]{2,1,0:T(8,128)(2,1)} %shard_map.452, f32[512,768]{1,0:T(8,128)S(1)} %get-tuple-element.285, f32[768]{0:T(1024)S(1)} %copy-done.78, f32[512]{0:T(512)S(1)} %fusion.184), kind=kOutput, calls=%fused_computation.26 | convolution fusion | flops 2417098752 | bytes 12588032 | tf_op jit(solution)/shard_map/dot_general | solution.py:36
  300.4 5.4 shard_map.453
  305.8 8.1 %add_convert_fusion.7 = bf16[512,768]{1,0:T(8,128)(2,1)S(1)} fusion(f32[512,768]{1,0:T(8,128)S(1)} %copy-done.20, bf16[1,768,3072]{2,1,0:T(8,128)(2,1)} %shard_map.453, f32[512,3072]{1,0:T(8,128)} %fusion.21), kind=kOutput, calls=%fused_computation.69 | convolution fusion | flops 2430861312 | bytes 13369344 | tf_op jit(solution)/shard_map/dot_general | solution.py:40
  319.1 8.2 %collective-permute-done.95.refs_1_ = bf16[1,192,1536]{2,1,0:T(8,128)(2,1)S(1)} collective-permute-done((bf16[1,192,1536]{2,1,0:T(8,128)(2,1)}, bf16[1,192,1536]{2,1,0:T(8,128)(2,1)S(1)}, u32[]{:S(2)}, u32[]{:S(2)}) %collective-permute-start.95) | collective-permute-done | bytes 589856 | tf_op jit(solution)/shard_map/ppermute | solution.py:236
  328.6 4.6 collective-permute-done.96.refs_2_
  333.8 5.4 collective-permute-done.86.refs_3_
  339.2 5.8 collective-permute-done.97.refs_3_
  354.8 4.6 shard_map.455
  359.5 4.2 shard_map.456
  421.9 6.4 fusion.6
  428.4 4.7 fusion.24
  440.2 26.6 %shard_map.457 = (bf16[512,768]{1,0:T(8,128)(2,1)S(1)}, bf16[512,768]{1,0:T(8,128)(2,1)S(1)}, bf16[512,768]{1,0:T(8,128)(2,1)S(1)}, f32[6,2,512]{2,1,0:T(2,128)S(1)}) custom-call(bf16[512,768]{1,0:T(8,128)(2,1)S(1)} %copy-done.17, bf16[512,768]{1,0:T(8,128)(2,1)S(1)} %copy-done.15, bf16[512,768]{1,0:T(8,128)(2,1)S(1)} %copy-done.13, ...), custom_call_target="tpu_custom_call" | custom-call | flops 5038080000 | bytes 5505024 | tf_op jit(solution)/shard_map/pallas_call | solution.py:194
  478.5 4.5 fusion.23
  555.5 4.5 collective-permute-done.125
  574.2 4.9 collective-permute-done.155
  587.5 7.8 %concatenate.204 = bf16[64,13824]{1,0:T(8,128)(2,1)S(1)} concatenate(bf16[2,13824]{1,0:T(2,128)(2,1)} %constant_dynamic-update-slice_fusion.40, bf16[2,13824]{1,0:T(2,128)(2,1)} %copy-done.60, bf16[2,13824]{1,0:T(2,128)(2,1)} %copy-done.59, bf16[2,13824]{1,0:T(2,128)(2,1)} %copy-done.58, bf16[8,13824]{1,0:T(8,128)(2,1)} %copy-done.46, bf16[16,13824]{1,0:T(8,128)(2,1)} %copy-done.47, ...), dimensions={0} | concatenate | bytes 3538944 | tf_op jit(solution)/shard_map/concatenate | solution.py:363
  606.8 3.8 collective-permute-done.132
  620.3 5.1 collective-permute-done.117
  634.0 4.9 collective-permute-done.118
  650.6 5.4 collective-permute-done.138
  656.8 7.3 %collective-permute-done.145 = bf16[1,2,192,1536]{3,2,1,0:T(8,128)(2,1)S(1)} collective-permute-done((bf16[1,2,192,1536]{3,2,1,0:T(8,128)(2,1)S(1)}, bf16[1,2,192,1536]{3,2,1,0:T(8,128)(2,1)S(1)}, u32[]{:S(2)}, u32[]{:S(2)}) %collective-permute-start.145) | collective-permute-done | bytes 1179680 | tf_op jit(solution)/shard_map/ppermute | solution.py:236
  667.1 7.1 %collective-permute-done.139 = bf16[1,192,1536]{2,1,0:T(8,128)(2,1)S(1)} collective-permute-done((bf16[1,192,1536]{2,1,0:T(8,128)(2,1)S(1)}, bf16[1,192,1536]{2,1,0:T(8,128)(2,1)S(1)}, u32[]{:S(2)}, u32[]{:S(2)}) %collective-permute-start.139) | collective-permute-done | bytes 589856 | tf_op jit(solution)/shard_map/ppermute | solution.py:236
  683.1 6.7 collective-permute-start.148
  689.8 7.3 %collective-permute-done.141 = bf16[1,48,1536]{2,1,0:T(8,128)(2,1)S(1)} collective-permute-done((bf16[1,48,1536]{2,1,0:T(8,128)(2,1)S(1)}, bf16[1,48,1536]{2,1,0:T(8,128)(2,1)S(1)}, u32[]{:S(2)}, u32[]{:S(2)}) %collective-permute-start.141) | collective-permute-done | bytes 147488 | tf_op jit(solution)/shard_map/ppermute | solution.py:224
  697.3 4.2 collective-permute-done.148
  (988 shorter events, 363.6 us)
Async XLA Ops:
  1.9 37.0 %collective-permute-start = (bf16[4,24,384]{2,1,0:T(8,128)(2,1)S(1)}, bf16[4,24,384]{2,1,0:T(8,128)(2,1)S(1)}, u32[]{:S(2)}, u32[]{:S(2)}) collective-permute-start(bf16[4,24,384]{2,1,0:T(8,128)(2,1)S(1)} %broadcast_select_fusion.18), channel_id=1, source_target_pairs={{0,1},{1,0},{2,3},{3,2},{4,5},{5,4},{6,7},{7,6},{8,9},{9,8},{10,11... | collective-permute-start | bytes 221192 | tf_op jit(solution)/shard_map/ppermute | solution.py:224
  4.1 29.5 %collective-permute-start.18 = (bf16[3,24,384]{2,1,0:T(8,128)(2,1)S(1)}, bf16[3,24,384]{2,1,0:T(8,128)(2,1)S(1)}, u32[]{:S(2)}, u32[]{:S(2)}) collective-permute-start(bf16[3,24,384]{2,1,0:T(8,128)(2,1)S(1)} %broadcast_select_fusion.22), channel_id=1, source_target_pairs={{0,1},{1,0},{2,3},{3,2},{4,5},{5,4},{6,7},{7,6},{8,9},{9,8},{10,11... | collective-permute-start | bytes 165896 | tf_op jit(solution)/shard_map/ppermute | solution.py:224
  4.4 32.3 %collective-permute-start.40 = (bf16[1,24,1536]{2,1,0:T(8,128)(2,1)S(1)}, bf16[1,24,1536]{2,1,0:T(8,128)(2,1)S(1)}, u32[]{:S(2)}, u32[]{:S(2)}) collective-permute-start(bf16[1,24,1536]{2,1,0:T(8,128)(2,1)S(1)} %broadcast_select_fusion.14), channel_id=1, source_target_pairs={{0,1},{1,0},{2,3},{3,2},{4,5},{5,4},{6,7},{7,6},{8,9},{9,8},{10,11... | collective-permute-start | bytes 221192 | tf_op jit(solution)/shard_map/ppermute | solution.py:224
  15.7 21.9 %collective-permute-start.80 = (bf16[1,24,1536]{2,1,0:T(8,128)(2,1)S(1)}, bf16[1,24,1536]{2,1,0:T(8,128)(2,1)S(1)}, u32[]{:S(2)}, u32[]{:S(2)}) collective-permute-start(bf16[1,24,1536]{2,1,0:T(8,128)(2,1)S(1)} %broadcast_select_fusion.6), channel_id=1, source_target_pairs={{0,1},{1,0},{2,3},{3,2},{4,5},{5,4},{6,7},{7,6},{8,9},{9,8},{10,11... | collective-permute-start | bytes 221192 | tf_op jit(solution)/shard_map/ppermute | solution.py:224
  44.7 78.2 %collective-permute-start.36 = (bf16[1,192,384]{2,1,0:T(8,128)(2,1)S(1)}, bf16[1,192,384]{2,1,0:T(8,128)(2,1)S(1)}, u32[]{:S(2)}, u32[]{:S(2)}) collective-permute-start(bf16[1,192,384]{2,1,0:T(8,128)(2,1)S(1)} %constant_dynamic-update-slice_fusion.10.refs_0_), channel_id=1, source_target_pairs={{0,1},{1,0},{2,3},{3,2},{4,5},{5,4},{6,7},{7,6},{8,9},{9,8},{10,11... | collective-permute-start | bytes 442376 | tf_op jit(solution)/shard_map/ppermute | solution.py:224
  47.5 76.5 %collective-permute-start.34 = (bf16[1,192,384]{2,1,0:T(8,128)(2,1)S(1)}, bf16[1,192,384]{2,1,0:T(8,128)(2,1)S(1)}, u32[]{:S(2)}, u32[]{:S(2)}) collective-permute-start(bf16[1,192,384]{2,1,0:T(8,128)(2,1)S(1)} %constant_dynamic-update-slice_fusion.10.refs_0_), channel_id=1, source_target_pairs={{0,16},{8,24},{16,0},{24,8},{1,17},{9,25},{17,1},{25,9},{2,18},{10... | collective-permute-start | bytes 442376 | tf_op jit(solution)/shard_map/ppermute | solution.py:236
  50.8 73.7 %collective-permute-start.33 = (bf16[1,192,384]{2,1,0:T(8,128)(2,1)S(1)}, bf16[1,192,384]{2,1,0:T(8,128)(2,1)S(1)}, u32[]{:S(2)}, u32[]{:S(2)}) collective-permute-start(bf16[1,192,384]{2,1,0:T(8,128)(2,1)S(1)} %constant_dynamic-update-slice_fusion.10.refs_0_), channel_id=1, source_target_pairs={{0,8},{8,0},{16,24},{24,16},{1,9},{9,1},{17,25},{25,17},{2,10},{10... | collective-permute-start | bytes 442376 | tf_op jit(solution)/shard_map/ppermute | solution.py:236
  52.3 41.6 %collective-permute-start.43 = (bf16[1,48,1536]{2,1,0:T(8,128)(2,1)S(1)}, bf16[1,48,1536]{2,1,0:T(8,128)(2,1)S(1)}, u32[]{:S(2)}, u32[]{:S(2)}) collective-permute-start(bf16[1,48,1536]{2,1,0:T(8,128)(2,1)S(1)} %pad_maximum_fusion.6), channel_id=1, source_target_pairs={{0,2},{1,3},{2,4},{3,5},{4,6},{5,7},{6,0},{7,1},{8,10},{9,11},{10,... | collective-permute-start | bytes 442376 | tf_op jit(solution)/shard_map/ppermute | solution.py:224
  107.8 18.9 %collective-permute-start.54 = (bf16[1,48,1536]{2,1,0:T(8,128)(2,1)S(1)}, bf16[1,48,1536]{2,1,0:T(8,128)(2,1)S(1)}, u32[]{:S(2)}, u32[]{:S(2)}) collective-permute-start(bf16[1,48,1536]{2,1,0:T(8,128)(2,1)S(1)} %pad_maximum_fusion.7), channel_id=1, source_target_pairs={{0,2},{1,3},{2,4},{3,5},{4,6},{5,7},{6,0},{7,1},{8,10},{9,11},{10,... | collective-permute-start | bytes 442376 | tf_op jit(solution)/shard_map/ppermute | solution.py:224
  144.8 30.7 %collective-permute-start.4 = (bf16[4,192,384]{2,1,0:T(8,128)(2,1)S(1)}, bf16[4,192,384]{2,1,0:T(8,128)(2,1)S(1)}, u32[]{:S(2)}, u32[]{:S(2)}) collective-permute-start(bf16[4,192,384]{2,1,0:T(8,128)(2,1)S(1)} %constant_dynamic-update-slice_fusion.refs_0_), channel_id=1, source_target_pairs={{0,8},{8,0},{16,24},{24,16},{1,9},{9,1},{17,25},{25,17},{2,10},{10... | collective-permute-start | bytes 1769480 | tf_op jit(solution)/shard_map/ppermute | solution.py:236
  146.3 28.7 %collective-permute-start.68 = (bf16[2,192,384]{2,1,0:T(8,128)(2,1)S(1)}, bf16[2,192,384]{2,1,0:T(8,128)(2,1)S(1)}, u32[]{:S(2)}, u32[]{:S(2)}) collective-permute-start(bf16[2,192,384]{2,1,0:T(8,128)(2,1)S(1)} %collective-permute-done.67.refs_2_), channel_id=1, source_target_pairs={{0,8},{8,0},{16,24},{24,16},{1,9},{9,1},{17,25},{25,17},{2,10},{10... | collective-permute-start | bytes 884744 | tf_op jit(solution)/shard_map/ppermute | solution.py:236
  147.5 27.5 %collective-permute-start.71 = (bf16[2,192,384]{2,1,0:T(8,128)(2,1)S(1)}, bf16[2,192,384]{2,1,0:T(8,128)(2,1)S(1)}, u32[]{:S(2)}, u32[]{:S(2)}) collective-permute-start(bf16[2,192,384]{2,1,0:T(8,128)(2,1)S(1)} %collective-permute-done.67.refs_2_), channel_id=1, source_target_pairs={{0,1},{1,0},{2,3},{3,2},{4,5},{5,4},{6,7},{7,6},{8,9},{9,8},{10,11... | collective-permute-start | bytes 884744 | tf_op jit(solution)/shard_map/ppermute | solution.py:224
  154.6 22.6 %collective-permute-start.70 = (bf16[2,192,384]{2,1,0:T(8,128)(2,1)S(1)}, bf16[2,192,384]{2,1,0:T(8,128)(2,1)S(1)}, u32[]{:S(2)}, u32[]{:S(2)}) collective-permute-start(bf16[2,192,384]{2,1,0:T(8,128)(2,1)S(1)} %collective-permute-done.66.refs_1_), channel_id=1, source_target_pairs={{0,1},{1,0},{2,3},{3,2},{4,5},{5,4},{6,7},{7,6},{8,9},{9,8},{10,11... | collective-permute-start | bytes 884744 | tf_op jit(solution)/shard_map/ppermute | solution.py:224
  157.4 20.4 %collective-permute-start.24 = (bf16[3,192,384]{2,1,0:T(8,128)(2,1)S(1)}, bf16[3,192,384]{2,1,0:T(8,128)(2,1)S(1)}, u32[]{:S(2)}, u32[]{:S(2)}) collective-permute-start(bf16[3,192,384]{2,1,0:T(8,128)(2,1)S(1)} %collective-permute-done.22.refs_1_), channel_id=1, source_target_pairs={{0,16},{8,24},{16,0},{24,8},{1,17},{9,25},{17,1},{25,9},{2,18},{10... | collective-permute-start | bytes 1327112 | tf_op jit(solution)/shard_map/ppermute | solution.py:236
  175.5 28.4 %collective-permute-start.6 = (bf16[4,192,384]{2,1,0:T(8,128)(2,1)S(1)}, bf16[4,192,384]{2,1,0:T(8,128)(2,1)S(1)}, u32[]{:S(2)}, u32[]{:S(2)}) collective-permute-start(bf16[4,192,384]{2,1,0:T(8,128)(2,1)S(1)} %collective-permute-done.4.refs_1_), channel_id=1, source_target_pairs={{0,16},{8,24},{16,0},{24,8},{1,17},{9,25},{17,1},{25,9},{2,18},{10... | collective-permute-start | bytes 1769480 | tf_op jit(solution)/shard_map/ppermute | solution.py:236
  177.8 26.1 %collective-permute-start.28 = (bf16[3,192,384]{2,1,0:T(8,128)(2,1)S(1)}, bf16[3,192,384]{2,1,0:T(8,128)(2,1)S(1)}, u32[]{:S(2)}, u32[]{:S(2)}) collective-permute-start(bf16[3,192,384]{2,1,0:T(8,128)(2,1)S(1)} %collective-permute-done.24.refs_3_), channel_id=1, source_target_pairs={{0,1},{1,0},{2,3},{3,2},{4,5},{5,4},{6,7},{7,6},{8,9},{9,8},{10,11... | collective-permute-start | bytes 1327112 | tf_op jit(solution)/shard_map/ppermute | solution.py:224
  191.3 40.0 %collective-permute-start.7 = (bf16[4,192,384]{2,1,0:T(8,128)(2,1)S(1)}, bf16[4,192,384]{2,1,0:T(8,128)(2,1)S(1)}, u32[]{:S(2)}, u32[]{:S(2)}) collective-permute-start(bf16[4,192,384]{2,1,0:T(8,128)(2,1)S(1)} %constant_dynamic-update-slice_fusion.refs_0_), channel_id=1, source_target_pairs={{0,1},{1,0},{2,3},{3,2},{4,5},{5,4},{6,7},{7,6},{8,9},{9,8},{10,11... | collective-permute-start | bytes 1769480 | tf_op jit(solution)/shard_map/ppermute | solution.py:224
  191.3 40.1 %collective-permute-start.45 = (bf16[1,192,1536]{2,1,0:T(8,128)(2,1)S(1)}, bf16[1,192,1536]{2,1,0:T(8,128)(2,1)S(1)}, u32[]{:S(2)}, u32[]{:S(2)}) collective-permute-start(bf16[1,192,1536]{2,1,0:T(8,128)(2,1)S(1)} %constant_dynamic-update-slice_fusion.15.refs_0_), channel_id=1, source_target_pairs={{0,16},{8,24},{16,0},{24,8},{1,17},{9,25},{17,1},{25,9},{2,18},{10... | collective-permute-start | bytes 1769480 | tf_op jit(solution)/shard_map/ppermute | solution.py:236
  191.6 40.7 %collective-permute-start.8 = (bf16[4,192,384]{2,1,0:T(8,128)(2,1)S(1)}, bf16[4,192,384]{2,1,0:T(8,128)(2,1)S(1)}, u32[]{:S(2)}, u32[]{:S(2)}) collective-permute-start(bf16[4,192,384]{2,1,0:T(8,128)(2,1)S(1)} %collective-permute-done.4.refs_1_), channel_id=1, source_target_pairs={{0,1},{1,0},{2,3},{3,2},{4,5},{5,4},{6,7},{7,6},{8,9},{9,8},{10,11... | collective-permute-start | bytes 1769480 | tf_op jit(solution)/shard_map/ppermute | solution.py:224
  203.9 28.1 %collective-permute-start.9 = (bf16[4,192,384]{2,1,0:T(8,128)(2,1)S(1)}, bf16[4,192,384]{2,1,0:T(8,128)(2,1)S(1)}, u32[]{:S(2)}, u32[]{:S(2)}) collective-permute-start(bf16[4,192,384]{2,1,0:T(8,128)(2,1)S(1)} %collective-permute-done.5.refs_2_), channel_id=1, source_target_pairs={{0,1},{1,0},{2,3},{3,2},{4,5},{5,4},{6,7},{7,6},{8,9},{9,8},{10,11... | collective-permute-start | bytes 1769480 | tf_op jit(solution)/shard_map/ppermute | solution.py:224
  204.7 29.2 %collective-permute-start.10 = (bf16[4,192,384]{2,1,0:T(8,128)(2,1)S(1)}, bf16[4,192,384]{2,1,0:T(8,128)(2,1)S(1)}, u32[]{:S(2)}, u32[]{:S(2)}) collective-permute-start(bf16[4,192,384]{2,1,0:T(8,128)(2,1)S(1)} %collective-permute-done.6.refs_3_), channel_id=1, source_target_pairs={{0,1},{1,0},{2,3},{3,2},{4,5},{5,4},{6,7},{7,6},{8,9},{9,8},{10,11... | collective-permute-start | bytes 1769480 | tf_op jit(solution)/shard_map/ppermute | solution.py:224
  232.0 41.1 %collective-permute-start.56 = (bf16[1,192,1536]{2,1,0:T(8,128)(2,1)}, bf16[1,192,1536]{2,1,0:T(8,128)(2,1)}, u32[]{:S(2)}, u32[]{:S(2)}) collective-permute-start(bf16[1,192,1536]{2,1,0:T(8,128)(2,1)} %constant_dynamic-update-slice_fusion.20.refs_0_), channel_id=1, source_target_pairs={{0,16},{8,24},{16,0},{24,8},{1,17},{9,25},{17,1},{25,9},{2,18},{10... | collective-permute-start | bytes 1769480 | tf_op jit(solution)/shard_map/ppermute | solution.py:236
  232.3 28.0 %collective-permute-start.55 = (bf16[1,192,1536]{2,1,0:T(8,128)(2,1)}, bf16[1,192,1536]{2,1,0:T(8,128)(2,1)}, u32[]{:S(2)}, u32[]{:S(2)}) collective-permute-start(bf16[1,192,1536]{2,1,0:T(8,128)(2,1)} %constant_dynamic-update-slice_fusion.20.refs_0_), channel_id=1, source_target_pairs={{0,8},{8,0},{16,24},{24,16},{1,9},{9,1},{17,25},{25,17},{2,10},{10... | collective-permute-start | bytes 1769480 | tf_op jit(solution)/shard_map/ppermute | solution.py:236
  233.8 38.6 %collective-permute-start.46 = (bf16[1,192,1536]{2,1,0:T(8,128)(2,1)S(1)}, bf16[1,192,1536]{2,1,0:T(8,128)(2,1)S(1)}, u32[]{:S(2)}, u32[]{:S(2)}) collective-permute-start(bf16[1,192,1536]{2,1,0:T(8,128)(2,1)S(1)} %collective-permute-done.45.refs_2_), channel_id=1, source_target_pairs={{0,8},{8,0},{16,24},{24,16},{1,9},{9,1},{17,25},{25,17},{2,10},{10... | collective-permute-start | bytes 1769480 | tf_op jit(solution)/shard_map/ppermute | solution.py:236
  243.6 30.9 %collective-permute-start.49 = (bf16[1,192,1536]{2,1,0:T(8,128)(2,1)S(1)}, bf16[1,192,1536]{2,1,0:T(8,128)(2,1)S(1)}, u32[]{:S(2)}, u32[]{:S(2)}) collective-permute-start(bf16[1,192,1536]{2,1,0:T(8,128)(2,1)S(1)} %collective-permute-done.45.refs_2_), channel_id=1, source_target_pairs={{0,1},{1,0},{2,3},{3,2},{4,5},{5,4},{6,7},{7,6},{8,9},{9,8},{10,11... | collective-permute-start | bytes 1769480 | tf_op jit(solution)/shard_map/ppermute | solution.py:224
  247.6 27.6 %collective-permute-start.48 = (bf16[1,192,1536]{2,1,0:T(8,128)(2,1)S(1)}, bf16[1,192,1536]{2,1,0:T(8,128)(2,1)S(1)}, u32[]{:S(2)}, u32[]{:S(2)}) collective-permute-start(bf16[1,192,1536]{2,1,0:T(8,128)(2,1)S(1)} %collective-permute-done.44.refs_1_), channel_id=1, source_target_pairs={{0,1},{1,0},{2,3},{3,2},{4,5},{5,4},{6,7},{7,6},{8,9},{9,8},{10,11... | collective-permute-start | bytes 1769480 | tf_op jit(solution)/shard_map/ppermute | solution.py:224
  295.0 21.8 %collective-permute-start.87 = (bf16[1,192,1536]{2,1,0:T(8,128)(2,1)}, bf16[1,192,1536]{2,1,0:T(8,128)(2,1)}, u32[]{:S(2)}, u32[]{:S(2)}) collective-permute-start(bf16[1,192,1536]{2,1,0:T(8,128)(2,1)} %constant_dynamic-update-slice_fusion.30.refs_0_), channel_id=1, source_target_pairs={{0,1},{1,0},{2,3},{3,2},{4,5},{5,4},{6,7},{7,6},{8,9},{9,8},{10,11... | collective-permute-start | bytes 1769480 | tf_op jit(solution)/shard_map/ppermute | solution.py:224
  297.3 21.1 %collective-permute-start.85 = (bf16[1,192,1536]{2,1,0:T(8,128)(2,1)}, bf16[1,192,1536]{2,1,0:T(8,128)(2,1)S(1)}, u32[]{:S(2)}, u32[]{:S(2)}) collective-permute-start(bf16[1,192,1536]{2,1,0:T(8,128)(2,1)} %constant_dynamic-update-slice_fusion.30.refs_0_), channel_id=1, source_target_pairs={{0,16},{8,24},{16,0},{24,8},{1,17},{9,25},{17,1},{25,9},{2,18},{10... | collective-permute-start | bytes 1769480 | tf_op jit(solution)/shard_map/ppermute | solution.py:236
  298.3 20.2 %collective-permute-start.84 = (bf16[1,192,1536]{2,1,0:T(8,128)(2,1)}, bf16[1,192,1536]{2,1,0:T(8,128)(2,1)S(1)}, u32[]{:S(2)}, u32[]{:S(2)}) collective-permute-start(bf16[1,192,1536]{2,1,0:T(8,128)(2,1)} %constant_dynamic-update-slice_fusion.30.refs_0_), channel_id=1, source_target_pairs={{0,8},{8,0},{16,24},{24,16},{1,9},{9,1},{17,25},{25,17},{2,10},{10... | collective-permute-start | bytes 1769480 | tf_op jit(solution)/shard_map/ppermute | solution.py:236
  298.8 29.7 %collective-permute-start.98 = (bf16[1,192,1536]{2,1,0:T(8,128)(2,1)}, bf16[1,192,1536]{2,1,0:T(8,128)(2,1)S(1)}, u32[]{:S(2)}, u32[]{:S(2)}) collective-permute-start(bf16[1,192,1536]{2,1,0:T(8,128)(2,1)} %copy-done), channel_id=1, source_target_pairs={{0,1},{1,0},{2,3},{3,2},{4,5},{5,4},{6,7},{7,6},{8,9},{9,8},{10,11... | collective-permute-start | bytes 1769480 | tf_op jit(solution)/shard_map/ppermute | solution.py:224
  298.8 28.5 %collective-permute-start.95 = (bf16[1,192,1536]{2,1,0:T(8,128)(2,1)}, bf16[1,192,1536]{2,1,0:T(8,128)(2,1)S(1)}, u32[]{:S(2)}, u32[]{:S(2)}) collective-permute-start(bf16[1,192,1536]{2,1,0:T(8,128)(2,1)} %copy-done), channel_id=1, source_target_pairs={{0,8},{8,0},{16,24},{24,16},{1,9},{9,1},{17,25},{25,17},{2,10},{10... | collective-permute-start | bytes 1769480 | tf_op jit(solution)/shard_map/ppermute | solution.py:236
  318.5 20.7 %collective-permute-start.86 = (bf16[1,192,1536]{2,1,0:T(8,128)(2,1)S(1)}, bf16[1,192,1536]{2,1,0:T(8,128)(2,1)S(1)}, u32[]{:S(2)}, u32[]{:S(2)}) collective-permute-start(bf16[1,192,1536]{2,1,0:T(8,128)(2,1)S(1)} %collective-permute-done.85.refs_2_), channel_id=1, source_target_pairs={{0,8},{8,0},{16,24},{24,16},{1,9},{9,1},{17,25},{25,17},{2,10},{10... | collective-permute-start | bytes 1769480 | tf_op jit(solution)/shard_map/ppermute | solution.py:236
  483.8 30.9 %collective-permute-start.115 = (f32[1,768]{1,0:T(1,128)}, f32[1,768]{1,0:T(1,128)}, u32[]{:S(2)}, u32[]{:S(2)}) collective-permute-start(f32[1,768]{1,0:T(1,128)} %get-tuple-element.258), channel_id=1, source_target_pairs={{0,7},{1,0},{2,1},{3,2},{4,3},{5,4},{6,5},{7,6},{8,15},{9,8},{10,9... | collective-permute-start | bytes 9224 | tf_op jit(solution)/shard_map/ppermute | solution.py:224
  486.8 29.0 %collective-permute-start.114 = (f32[1,768]{1,0:T(1,128)}, f32[1,768]{1,0:T(1,128)}, u32[]{:S(2)}, u32[]{:S(2)}) collective-permute-start(f32[1,768]{1,0:T(1,128)} %get-tuple-element.259), channel_id=1, source_target_pairs={{0,6},{1,7},{2,0},{3,1},{4,2},{5,3},{6,4},{7,5},{8,14},{9,15},{10,... | collective-permute-start | bytes 9224 | tf_op jit(solution)/shard_map/ppermute | solution.py:224
  486.8 30.2 %collective-permute-start.113 = (f32[1,768]{1,0:T(1,128)}, f32[1,768]{1,0:T(1,128)}, u32[]{:S(2)}, u32[]{:S(2)}) collective-permute-start(f32[1,768]{1,0:T(1,128)} %get-tuple-element.260), channel_id=1, source_target_pairs={{0,5},{1,6},{2,7},{3,0},{4,1},{5,2},{6,3},{7,4},{8,13},{9,14},{10,... | collective-permute-start | bytes 9224 | tf_op jit(solution)/shard_map/ppermute | solution.py:224
  486.8 30.8 %collective-permute-start.112 = (f32[1,768]{1,0:T(1,128)}, f32[1,768]{1,0:T(1,128)}, u32[]{:S(2)}, u32[]{:S(2)}) collective-permute-start(f32[1,768]{1,0:T(1,128)} %get-tuple-element.261), channel_id=1, source_target_pairs={{0,4},{1,5},{2,6},{3,7},{4,0},{5,1},{6,2},{7,3},{8,12},{9,13},{10,... | collective-permute-start | bytes 9224 | tf_op jit(solution)/shard_map/ppermute | solution.py:224
  489.5 28.2 %collective-permute-start.111 = (f32[1,768]{1,0:T(1,128)}, f32[1,768]{1,0:T(1,128)}, u32[]{:S(2)}, u32[]{:S(2)}) collective-permute-start(f32[1,768]{1,0:T(1,128)} %get-tuple-element.262), channel_id=1, source_target_pairs={{0,3},{1,4},{2,5},{3,6},{4,7},{5,0},{6,1},{7,2},{8,11},{9,12},{10,... | collective-permute-start | bytes 9224 | tf_op jit(solution)/shard_map/ppermute | solution.py:224
  517.0 27.5 %collective-permute-start.123 = (bf16[1,768,384]{2,1,0:T(8,128)(2,1)}, bf16[1,768,384]{2,1,0:T(8,128)(2,1)S(1)}, u32[]{:S(2)}, u32[]{:S(2)}) collective-permute-start(bf16[1,768,384]{2,1,0:T(8,128)(2,1)} %get-tuple-element.179), channel_id=1, source_target_pairs={{0,1},{1,0},{2,3},{3,2},{4,5},{5,4},{6,7},{7,6},{8,9},{9,8},{10,11... | collective-permute-start | bytes 1769480 | tf_op jit(solution)/shard_map/ppermute | solution.py:224
  517.6 65.0 %collective-permute-start.130 = (bf16[2,768,384]{2,1,0:T(8,128)(2,1)}, bf16[2,768,384]{2,1,0:T(8,128)(2,1)}, u32[]{:S(2)}, u32[]{:S(2)}) collective-permute-start(bf16[2,768,384]{2,1,0:T(8,128)(2,1)} %get-tuple-element.163), channel_id=1, source_target_pairs={{0,1},{1,0},{2,3},{3,2},{4,5},{5,4},{6,7},{7,6},{8,9},{9,8},{10,11... | collective-permute-start | bytes 3538952 | tf_op jit(solution)/shard_map/ppermute | solution.py:224
  565.2 37.3 %collective-permute-start.116 = (bf16[3,768,384]{2,1,0:T(8,128)(2,1)}, bf16[3,768,384]{2,1,0:T(8,128)(2,1)}, u32[]{:S(2)}, u32[]{:S(2)}) collective-permute-start(bf16[3,768,384]{2,1,0:T(8,128)(2,1)} %get-tuple-element.157), channel_id=1, source_target_pairs={{0,1},{1,0},{2,3},{3,2},{4,5},{5,4},{6,7},{7,6},{8,9},{9,8},{10,11... | collective-permute-start | bytes 5308424 | tf_op jit(solution)/shard_map/ppermute | solution.py:224
  566.5 60.8 %collective-permute-start.137 = (bf16[1,768,1536]{2,1,0:T(8,128)(2,1)}, bf16[1,768,1536]{2,1,0:T(8,128)(2,1)}, u32[]{:S(2)}, u32[]{:S(2)}) collective-permute-start(bf16[1,768,1536]{2,1,0:T(8,128)(2,1)} %get-tuple-element.151), channel_id=1, source_target_pairs={{0,1},{1,0},{2,3},{3,2},{4,5},{5,4},{6,7},{7,6},{8,9},{9,8},{10,11... | collective-permute-start | bytes 7077896 | tf_op jit(solution)/shard_map/ppermute | solution.py:224
  579.2 51.8 %collective-permute-start.144 = (bf16[1,768,1536]{2,1,0:T(8,128)(2,1)}, bf16[1,768,1536]{2,1,0:T(8,128)(2,1)}, u32[]{:S(2)}, u32[]{:S(2)}) collective-permute-start(bf16[1,768,1536]{2,1,0:T(8,128)(2,1)} %get-tuple-element.155), channel_id=1, source_target_pairs={{0,1},{1,0},{2,3},{3,2},{4,5},{5,4},{6,7},{7,6},{8,9},{9,8},{10,11... | collective-permute-start | bytes 7077896 | tf_op jit(solution)/shard_map/ppermute | solution.py:224
  604.4 21.0 %collective-permute-start.117 = (bf16[3,2,192,384]{3,2,0,1:T(8,128)(2,1)S(1)}, bf16[3,2,192,384]{3,2,0,1:T(8,128)(2,1)S(1)}, u32[]{:S(2)}, u32[]{:S(2)}) collective-permute-start(bf16[3,2,192,384]{3,2,0,1:T(8,128)(2,1)S(1)} %fusion.82), channel_id=1, source_target_pairs={{0,16},{8,24},{16,0},{24,8},{1,17},{9,25},{17,1},{25,9},{2,18},{10... | collective-permute-start | bytes 2654216 | tf_op jit(solution)/shard_map/ppermute | solution.py:236
  629.8 26.2 %collective-permute-start.138 = (bf16[1,2,192,1536]{3,2,1,0:T(8,128)(2,1)S(1)}, bf16[1,2,192,1536]{3,2,1,0:T(8,128)(2,1)S(1)}, u32[]{:S(2)}, u32[]{:S(2)}) collective-permute-start(bf16[1,2,192,1536]{3,2,1,0:T(8,128)(2,1)S(1)} %get-tuple-element.149), channel_id=1, source_target_pairs={{0,16},{8,24},{16,0},{24,8},{1,17},{9,25},{17,1},{25,9},{2,18},{10... | collective-permute-start | bytes 3538952 | tf_op jit(solution)/shard_map/ppermute | solution.py:236
  633.3 30.8 %collective-permute-start.145 = (bf16[1,2,192,1536]{3,2,1,0:T(8,128)(2,1)S(1)}, bf16[1,2,192,1536]{3,2,1,0:T(8,128)(2,1)S(1)}, u32[]{:S(2)}, u32[]{:S(2)}) collective-permute-start(bf16[1,2,192,1536]{3,2,1,0:T(8,128)(2,1)S(1)} %get-tuple-element.153), channel_id=1, source_target_pairs={{0,8},{8,0},{16,24},{24,16},{1,9},{9,1},{17,25},{25,17},{2,10},{10... | collective-permute-start | bytes 3538952 | tf_op jit(solution)/shard_map/ppermute | solution.py:236
  678.2 18.9 %collective-permute-start.141 = (bf16[1,48,1536]{2,1,0:T(8,128)(2,1)S(1)}, bf16[1,48,1536]{2,1,0:T(8,128)(2,1)S(1)}, u32[]{:S(2)}, u32[]{:S(2)}) collective-permute-start(bf16[1,48,1536]{2,1,0:T(8,128)(2,1)S(1)} %get-tuple-element.172), channel_id=1, source_target_pairs={{0,4},{1,5},{2,6},{3,7},{4,0},{5,1},{6,2},{7,3},{8,12},{9,13},{10,... | collective-permute-start | bytes 442376 | tf_op jit(solution)/shard_map/ppermute | solution.py:224
  678.7 18.7 %collective-permute-start.147 = (bf16[1,48,1536]{2,1,0:T(8,128)(2,1)S(1)}, bf16[1,48,1536]{2,1,0:T(8,128)(2,1)S(1)}, u32[]{:S(2)}, u32[]{:S(2)}) collective-permute-start(bf16[1,48,1536]{2,1,0:T(8,128)(2,1)S(1)} %get-tuple-element.173), channel_id=1, source_target_pairs={{0,2},{1,3},{2,4},{3,5},{4,6},{5,7},{6,0},{7,1},{8,10},{9,11},{10,... | collective-permute-start | bytes 442376 | tf_op jit(solution)/shard_map/ppermute | solution.py:224
  679.0 18.4 %collective-permute-start.149 = (bf16[1,48,1536]{2,1,0:T(8,128)(2,1)S(1)}, bf16[1,48,1536]{2,1,0:T(8,128)(2,1)S(1)}, u32[]{:S(2)}, u32[]{:S(2)}) collective-permute-start(bf16[1,48,1536]{2,1,0:T(8,128)(2,1)S(1)} %get-tuple-element.174), channel_id=1, source_target_pairs={{0,6},{1,7},{2,0},{3,1},{4,2},{5,3},{6,4},{7,5},{8,14},{9,15},{10,... | collective-permute-start | bytes 442376 | tf_op jit(solution)/shard_map/ppermute | solution.py:224
  (312 other events, 2508.9 us)

commit v2 on v1

v2 whole, which is shorter than its diff:
```python
import jax
import jax.numpy as jnp
from jax import lax
from jax.experimental import pallas as pl
from jax.experimental.pallas import tpu as pltpu
from jax.sharding import PartitionSpec as P

EPSILON = 1e-06
SCALING = 0.125
NEGATIVE = -1e30
MOMENTUM = 0.5
AVERAGING = 0.5
RATE = 0.02
THRESHOLDS = (12, 16, 23, 32, 46, 64, 91)
BF = jnp.bfloat16
F32 = jnp.float32
QB = 128
DIAG = 512
SPAN = 3 * QB
VMEM = 48 * 2**20


def bucket_ids(relative):
    magnitude = jnp.abs(relative)
    bucket = jnp.minimum(magnitude, 8)
    for limit in THRESHOLDS:
        bucket = bucket + (magnitude >= limit).astype(jnp.int32)
    return bucket + 16 * (relative > 0).astype(jnp.int32)


def rms_norm(values, gain):
    return values * lax.rsqrt(jnp.mean(values * values, axis=-1, keepdims=True) + EPSILON) * gain


def dot_nn(left, right):
    return lax.dot_general(left, right, (((1,), (0,)), ((), ())), preferred_element_type=F32)


def dot_nt(left, right):
    return lax.dot_general(left, right, (((1,), (1,)), ((), ())), preferred_element_type=F32)


def dot_tn(left, right):
    return lax.dot_general(left, right, (((0,), (0,)), ((), ())), preferred_element_type=F32)


def norm_back(values, gain, upstream):
    result, pullback = jax.vjp(rms_norm, values, gain)
    return pullback(upstream)


def gelu_back(values, upstream):
    result, pullback = jax.vjp(jax.nn.gelu, values)
    return pullback(upstream)[0]


def update(weight, moment, average, gradient):
    new_moment = MOMENTUM * moment + gradient
    new_weight = weight - RATE * (gradient + MOMENTUM * new_moment)
    new_average = AVERAGING * average + (1.0 - AVERAGING) * new_weight
    return (new_moment, new_average, new_weight, new_weight.astype(BF))


def window(block, blocks):
    return max(0, block - 1) * QB, min(blocks, block + 2) * QB


def diagonal_onehot(buckets):
    place = jnp.arange(DIAG, dtype=jnp.int32)
    relative = jnp.where(place < SPAN, place, place - DIAG) - QB
    return (bucket_ids(relative)[:, None] == jnp.arange(buckets, dtype=jnp.int32)[None, :]).astype(
        F32
    )


def bias_tile(rows_ref, head):
    row = jnp.broadcast_to(rows_ref[0, head : head + 1, :], (QB, DIAG))
    return pltpu.roll(row, 0, 1, stride=1, stride_axis=0)[:, :SPAN]


def attention_kernel(q_ref, k_ref, v_ref, rows_ref, column_ref, line_ref, out_ref):
    blocks = q_ref.shape[0] // QB
    half = lax.broadcasted_iota(jnp.int32, (QB, QB), 1) < 64
    bias = [bias_tile(rows_ref, head) for head in range(2)]
    for block in range(blocks):
        low, high = window(block, blocks)
        off = low - (block - 1) * QB
        mine = pl.ds(block * QB, QB)
        query = q_ref[mine, :]
        same = column_ref[mine, :] == line_ref[:, low:high]
        outs = []
        for head in range(2):
            part = jnp.where(half if head == 0 else ~half, query, jnp.zeros((), BF))
            scores = dot_nt(part, k_ref[low:high, :]) * SCALING
            scores = jnp.where(same, scores + bias[head][:, off : off + high - low], NEGATIVE)
            expo = jnp.exp(scores - jnp.max(scores, axis=1, keepdims=True))
            probs = (expo * (1.0 / jnp.sum(expo, axis=1, keepdims=True))).astype(BF)
            outs.append(dot_nn(probs, v_ref[low:high, :]))
        out_ref[mine, :] = jnp.where(half, outs[0], outs[1]).astype(BF)


def attention_back_kernel(
    q_ref,
    k_ref,
    v_ref,
    up_ref,
    rows_ref,
    column_ref,
    line_ref,
    gq_ref,
    gk_ref,
    gv_ref,
    diag_ref,
    gk_sum,
    gv_sum,
    grid_sum,
):
    blocks = q_ref.shape[0] // QB
    lanes = lax.broadcasted_iota(jnp.int32, (QB, QB), 1)
    half = lanes < 64
    flip = (lax.broadcasted_iota(jnp.int32, (QB, QB), 0) + lanes == QB - 1).astype(BF)
    bias = [bias_tile(rows_ref, head) for head in range(2)]
    gk_sum[...] = jnp.zeros_like(gk_sum)
    gv_sum[...] = jnp.zeros_like(gv_sum)
    grid_sum[...] = jnp.zeros_like(grid_sum)
    for block in range(blocks):
        low, high = window(block, blocks)
        off = low - (block - 1) * QB
        span = high - low
        mine = pl.ds(block * QB, QB)
        query = q_ref[mine, :]
        up = up_ref[mine, :]
        same = column_ref[mine, :] == line_ref[:, low:high]
        outs = []
        gks = 0.0
        gvs = 0.0
        for head in range(2):
            keep = half if head == 0 else ~half
            query_part = jnp.where(keep, query, jnp.zeros((), BF))
            up_part = jnp.where(keep, up, jnp.zeros((), BF))
            scores = dot_nt(query_part, k_ref[low:high, :]) * SCALING
            scores = jnp.where(same, scores + bias[head][:, off : off + span], NEGATIVE)
            expo = jnp.exp(scores - jnp.max(scores, axis=1, keepdims=True))
            probs = expo * (1.0 / jnp.sum(expo, axis=1, keepdims=True))
            grad = dot_nt(up_part, v_ref[low:high, :])
            inner = jnp.sum(probs * grad, axis=1, keepdims=True)
            grad = (probs * (grad - inner)).astype(BF)
            outs.append(dot_nn(grad, k_ref[low:high, :]))
            gvs = gvs + dot_tn(probs.astype(BF), up_part)
            gks = gks + dot_tn(grad, query_part)
            grid_sum[head, :, off : off + span] += dot_nn(flip, grad)
        gk_sum[low:high, :] += gks
        gv_sum[low:high, :] += gvs
        gq_ref[mine, :] = (jnp.where(half, outs[0], outs[1]) * SCALING).astype(BF)
    gk_ref[...] = (gk_sum[...] * SCALING).astype(BF)
    gv_ref[...] = gv_sum[...].astype(BF)
    for head in range(2):
        rolled = pltpu.roll(grid_sum[head], DIAG - QB + 1, 1, stride=1, stride_axis=0)
        diag_ref[0, head : head + 1, :] = jnp.sum(rolled, axis=0, keepdims=True)


def attention_specs(length, slabs, first=0):
    slab = pl.BlockSpec((length, 128), lambda h: (0, h + first))
    rows = pl.BlockSpec((1, 2, DIAG), lambda h: (h + first, 0, 0))
    column = pl.BlockSpec((length, 1), lambda h: (0, 0))
    line = pl.BlockSpec((1, length), lambda h: (0, 0))
    out = pl.BlockSpec((length, 128), lambda h: (0, h))
    out_rows = pl.BlockSpec((1, 2, DIAG), lambda h: (h, 0, 0))
    return [slab] * slabs + [rows, column, line], out, out_rows


def attention_forward(q, k, v, rows, segment):
    length, width = q.shape
    pairs = width // 128
    specs, slab, _ = attention_specs(length, 3)
    area = 24 * 164000
    return pl.pallas_call(
        attention_kernel,
        grid=(pairs,),
        in_specs=specs,
        out_specs=slab,
        out_shape=jax.ShapeDtypeStruct((length, width), BF),
        compiler_params=pltpu.CompilerParams(vmem_limit_bytes=VMEM),
        cost_estimate=pl.CostEstimate(
            flops=20 * area * 128, bytes_accessed=8 * length * width, transcendentals=area
        ),
    )(q, k, v, rows.reshape(pairs, 2, DIAG), segment[:, None], segment[None, :])


def attention_backward(q, k, v, up, rows, segment, first, count):
    length, width = q.shape
    pairs = width // 128
    specs, slab, rows_spec = attention_specs(length, 4, first)
    shape = jax.ShapeDtypeStruct((length, count * 128), BF)
    area = 4 * count * 164000
    gq, gk, gv, diag = pl.pallas_call(
        attention_back_kernel,
        grid=(count,),
        in_specs=specs,
        out_specs=[slab] * 3 + [rows_spec],
        out_shape=[shape] * 3 + [jax.ShapeDtypeStruct((count, 2, DIAG), F32)],
        scratch_shapes=[
            pltpu.VMEM((length, 128), F32),
            pltpu.VMEM((length, 128), F32),
            pltpu.VMEM((2, QB, DIAG), F32),
        ],
        compiler_params=pltpu.CompilerParams(vmem_limit_bytes=VMEM),
        cost_estimate=pl.CostEstimate(
            flops=40 * area * 128, bytes_accessed=14 * length * width, transcendentals=area
        ),
    )(q, k, v, up, rows.reshape(pairs, 2, DIAG), segment[:, None], segment[None, :])
    return gq, gk, gv, diag.reshape(2 * count, DIAG)


def spread_heads(rows, lane_head, heads):
    parts = [jnp.where(lane_head == head, rows, 0.0) for head in range(heads)]
    return jnp.concatenate(parts, axis=0).astype(BF)


def own_turn(rows, core):
    return jnp.where(core == 0, rows, pltpu.roll(rows, rows.shape[1] // 2, 1))


def cross_setup(core_ref, query_ref, key_ref, line_ref, heads):
    core = core_ref[0]
    pairs, width = query_ref.shape
    lane_head = lax.broadcasted_iota(jnp.int32, (pairs, width), 1) // (width // heads)
    query_heads = spread_heads(own_turn(query_ref[...], core), lane_head, heads)
    scores = dot_nt(query_heads, key_ref[...]) * SCALING
    row = lax.broadcasted_iota(jnp.int32, scores.shape, 0)
    inside = lax.rem(row, pairs) == line_ref[...]
    return core, lane_head, query_heads, scores, inside


def gather_heads(rows, lane_head, heads, core):
    pairs = lane_head.shape[0]
    total = jnp.zeros(lane_head.shape, F32)
    for head in range(heads):
        total = jnp.where(lane_head == head, rows[head * pairs : (head + 1) * pairs], total)
    return own_turn(total, core)


def cross_kernel(core_ref, query_ref, key_ref, value_ref, line_ref, out_ref, *, heads):
    pairs, width = query_ref.shape
    core, lane_head, _, scores, inside = cross_setup(core_ref, query_ref, key_ref, line_ref, heads)
    scores = jnp.where(inside, scores, NEGATIVE)
    peak = jnp.max(scores, axis=1, keepdims=True)
    expo = jnp.exp(scores - peak)
    total = jnp.sum(expo, axis=1, keepdims=True)
    high = expo.astype(BF)
    low = (expo - high.astype(F32)).astype(BF)
    weighted = dot_nn(high, value_ref[...]) + dot_nn(low, value_ref[...])
    out_ref[:, :width] = gather_heads(weighted, lane_head, heads, core)
    lane = lax.broadcasted_iota(jnp.int32, (pairs, 128), 1)
    peaks = jnp.zeros((pairs, 128), F32)
    totals = jnp.ones((pairs, 128), F32)
    for head in range(heads):
        there = lane == lax.rem(head + core * (heads // 2), heads)
        part = slice(head * pairs, (head + 1) * pairs)
        peaks = jnp.where(there, peak[part], peaks)
        totals = jnp.where(there, total[part], totals)
    out_ref[:, width : width + 128] = peaks
    out_ref[:, width + 128 :] = totals


def cross_back_kernel(
    core_ref, query_ref, up_ref, stat_ref, key_ref, value_ref, line_ref, gk_ref, gv_ref, gq_ref, *, heads
):
    pairs, width = query_ref.shape
    core, lane_head, query_heads, scores, inside = cross_setup(
        core_ref, query_ref, key_ref, line_ref, heads
    )
    up_heads = spread_heads(own_turn(up_ref[...], core), lane_head, heads)
    lane = lax.broadcasted_iota(jnp.int32, (pairs, 128), 1)
    logs = []
    inners = []
    for head in range(heads):
        there = lane == lax.rem(head + core * (heads // 2), heads)
        logs.append(jnp.sum(jnp.where(there, stat_ref[:, :128], 0.0), axis=1, keepdims=True))
        inners.append(jnp.sum(jnp.where(there, stat_ref[:, 128:], 0.0), axis=1, keepdims=True))
    log = jnp.concatenate(logs, axis=0)
    inner = jnp.concatenate(inners, axis=0)
    probs = jnp.exp(jnp.where(inside, scores - log, NEGATIVE))
    grad = dot_nt(up_heads, value_ref[...])
    grad = (probs * (grad - inner)).astype(BF)
    gv_ref[...] = dot_tn(probs.astype(BF), up_heads).astype(BF)
    gk_ref[...] = (dot_tn(grad, query_heads) * SCALING).astype(BF)
    gq_ref[...] = gather_heads(dot_nn(grad, key_ref[...]), lane_head, heads, core)


def cross_forward(core, query, keys, values, segment, heads):
    pairs, width = query.shape
    vmem = pl.BlockSpec(memory_space=pltpu.VMEM)
    return pl.pallas_call(
        lambda *refs: cross_kernel(*refs, heads=heads),
        in_specs=[pl.BlockSpec(memory_space=pltpu.SMEM)] + [vmem] * 4,
        out_specs=vmem,
        out_shape=jax.ShapeDtypeStruct((pairs, width + 256), F32),
        compiler_params=pltpu.CompilerParams(vmem_limit_bytes=VMEM),
        cost_estimate=pl.CostEstimate(
            flops=6 * 96 * keys.size, bytes_accessed=4 * keys.size, transcendentals=96 * 512
        ),
    )(core.reshape(1), query, keys, values, segment[None, :])


def cross_backward(core, query, up, stat, keys, values, segment, heads):
    pairs, width = query.shape
    vmem = pl.BlockSpec(memory_space=pltpu.VMEM)
    grad = jax.ShapeDtypeStruct(keys.shape, BF)
    return pl.pallas_call(
        lambda *refs: cross_back_kernel(*refs, heads=heads),
        in_specs=[pl.BlockSpec(memory_space=pltpu.SMEM)] + [vmem] * 6,
        out_specs=[vmem] * 3,
        out_shape=[grad, grad, jax.ShapeDtypeStruct((pairs, width), F32)],
        compiler_params=pltpu.CompilerParams(vmem_limit_bytes=VMEM),
        cost_estimate=pl.CostEstimate(
            flops=10 * 96 * keys.size, bytes_accessed=8 * keys.size, transcendentals=96 * 512
        ),
    )(core.reshape(1), query, up, stat, keys, values, segment[None, :])


class Net:
    def __init__(self):
        self.n_dp = lax.axis_size("dp")
        self.n_tok = lax.axis_size("tok")
        self.n_z = self.n_tok // 2
        self.tree = self.n_dp == 4 and self.n_z == 4
        self.dp, self.tok = lax.axis_index("dp"), lax.axis_index("tok")
        self.core, self.z = self.tok % 2, self.tok // 2
        self.x, self.y = self.dp % 2, self.dp // 2

    def tok_to(self, array, where):
        return lax.ppermute(array, "tok", [(t, where(t)) for t in range(self.n_tok)])

    def swap_core(self, array):
        return self.tok_to(array, lambda t: t ^ 1)

    def shift_z(self, array, by):
        return self.tok_to(array, lambda t: (t + 2 * by) % self.n_tok)

    def flip_dp(self, array, bit):
        return lax.ppermute(array, "dp", [(d, d ^ bit) for d in range(self.n_dp)])

    def swap_x(self, array):
        return self.flip_dp(array, 1)

    def swap_y(self, array):
        return self.flip_dp(array, 2)

    def own_first(self, array, axis=-1):
        low, high = jnp.split(array, 2, axis=axis)
        flipped = jnp.concatenate([high, low], axis=axis)
        return jnp.where(self.core == 0, array, flipped)


def after(array, *others):
    if not others:
        return array
    return lax.optimization_barrier((array, *others))[0]


def place_kernel(meta_ref, *refs, plan, sources):
    outs, sems = refs[sources:-1], refs[-1]
    copies = []
    for source, row, spot, column, wide, target, flag in plan:
        top = pl.multiple_of(meta_ref[spot], 48)
        left = pl.multiple_of(meta_ref[flag[0]] * 128 + flag[1], 128)
        copies.append(
            pltpu.make_async_copy(
                refs[source].at[pl.ds(row, 48), pl.ds(column, wide)],
                outs[target].at[pl.ds(top, 48), pl.ds(left, wide)],
                sems.at[len(copies)],
            )
        )
        copies[-1].start()
    for copy in copies:
        copy.wait()


def place(net, pieces, widths, halves, own_columns, own_rows):
    spots = {}
    values = []

    def scalar(key, value):
        if key not in spots:
            spots[key] = len(values)
            values.append(jnp.asarray(value, jnp.int32))
        return spots[key]

    plan = []
    rows = 192
    for source, (array, corners, first, mine) in enumerate(pieces):
        for part, (dy, dx) in enumerate(corners):
            for block in range(4):
                for target, (half, start) in enumerate(zip(widths, halves)):
                    low = max(start, first)
                    high = min(start + half, first + array.shape[1])
                    if low >= high:
                        continue
                    flip = own_rows[target]
                    top = (net.y ^ dy ^ net.core) if flip else (net.y ^ dy)
                    spot = scalar(
                        (dy, dx, block, flip),
                        (top * 2 + (net.x ^ dx)) * rows + (net.z + 1 + block) % 4 * 48,
                    )
                    if own_columns[target]:
                        base = scalar("zero", 0)
                        shift = 0 if mine else half
                    else:
                        side = net.core if mine else 1 - net.core
                        base = scalar((mine, half), side * (half // 128))
                        shift = 0
                    plan.append(
                        (
                            source,
                            part * rows + block * 48,
                            spot,
                            low - first,
                            high - low,
                            target,
                            (base, shift + low - start),
                        )
                    )
    count = len(pieces)
    size = sum(widths) * 2 * 4 * rows
    return pl.pallas_call(
        lambda *refs: place_kernel(*refs, plan=plan, sources=count),
        in_specs=[pl.BlockSpec(memory_space=pltpu.SMEM)]
        + [pl.BlockSpec(memory_space=pl.ANY)] * count,
        out_specs=[pl.BlockSpec(memory_space=pltpu.VMEM)] * len(widths),
        out_shape=[jax.ShapeDtypeStruct((4 * rows, 2 * half), BF) for half in widths],
        scratch_shapes=[pltpu.SemaphoreType.DMA((len(plan),))],
        compiler_params=pltpu.CompilerParams(vmem_limit_bytes=VMEM),
        cost_estimate=pl.CostEstimate(flops=0, bytes_accessed=4 * size, transcendentals=0),
    )(jnp.stack(values), *[piece[0] for piece in pieces])


class Gather:
    def __init__(self, net, shards, own_columns, own_rows, cut, *ready):
        self.net, self.own_columns, self.own_rows, self.cut = net, own_columns, own_rows, cut
        self.shards = [after(shard, *ready).astype(BF) for shard in shards]
        self.widths = [shard.shape[1] // 2 for shard in shards]
        if not net.tree:
            return
        low = [shard[:, :half] for shard, half in zip(self.shards, self.widths)]
        high = [shard[:, half:] for shard, half in zip(self.shards, self.widths)]
        low, high = jnp.concatenate(low, axis=1), jnp.concatenate(high, axis=1)
        keep = jnp.where(net.core == 0, low, high)
        got = net.swap_core(jnp.where(net.core == 0, high, low))
        first = jnp.where(net.core == 0, keep, got)
        second = jnp.where(net.core == 0, got, keep)
        self.chip = jnp.concatenate([first, second], axis=0)

    def over_z(self, *ready):
        if not self.net.tree:
            return ()
        chip = after(self.chip, *ready)
        self.line = [self.net.shift_z(chip, by) for by in (3, 2, 1)] + [chip]
        return (chip,)

    def join(self, *ready):
        if not self.net.tree:
            return ()
        line = [after(part, *ready) for part in self.line]
        self.one = jnp.concatenate([part[:, : self.cut] for part in line], axis=0)
        self.two = jnp.concatenate([part[:, self.cut :] for part in line], axis=0)
        return (self.one, self.two)

    def first(self, ready=(), join=()):
        if not self.net.tree:
            return ()
        one, two = after(self.one, *ready), after(self.two, *ready)
        self.one = jnp.concatenate([one, after(self.net.swap_x(one), *join)], axis=0)
        self.two = jnp.concatenate([two, after(self.net.swap_y(two), *join)], axis=0)
        return (self.one, self.two)

    def second(self, ready=(), join=()):
        if not self.net.tree:
            return ()
        one, two = after(self.one, *ready), after(self.two, *ready)
        self.one_far = after(self.net.swap_y(one), *join)
        self.two_far = after(self.net.swap_x(two), *join)
        return (self.one_far, self.two_far)

    def finish(self):
        net = self.net
        if not net.tree:
            outs = []
            for shard, columns, rows in zip(self.shards, self.own_columns, self.own_rows):
                whole = lax.all_gather(shard, ("dp", "tok"), axis=0, tiled=True)
                whole = net.own_first(whole, 1) if columns else whole
                outs.append(net.own_first(whole, 0) if rows else whole)
            return outs
        pieces = []
        for array, corners, first in (
            (self.one, ((0, 0), (0, 1)), 0),
            (self.two, ((0, 0), (1, 0)), self.cut),
            (self.one_far, ((1, 0), (1, 1)), 0),
            (self.two_far, ((0, 1), (1, 1)), self.cut),
        ):
            pieces.append((array, corners, first, True))
            pieces.append((net.swap_core(array), corners, first, False))
        starts = [sum(self.widths[:i]) for i in range(len(self.widths))]
        return place(net, pieces, self.widths, starts, self.own_columns, self.own_rows)


def pick(array, index, axis):
    return lax.dynamic_index_in_dim(array, index, axis, keepdims=False)


def add(*parts):
    total = parts[0].astype(F32)
    for part in parts[1:]:
        total = total + part.astype(F32)
    return total


class Sum:
    def __init__(self, net, mine, theirs, cut):
        self.net, self.cut = net, cut
        self.mine, self.theirs = mine, theirs
        self.halves = [grad.shape[1] for grad in mine]
        if not net.tree:
            return
        rows, wide = mine[0].shape[0], sum(self.halves)
        self.rows, self.wide = rows, wide
        got = net.swap_core(jnp.concatenate(theirs, axis=1)).reshape(2, 2, rows // 4, wide)
        own = jnp.concatenate(mine, axis=1).reshape(2, 2, rows // 4, wide)
        self.parts = (own, got)

    def start(self, *join):
        if not self.net.tree:
            return
        own, got, cut = self.parts[0], after(self.parts[1], *join), self.cut
        one = (own[..., :cut], got[..., :cut])
        two = (own[..., cut:], got[..., cut:])
        self.one = [self.halve(one, 0, self.net.y, keep) for keep in (True, False)]
        self.two = [self.halve(two, 1, self.net.x, keep) for keep in (True, False)]

    def halve(self, parts, axis, index, keep):
        index = index if keep else 1 - index
        return add(*[pick(part, index, axis) for part in parts]).astype(BF)

    def state(self):
        return (*self.one, *self.two) if self.net.tree else ()

    def first(self, ready=(), join=()):
        if not self.net.tree:
            return
        net = self.net
        one = (self.one[0], after(net.swap_y(after(self.one[1], *ready)), *join))
        two = (self.two[0], after(net.swap_x(after(self.two[1], *ready)), *join))
        self.one = [self.halve(one, 0, net.x, keep) for keep in (True, False)]
        self.two = [self.halve(two, 0, net.y, keep) for keep in (True, False)]

    def second(self, ready=(), join=()):
        if not self.net.tree:
            return
        net = self.net
        one = (self.one[0], after(net.swap_x(after(self.one[1], *ready)), *join))
        two = (self.two[0], after(net.swap_y(after(self.two[1], *ready)), *join))
        shape = (4, self.rows // 16, -1)
        one, two = [part.reshape(shape) for part in one], [part.reshape(shape) for part in two]

        def chunk(at):
            sums = [add(*[pick(part, at, 0) for part in parts]) for parts in (one, two)]
            return jnp.concatenate(sums, axis=1)

        self.own = chunk(net.z)
        self.sent = [chunk((net.z + by) % 4).astype(BF) for by in (1, 2, 3)]

    def pending(self):
        return tuple(self.sent) if self.net.tree else ()

    def finish(self, ready=(), join=()):
        net = self.net
        if not net.tree:
            outs = []
            for mine, theirs in zip(self.mine, self.theirs):
                whole = net.own_first(jnp.concatenate([mine, theirs], axis=1), 1)
                total = lax.psum_scatter(whole, ("dp", "tok"), scatter_dimension=0, tiled=True)
                outs.append(total.astype(F32))
            return outs
        got = [
            after(net.shift_z(after(sent, *ready), by), *join)
            for by, sent in zip((1, 2, 3), self.sent)
        ]
        total = add(self.own, *got).reshape(2, self.rows // 32, self.wide)
        keep = pick(total, net.core, 0)
        other = net.swap_core(pick(total, 1 - net.core, 0))
        low = jnp.where(net.core == 0, keep, other)
        high = jnp.where(net.core == 0, other, keep)
        outs = []
        start = 0
        for half in self.halves:
            part = slice(start, start + half)
            outs.append(jnp.concatenate([low[:, part], high[:, part]], axis=1))
            start += half
        return outs


def gather_tok(net, array):
    if not net.tree:
        return lax.all_gather(array, "tok", axis=0), jnp.arange(net.n_tok, dtype=jnp.int32)
    steps = (0, 1, 2, 3)
    array = jnp.stack([array] + [net.shift_z(array, by) for by in steps[1:]])
    array = jnp.concatenate([array, net.swap_core(array)], axis=0)
    source = [(net.z - by) % 4 * 2 + net.core for by in steps]
    source += [(net.z - by) % 4 * 2 + 1 - net.core for by in steps]
    return array, jnp.stack(source).astype(jnp.int32)


def gather_dp(net, array):
    if not net.tree:
        whole = lax.all_gather(array, "dp", axis=0)
        order = net.dp ^ jnp.arange(net.n_dp, dtype=jnp.int32)
        same = order[:, None] == jnp.arange(net.n_dp, dtype=jnp.int32)[None, :]
        zero = jnp.zeros((), array.dtype)
        turned = jnp.sum(jnp.where(same[:, :, None, None], whole[None], zero), axis=1)
        return turned.reshape(-1, array.shape[1]).astype(array.dtype)
    array = jnp.concatenate([array, net.swap_x(array)], axis=0)
    return jnp.concatenate([array, net.swap_y(array)], axis=0)


def sum_small(net, array):
    bit = 1
    while bit < net.n_tok:
        array = array + net.tok_to(array, lambda t, bit=bit: t ^ bit)
        bit *= 2
    bit = 1
    while bit < net.n_dp:
        array = array + net.flip_dp(array, bit)
        bit *= 2
    return array


def per_device(
    encoder_input,
    decoder_input,
    output_cotangent,
    pair_lengths,
    pair_offset,
    pair_query,
    attention_master,
    attention_moment,
    attention_average,
    feedforward_master,
    feedforward_moment,
    feedforward_average,
    decoder_master,
    decoder_moment,
    decoder_average,
    expansion_master,
    expansion_moment,
    expansion_average,
    gain_master,
    gain_moment,
    gain_average,
    bias_master,
    bias_moment,
    bias_average,
):
    net = Net()
    length = encoder_input.shape[1]
    width = encoder_input.shape[2]
    buckets, heads = bias_master.shape
    head_size = width // heads
    pairs = pair_lengths.shape[1]
    nquery = decoder_input.shape[0]

    half = width // 2
    wide = feedforward_master.shape[2] // 2
    att = [attention_master[i] for i in range(6)]
    feed = [feedforward_master[i] for i in range(2)]
    dec = [decoder_master[i] for i in range(4)]
    expand = [expansion_master[i] for i in range(2)]
    get_att = Gather(net, att[:4], [True] * 3 + [False], [False] * 3 + [True], 2 * half)
    chip = get_att.over_z()
    both = jnp.concatenate([decoder_input, output_cotangent], axis=1)
    got, source = gather_tok(net, both)
    spot = source[None, :] == jnp.arange(net.n_tok, dtype=jnp.int32)[:, None]
    ordered = jnp.sum(jnp.where(spot[:, :, None, None], got[None], jnp.zeros((), BF)), axis=1)
    ordered = gather_dp(net, ordered.astype(BF).reshape(net.n_tok * nquery, 2 * width))
    get_feed = Gather(net, feed, [True] * 2, [False] * 2, wide, *chip)
    step = get_att.join()
    get_feed.over_z(*step)
    get_att.first((ordered,))
    step_att = get_att.second()
    get_dec = Gather(net, att[4:] + dec, [True] * 2 + [False] * 4, [False] * 6, 3 * half, *step)
    get_exp = Gather(net, expand, [True] * 2, [False] * 2, wide, *step)
    step_feed = get_feed.join(*step_att)
    get_dec.over_z(*step_feed)
    w_q, w_k, w_v, w_out = get_att.finish()

    counter = jnp.arange(pairs, dtype=jnp.int32)
    hidden = encoder_input[0].astype(F32)
    lengths = pair_lengths[0]
    ends = jnp.sum(jnp.where(counter[:, None] <= counter[None, :], lengths[:, None], 0), axis=0)
    position = jnp.arange(length, dtype=jnp.int32)
    segment = jnp.sum((position[:, None] >= ends[None, :]).astype(jnp.int32), axis=1)
    onehot = diagonal_onehot(buckets)
    bias_rows = jnp.sum(bias_master.T[:, None, :] * onehot[None], axis=2)
    bias_rows = net.own_first(bias_rows, 0)

    normed = rms_norm(hidden, gain_master[0]).astype(BF)
    queries, keys, values = (dot_nn(normed, weight).astype(BF) for weight in (w_q, w_k, w_v))
    feed_half = get_feed.first(join=(queries, keys, values))
    attended = attention_forward(after(queries, *feed_half), keys, values, bias_rows, segment)
    residual = hidden + dot_nn(attended, w_out)
    normed_two = rms_norm(residual, gain_master[1]).astype(BF)
    step_two = get_feed.second(join=(normed_two,))
    step_dec = get_dec.join(*step_two)
    get_exp.over_z(*step_dec)
    w_up, w_down = get_feed.finish()
    inner = dot_nn(normed_two, w_up)
    activated = jax.nn.gelu(inner).astype(BF)
    dec_half = get_dec.first(join=(activated,))
    encoded = (residual + dot_nt(after(activated, *dec_half), w_down)).astype(BF)
    step_three = get_dec.second(join=(encoded,))
    w_ck, w_cv, e_zero, e_one, e_two, e_three = get_dec.finish()
    cross_keys = dot_nn(encoded, w_ck).astype(BF)
    cross_values = dot_nn(encoded, w_cv).astype(BF)
    get_exp.join(*step_three)

    state = ordered[:, :width].astype(F32)
    up_low = ordered[:, width:]
    upstream = up_low.astype(F32)
    group = net.n_tok * nquery
    total_rows = state.shape[0]
    row_id = jnp.arange(total_rows, dtype=jnp.int32)
    own_row = (row_id // nquery == net.tok)[:, None]

    def own_rows(rows):
        return lax.dynamic_slice_in_dim(rows, net.tok * nquery, nquery, axis=0)

    self_in = rms_norm(state, gain_master[2]).astype(BF)
    self_values = dot_nn(self_in, e_zero).astype(BF)
    after_self = state + dot_nn(self_values, e_one)
    cross_in = rms_norm(after_self, gain_master[3]).astype(BF)
    cross_query = dot_nn(cross_in, e_two).astype(BF)

    offsets = pair_offset[0]
    owners = pair_query[0]
    query_id = jnp.arange(group, dtype=jnp.int32)
    own_id = (net.tok + offsets) % net.n_tok * nquery + owners
    own_match = own_id[:, None] == query_id[None, :]

    def at_pairs(rows):
        return jnp.sum(jnp.where(own_match[:, :, None], rows[None, :group].astype(F32), 0.0), axis=1)

    pair_match = (source[:, None] + offsets[None, :]) % net.n_tok * nquery + owners[None, :]
    pair_match = pair_match.reshape(1, -1) == query_id[:, None]

    def sum_pairs(rows):
        return lax.dot_general(
            pair_match.astype(F32),
            rows,
            (((1,), (0,)), ((), ())),
            precision=lax.Precision.HIGHEST,
            preferred_element_type=F32,
        )

    exp_half = get_exp.first(join=(cross_query, cross_keys, cross_values))
    pair_queries = at_pairs(after(cross_query, *exp_half))
    partial = cross_forward(net.core, pair_queries, cross_keys, cross_values, segment, heads)
    get_exp.second(join=(partial,))
    got, _ = gather_tok(net, partial)
    got = got.reshape(-1, width + 256)
    pair_peak = got[:, width : width + heads]
    pair_total = got[:, width + 128 : width + 128 + heads]
    row_peak = jnp.max(jnp.where(pair_match[:, :, None], pair_peak[None], NEGATIVE), axis=1)
    factor = jnp.where(pair_match[:, :, None], jnp.exp(pair_peak[None] - row_peak[:, None]), 0.0)
    row_total = jnp.sum(factor * pair_total[None], axis=1)
    factor = jnp.sum(factor / row_total[:, None], axis=0)
    cross_wide = sum_pairs(got[:, :width] * jnp.repeat(factor, head_size, axis=1))
    row_log = row_peak + jnp.log(row_total)
    cross_out = gather_dp(net, cross_wide.astype(BF))

    after_cross = after_self + dot_nn(cross_out, e_three)
    final_in = rms_norm(after_cross, gain_master[4]).astype(BF)
    x_up, x_down = get_exp.finish()
    grad_act = dot_nn(up_low, x_down)
    final_inner = dot_nn(final_in, x_up)
    grad_inner = gelu_back(final_inner, grad_act).astype(BF)
    grad_final_in = dot_nt(grad_inner, x_up)

    def decoder_norm_back(values, gain, up):
        grad, _ = norm_back(values, gain, up)
        _, grad_gain = norm_back(values, gain, jnp.where(own_row, up, 0.0))
        return grad, grad_gain

    grad_state_four, grad_gain_four = decoder_norm_back(after_cross, gain_master[4], grad_final_in)
    grad_cross_total = upstream + grad_state_four
    cross_grad_low = grad_cross_total.astype(BF)
    grad_cross_out = dot_nt(cross_grad_low, e_three)[:group].astype(BF).astype(F32)
    row_inner = jnp.sum((grad_cross_out * cross_wide).reshape(group, heads, head_size), axis=2)
    empty = jnp.zeros((group, 128 - heads), F32)
    back = at_pairs(jnp.concatenate([grad_cross_out, row_log, empty, row_inner, empty], axis=1))
    final_act = jax.nn.gelu(final_inner).astype(BF)
    decoder_output = own_rows(after_cross + dot_nt(final_act, x_down))

    grad_keys_cross, grad_values_cross, grad_query_part = cross_backward(
        net.core,
        pair_queries,
        back[:, :width],
        back[:, width:],
        cross_keys,
        cross_values,
        segment,
        heads,
    )
    grad_encoded = (dot_nt(grad_keys_cross, w_ck) + dot_nt(grad_values_cross, w_cv)).astype(BF)

    grad_down = [
        dot_tn(grad_encoded, part).astype(BF) for part in (activated[:, :wide], activated[:, wide:])
    ]
    crosses = [
        dot_tn(encoded, grad_keys_cross).astype(BF),
        dot_tn(encoded, grad_values_cross).astype(BF),
    ]
    down = Sum(
        net,
        [grad_down[0], *[grad[:, :half] for grad in crosses]],
        [grad_down[1], *[grad[:, half:] for grad in crosses]],
        3 * half,
    )
    grad_activated = dot_nn(after(grad_encoded, *grad_down, *crosses), w_down)
    grad_inner_enc = gelu_back(inner, grad_activated).astype(BF)
    down.start(grad_inner_enc)
    grad_inner_enc = after(grad_inner_enc, *down.state())
    grad_up = [
        dot_tn(normed_two, part).astype(BF)
        for part in (grad_inner_enc[:, :wide], grad_inner_enc[:, wide:])
    ]
    grad_normed_two = dot_nt(after(grad_inner_enc, *grad_up), w_up)
    grad_resid, grad_gain_one = norm_back(residual, gain_master[1], grad_normed_two)
    grad_residual = grad_encoded.astype(F32) + grad_resid
    attn_low = grad_residual.astype(BF)
    grad_out = dot_tn(net.own_first(attended), net.own_first(attn_low)).astype(BF)
    middle = Sum(
        net,
        [grad_up[0], grad_out[:, :half]],
        [grad_up[1], grad_out[:, half:]],
        7 * half // 3,
    )
    grad_attended = dot_nt(after(attn_low, grad_out), w_out).astype(BF)
    down.first(join=(grad_attended,))
    middle.start(grad_attended)
    grad_attended = after(grad_attended, *middle.state(), *down.state())
    blocks = width // 256

    def attention_part(up, first):
        grads = attention_backward(queries, keys, values, up, bias_rows, segment, first, blocks)
        return grads[:3], [dot_tn(normed, grad).astype(BF) for grad in grads[:3]], grads[3]

    their_grads, their_qkv, their_diagonals = attention_part(grad_attended, blocks)
    down.second(join=their_qkv)
    middle.first(join=their_qkv)
    own_up = after(grad_attended, *their_qkv, *down.pending(), *middle.state())
    own_grads, own_qkv, own_diagonals = attention_part(own_up, 0)
    last = Sum(net, own_qkv, their_qkv, 5 * half // 3)
    sum_down, sum_ck, sum_cv = down.finish(join=own_qkv)
    middle.second(join=own_qkv)
    diagonals = jnp.concatenate([own_diagonals, their_diagonals], axis=0)
    grad_normed = sum(
        dot_nt(jnp.concatenate([after(own, *own_qkv), their], axis=1), weight)
        for own, their, weight in zip(own_grads, their_grads, (w_q, w_k, w_v))
    )
    last.start(grad_normed)
    grad_input_part, grad_gain_zero = norm_back(hidden, gain_master[0], grad_normed)
    encoder_gradient = (grad_residual + grad_input_part)[None]

    got, _ = gather_tok(net, after(grad_query_part, *their_qkv))
    got = after(got, grad_normed)
    grad_query_cross = (sum_pairs(got.reshape(-1, width)) * SCALING).astype(BF)
    grad_query_cross = after(gather_dp(net, grad_query_cross), *last.state())
    grad_cross_in = dot_nt(grad_query_cross, e_two)
    grad_state_three, grad_gain_three = decoder_norm_back(
        after_self, gain_master[3], grad_cross_in
    )
    grad_self_total = grad_cross_total + grad_state_three
    self_grad_low = grad_self_total.astype(BF)
    grad_self_values = dot_nt(self_grad_low, e_one).astype(BF)
    grad_self_in = dot_nt(grad_self_values, e_zero)
    grad_state_two, grad_gain_two = decoder_norm_back(state, gain_master[2], grad_self_in)
    decoder_gradient = own_rows(grad_self_total + grad_state_two)
    own = decoder_master.shape[1]
    rank = net.dp * net.n_tok + net.tok

    def own_weight_rows(left, right):
        return dot_tn(lax.dynamic_slice_in_dim(left, rank * own, own, axis=1), right)

    grad_dec = jnp.stack(
        [
            own_weight_rows(self_in, grad_self_values),
            own_weight_rows(self_values, self_grad_low),
            own_weight_rows(cross_in, grad_query_cross),
            own_weight_rows(cross_out, cross_grad_low),
        ]
    )
    grad_exp = jnp.stack(
        [
            net.own_first(own_weight_rows(final_in, grad_inner)),
            net.own_first(own_weight_rows(up_low, final_act)),
        ]
    )

    last.first(join=(decoder_gradient,))
    sum_up, sum_out = middle.finish(join=(decoder_gradient,))
    last.second(join=(grad_dec, grad_exp))
    sum_q, sum_k, sum_v = last.finish()
    grad_table = jnp.dot(
        net.own_first(diagonals, 0),
        onehot,
        precision=lax.Precision.HIGHEST,
        preferred_element_type=F32,
    ).T
    gain_grad = jnp.concatenate(
        [grad_gain_zero, grad_gain_one, grad_gain_two, grad_gain_three, grad_gain_four]
    )
    small = sum_small(net, jnp.concatenate([gain_grad, grad_table.reshape(-1)]))
    gain_sum = small[: 5 * width].reshape(5, width)
    bias_sum = small[5 * width :].reshape(buckets, heads)

    results = [decoder_output, encoder_gradient, decoder_gradient]
    groups = (
        (
            attention_master,
            attention_moment,
            attention_average,
            jnp.stack([sum_q, sum_k, sum_v, sum_out, sum_ck, sum_cv]),
        ),
        (
            feedforward_master,
            feedforward_moment,
            feedforward_average,
            jnp.stack([sum_up, sum_down]),
        ),
        (decoder_master, decoder_moment, decoder_average, grad_dec),
        (expansion_master, expansion_moment, expansion_average, grad_exp),
        (gain_master, gain_moment, gain_average, gain_sum),
        (bias_master, bias_moment, bias_average, bias_sum),
    )
    for weight, moment, average, gradient in groups:
        results.extend(update(weight, moment, average, gradient))
    return tuple(results)


def solution(mesh):
    spread = P(("dp", "tok"), None)
    weights = P(None, ("dp", "tok"), None)
    in_specs = (
        P(("dp", "tok"), None, None),
        spread,
        spread,
        spread,
        P("dp", None),
        P("dp", None),
        *[weights] * 12,
        *[P()] * 6,
    )
    out_specs = (spread, P(("dp", "tok"), None, None), spread, *[weights] * 16, *[P()] * 8)
    return jax.shard_map(
        per_device, mesh=mesh, in_specs=in_specs, out_specs=out_specs, check_vma=False
    )
```

time: 713 us -> 489 us (0.69)
  waiting for transfers between devices: 260 us -> 107 us
  starting transfers between devices: 148 us -> 104 us
  matrix products: 90 us -> 68.3 us
  local copies, waits for them, and re-layouts: 78.9 us -> 68.5 us
    ppermute x124 -> x62, waiting for transfers between devices: 107 us -> 23.8 us  [tok_to(): lax.ppermute(array, 'tok', [(t, where(t)) for t in range(self.n_tok)])]
    ppermute x38 -> x36, waiting for transfers between devices: 154 us -> 83.3 us  [flip_dp(): return lax.ppermute(array, 'dp', [(d, d ^ bit) for d in range(self.n_dp)])]
    ppermute x124 -> x62, starting transfers between devices: 114 us -> 62.3 us  [tok_to(): lax.ppermute(array, 'tok', [(t, where(t)) for t in range(self.n_tok)])]
    dot_general x16 -> x14, matrix products: 33.6 us -> 17.3 us  [dot_nt(): lax.dot_general(left, right, (((1,), (1,)), ((), ())), preferred_element_...]
    concatenate x15 -> x17, local copies, waits for them, and re-layouts: 16.8 us -> 6.17 us  [the longest x4 2.29 us: first(): jnp.concatenate([two, after(self.net.swap_y(two), *join)], axis=0)]
    ppermute x38 -> x36, starting transfers between devices: 34.1 us -> 41.2 us  [flip_dp(): return lax.ppermute(array, 'dp', [(d, d ^ bit) for d in range(self.n_dp)])]
    dot_general x16 -> x19, matrix products: 23.8 us -> 18.9 us  [dot_tn(): lax.dot_general(left, right, (((0,), (0,)), ((), ())), preferred_element_...]
    unnamed x442 -> x398, local copies, waits for them, and re-layouts: 27.8 us -> 32.5 us
  transfers between devices with their start and end apart: 162 -> 98, of which waited for: 58 -> 33; matrix products, arithmetic and copies ran while one was open for 18% -> 30% of each run, Pallas kernels for 6% -> 14%
where the time goes in v2:
time: 489 us; the launch traced here: 487 us
  waiting for transfers between devices  107 us (22%)
  starting transfers between devices  104 us (21%)
  Pallas kernels  76.7 us (16%)
  local copies, waits for them, and re-layouts  68.5 us (14%)
  matrix products  68.3 us (14%)
  other arithmetic  57.7 us (12%)
    ppermute x36, waiting for transfers between devices, flip_dp(): return lax.ppermute(array, 'dp', [(d, d ^ bit) for d in range(self.n_dp)])  83.3 us
    ppermute x62, starting transfers between devices, tok_to(): lax.ppermute(array, 'tok', [(t, where(t)) for t in range(self.n_tok)])  62.3 us
    ppermute x36, starting transfers between devices, flip_dp(): return lax.ppermute(array, 'dp', [(d, d ^ bit) for d in range(self.n_dp)])  41.2 us
    unnamed x398, local copies, waits for them, and re-layouts  32.5 us
    pallas_call x4, Pallas kernels, place(): pl.pallas_call(lambda *refs: place_kernel(*refs, plan=plan, sources=count...  30.2 us
    dot_general x14, matrix products, dot_nn(): lax.dot_general(left, right, (((1,), (0,)), ((), ())), preferred_element_...  29.8 us
    pallas_call x2, Pallas kernels, attention_backward(): pl.pallas_call(attention_back_kernel, grid=(count,), in_specs=specs, out_...  27.1 us
    ppermute x62, waiting for transfers between devices, tok_to(): lax.ppermute(array, 'tok', [(t, where(t)) for t in range(self.n_tok)])  23.8 us
  transfers between devices with their start and end apart: 98, of which 33 were waited for; matrix products, arithmetic and copies ran while one was open for 30% of the time, Pallas kernels for 14%

profile of v2, /device:TPU:0, one launch (start us, length us, event | category | flops | bytes accessed | tf_op | source)
XLA Modules:
  0.0 486.5 jit_solution(1761228884309097271)
XLA Ops:
  2.2 3.0 collective-permute-start
  5.2 2.6 collective-permute-start.1
  22.4 2.8 collective-permute-start.7
  27.0 3.7 collective-permute-done.5
  32.4 3.1 collective-permute-done.8
  36.4 2.6 collective-permute-start.12
  39.0 2.0 collective-permute-start.17
  43.5 7.2 %collective-permute-done.15 = bf16[192,768]{1,0:T(8,128)(2,1)S(1)} collective-permute-done((bf16[192,768]{1,0:T(8,128)(2,1)S(1)}, bf16[192,768]{1,0:T(8,128)(2,1)S(1)}, u32[]{:S(2)}, u32[]{:S(2)}) %collective-permute-start.15) | collective-permute-done | bytes 294944 | tf_op jit(solution)/shard_map/ppermute | solution.py:342
  53.9 11.6 %collective-permute-done.14.refs_5_ = bf16[384,768]{1,0:T(8,128)(2,1)S(1)} collective-permute-done((bf16[384,768]{1,0:T(8,128)(2,1)S(1)}, bf16[384,768]{1,0:T(8,128)(2,1)S(1)}, u32[]{:S(2)}, u32[]{:S(2)}) %collective-permute-start.14) | collective-permute-done | bytes 589856 | tf_op jit(solution)/shard_map/ppermute | solution.py:342
  70.9 2.1 collective-permute-start.29
  73.0 5.2 %shard_map.439 = (bf16[768,768]{1,0:T(8,128)(2,1)S(1)}, bf16[768,768]{1,0:T(8,128)(2,1)}, bf16[768,768]{1,0:T(8,128)(2,1)}, bf16[768,768]{1,0:T(8,128)(2,1)}) custom-call(s32[35]{0:T(128)S(1)} %stack.337.refs_0_, bf16[384,768]{1,0:T(8,128)(2,1)S(1)} %constant_dynamic-update-slice_fusion.22.refs_1_, bf16[384,768]{1,0:T(8,128)(2,1)S(1)} %collective-permute-done.21.refs_2_, ...), custom_call_target="tpu_custom_call" | custom-call | bytes 9437184 | tf_op jit(solution)/shard_map/pallas_call | solution.py:426
  85.5 17.4 %shard_map.440 = bf16[512,768]{1,0:T(8,128)(2,1)S(1)} custom-call(bf16[512,768]{1,0:T(8,128)(2,1)S(1)} %convolution_convert_fusion.12.q_ref, bf16[512,768]{1,0:T(8,128)(2,1)S(1)} %convolution_convert_fusion.11.k_ref, bf16[512,768]{1,0:T(8,128)(2,1)S(1)} %convolution_convert_fusion.10.v_ref, f32[6,2,512]{2,1,0:T(2,128)S(1)} %select_n.633.rows_ref, ...), custom_call_target="tpu_custom_call" | custom-call | flops 10076160000 | bytes 3145728 | tf_op jit(solution)/shard_map/pallas_call | solution.py:177
  104.0 6.3 %collective-permute-done.25.refs_5_ = bf16[384,1536]{1,0:T(8,128)(2,1)S(1)} collective-permute-done((bf16[384,1536]{1,0:T(8,128)(2,1)S(1)}, bf16[384,1536]{1,0:T(8,128)(2,1)S(1)}, u32[]{:S(2)}, u32[]{:S(2)}) %collective-permute-start.25) | collective-permute-done | bytes 1179680 | tf_op jit(solution)/shard_map/ppermute | solution.py:342
  119.3 8.2 %shard_map.441 = (bf16[768,3072]{1,0:T(8,128)(2,1)}, bf16[768,3072]{1,0:T(8,128)(2,1)}) custom-call(s32[17]{0:T(128)S(1)} %stack.338.refs_0_, bf16[384,1536]{1,0:T(8,128)(2,1)S(1)} %constant_dynamic-update-slice_fusion.26.refs_1_, bf16[384,1536]{1,0:T(8,128)(2,1)S(1)} %collective-permute-done.31.refs_2_, ...), custom_call_target="tpu_custom_call" | custom-call | bytes 18874368 | tf_op jit(solution)/shard_map/pallas_call | solution.py:426
  127.5 8.3 %multiply_convert_fusion = (bf16[512,3072]{1,0:T(8,128)(2,1)S(1)}, f32[512,3072]{1,0:T(8,128)}) fusion(bf16[512,768]{1,0:T(8,128)(2,1)S(1)} %multiply_convert_fusion.1, bf16[768,3072]{1,0:T(8,128)(2,1)} %get-tuple-element.156), kind=kOutput, calls=%fused_computation.9 | convolution fusion | flops 2430074880 | bytes 14942208 | tf_op jit(solution)/shard_map/dot_general | solution.py:36
  141.1 2.6 collective-permute-start.43
  143.7 2.7 add_convert_fusion.5
  146.4 11.2 %collective-permute-done.38.refs_5_ = bf16[384,1152]{1,0:T(8,128)(2,1)S(1)} collective-permute-done((bf16[384,1152]{1,0:T(8,128)(2,1)S(1)}, bf16[384,1152]{1,0:T(8,128)(2,1)S(1)}, u32[]{:S(2)}, u32[]{:S(2)}) %collective-permute-start.38) | collective-permute-done | bytes 884768 | tf_op jit(solution)/shard_map/ppermute | solution.py:342
  157.6 1.9 collective-permute-done.40.refs_7_
  160.0 2.7 collective-permute-done.44
  168.2 8.3 %shard_map.442 = (bf16[768,768]{1,0:T(8,128)(2,1)}, bf16[768,768]{1,0:T(8,128)(2,1)}, bf16[768,768]{1,0:T(8,128)(2,1)}, bf16[768,768]{1,0:T(8,128)(2,1)}, bf16[7...) custom-call(s32[19]{0:T(128)S(1)} %stack.320.refs_0_, bf16[384,1152]{1,0:T(8,128)(2,1)S(1)} %constant_dynamic-update-slice_fusion.36.refs_1_, ...), custom_call_target="tpu_custom_call" | custom-call | bytes 14155776 | tf_op jit(solution)/shard_map/pallas_call | solution.py:426
  184.6 6.0 %collective-permute-start.48 = (f32[8,1024]{1,0:T(8,128)S(1)}, f32[8,1024]{1,0:T(8,128)S(1)}, u32[]{:S(2)}, u32[]{:S(2)}) collective-permute-start(f32[8,1024]{1,0:T(8,128)S(1)} %shard_map.443), channel_id=1, source_target_pairs={{0,2},{1,3},{2,4},{3,5},{4,6},{5,7},{6,0},{7,1},{8,10},{9,11},{10,... | collective-permute-start | bytes 98312 | tf_op jit(solution)/shard_map/ppermute | solution.py:333
  191.6 12.6 %collective-permute-start.50 = (f32[8,1024]{1,0:T(8,128)S(1)}, f32[8,1024]{1,0:T(8,128)S(1)}, u32[]{:S(2)}, u32[]{:S(2)}) collective-permute-start(f32[8,1024]{1,0:T(8,128)S(1)} %shard_map.443), channel_id=1, source_target_pairs={{0,6},{1,7},{2,0},{3,1},{4,2},{5,3},{6,4},{7,5},{8,14},{9,15},{10,... | collective-permute-start | bytes 98312 | tf_op jit(solution)/shard_map/ppermute | solution.py:333
  219.3 1.8 reshape.684
  224.1 7.5 %collective-permute-done.56.refs_5_ = bf16[384,1536]{1,0:T(8,128)(2,1)} collective-permute-done((bf16[384,1536]{1,0:T(8,128)(2,1)S(1)}, bf16[384,1536]{1,0:T(8,128)(2,1)}, u32[]{:S(2)}, u32[]{:S(2)}) %collective-permute-start.56) | collective-permute-done | bytes 1179680 | tf_op jit(solution)/shard_map/ppermute | solution.py:342
  239.7 1.9 collective-permute-done.53
  244.9 8.4 %shard_map.444 = (bf16[768,3072]{1,0:T(8,128)(2,1)}, bf16[768,3072]{1,0:T(8,128)(2,1)}) custom-call(s32[17]{0:T(128)S(1)} %stack.338.refs_0_, bf16[384,1536]{1,0:T(8,128)(2,1)S(1)} %constant_dynamic-update-slice_fusion.46.refs_1_, bf16[384,1536]{1,0:T(8,128)(2,1)} %collective-permute-done.54.refs_2_, ...), custom_call_target="tpu_custom_call" | custom-call | bytes 18874368 | tf_op jit(solution)/shard_map/pallas_call | solution.py:426
  253.3 3.4 fusion.204
  259.4 2.3 multiply_reduce_fusion.4
  281.0 7.4 %fusion.6 = bf16[512,3072]{1,0:T(8,128)(2,1)} fusion(f32[512,3072]{1,0:T(8,128)S(1)} %bitcast.445, bf16[512,768]{1,0:T(8,128)(2,1)S(1)} %add_convert_fusion.4, bf16[768,3072]{1,0:T(8,128)(2,1)S(1)} %bitcast.442), kind=kOutput, calls=%fused_computation.8 | convolution fusion | flops 2447376384 | bytes 14942208 | tf_op jit(solution)/shard_map/dot_general | solution.py:36
  294.4 3.4 multiply_reduce_fusion
  311.6 15.7 %collective-permute-done.62 = bf16[2,192,1152]{2,1,0:T(8,128)(2,1)S(1)} collective-permute-done((bf16[2,192,1152]{2,1,0:T(8,128)(2,1)S(1)}, bf16[2,192,1152]{2,1,0:T(8,128)(2,1)S(1)}, u32[]{:S(2)}, u32[]{:S(2)}) %collective-permute-start.62) | collective-permute-done | bytes 884768 | tf_op jit(solution)/shard_map/ppermute | solution.py:342
  335.9 13.7 %shard_map.446 = (bf16[512,384]{1,0:T(8,128)(2,1)S(1)}, bf16[512,384]{1,0:T(8,128)(2,1)S(1)}, bf16[512,384]{1,0:T(8,128)(2,1)S(1)}, f32[3,2,512]{2,1,0:T(2,128)S(1)}) custom-call(bf16[512,768]{1,0:T(8,128)(2,1)S(1)} %copy-done.9, bf16[512,768]{1,0:T(8,128)(2,1)S(1)} %copy-done.11, bf16[512,768]{1,0:T(8,128)(2,1)S(1)} %copy-done.14, ...), custom_call_target="tpu_custom_call" | custom-call | flops 10076160000 | bytes 5505024 | tf_op jit(solution)/shard_map/pallas_call | solution.py:196
  352.0 1.9 collective-permute-start.69
  370.7 2.3 fusion.60
  374.5 2.3 fusion.55
  376.8 13.4 %shard_map.447 = (bf16[512,384]{1,0:T(8,128)(2,1)S(1)}, bf16[512,384]{1,0:T(8,128)(2,1)S(1)}, bf16[512,384]{1,0:T(8,128)(2,1)S(1)}, f32[3,2,512]{2,1,0:T(2,128)S(1)}) custom-call(bf16[512,768]{1,0:T(8,128)(2,1)S(1)} %copy-done.9, bf16[512,768]{1,0:T(8,128)(2,1)S(1)} %copy-done.12, bf16[512,768]{1,0:T(8,128)(2,1)S(1)} %copy-done.15, ...), custom_call_target="tpu_custom_call" | custom-call | flops 10076160000 | bytes 5505024 | tf_op jit(solution)/shard_map/pallas_call | solution.py:196
  397.5 1.9 fusion.14
  407.3 2.2 copy.127
  420.2 2.1 collective-permute-start.87
  424.5 2.9 copy.128
  437.0 1.9 collective-permute-done.86
  445.2 2.2 collective-permute-done.94
  449.1 2.9 collective-permute-done.95
  453.3 2.5 collective-permute-done.96
  456.7 2.9 collective-permute-done.97
  468.5 3.2 collective-permute-done.78
  478.2 4.6 collective-permute-done.80
  (861 shorter events, 233.1 us)
Async XLA Ops:
  2.2 15.9 %collective-permute-start = (bf16[2,1536]{1,0:T(2,128)(2,1)S(1)}, bf16[2,1536]{1,0:T(2,128)(2,1)S(1)}, u32[]{:S(2)}, u32[]{:S(2)}) collective-permute-start(bf16[2,1536]{1,0:T(2,128)(2,1)S(1)} %constant_dynamic-update-slice_fusion), channel_id=1, source_target_pairs={{0,2},{1,3},{2,4},{3,5},{4,6},{5,7},{6,0},{7,1},{8,10},{9,11},{10,... | collective-permute-start | bytes 18440 | tf_op jit(solution)/shard_map/ppermute | solution.py:333
  36.4 17.4 %collective-permute-start.12 = (bf16[48,3072]{1,0:T(8,128)(2,1)S(1)}, bf16[48,3072]{1,0:T(8,128)(2,1)S(1)}, u32[]{:S(2)}, u32[]{:S(2)}) collective-permute-start(bf16[48,3072]{1,0:T(8,128)(2,1)S(1)} %pad_maximum_fusion.16), channel_id=1, source_target_pairs={{0,6},{1,7},{2,0},{3,1},{4,2},{5,3},{6,4},{7,5},{8,14},{9,15},{10,... | collective-permute-start | bytes 884744 | tf_op jit(solution)/shard_map/ppermute | solution.py:333
  39.0 27.9 %collective-permute-start.17 = (bf16[48,3072]{1,0:T(8,128)(2,1)S(1)}, bf16[48,3072]{1,0:T(8,128)(2,1)S(1)}, u32[]{:S(2)}, u32[]{:S(2)}) collective-permute-start(bf16[48,3072]{1,0:T(8,128)(2,1)S(1)} %pad_maximum_fusion.16), channel_id=1, source_target_pairs={{0,4},{1,5},{2,6},{3,7},{4,0},{5,1},{6,2},{7,3},{8,12},{9,13},{10,... | collective-permute-start | bytes 884744 | tf_op jit(solution)/shard_map/ppermute | solution.py:333
  42.9 24.0 %collective-permute-start.18 = (bf16[48,3072]{1,0:T(8,128)(2,1)S(1)}, bf16[48,3072]{1,0:T(8,128)(2,1)S(1)}, u32[]{:S(2)}, u32[]{:S(2)}) collective-permute-start(bf16[48,3072]{1,0:T(8,128)(2,1)S(1)} %pad_maximum_fusion.16), channel_id=1, source_target_pairs={{0,2},{1,3},{2,4},{3,5},{4,6},{5,7},{6,0},{7,1},{8,10},{9,11},{10,... | collective-permute-start | bytes 884744 | tf_op jit(solution)/shard_map/ppermute | solution.py:333
  50.6 14.9 %collective-permute-start.14 = (bf16[384,768]{1,0:T(8,128)(2,1)S(1)}, bf16[384,768]{1,0:T(8,128)(2,1)S(1)}, u32[]{:S(2)}, u32[]{:S(2)}) collective-permute-start(bf16[384,768]{1,0:T(8,128)(2,1)S(1)} %constant_dynamic-update-slice_fusion.22.refs_1_), channel_id=1, source_target_pairs={{0,16},{8,24},{16,0},{24,8},{1,17},{9,25},{17,1},{25,9},{2,18},{10... | collective-permute-start | bytes 1769480 | tf_op jit(solution)/shard_map/ppermute | solution.py:342
  53.8 15.5 %collective-permute-start.21 = (bf16[384,768]{1,0:T(8,128)(2,1)S(1)}, bf16[384,768]{1,0:T(8,128)(2,1)S(1)}, u32[]{:S(2)}, u32[]{:S(2)}) collective-permute-start(bf16[384,768]{1,0:T(8,128)(2,1)S(1)} %constant_dynamic-update-slice_fusion.22.refs_1_), channel_id=1, source_target_pairs={{0,1},{1,0},{2,3},{3,2},{4,5},{5,4},{6,7},{7,6},{8,9},{9,8},{10,11... | collective-permute-start | bytes 1769480 | tf_op jit(solution)/shard_map/ppermute | solution.py:333
  67.7 15.4 %collective-permute-start.20 = (bf16[192,1536]{1,0:T(8,128)(2,1)S(1)}, bf16[192,1536]{1,0:T(8,128)(2,1)S(1)}, u32[]{:S(2)}, u32[]{:S(2)}) collective-permute-start(bf16[192,1536]{1,0:T(8,128)(2,1)S(1)} %pad_maximum_fusion.6), channel_id=1, source_target_pairs={{0,8},{8,0},{16,24},{24,16},{1,9},{9,1},{17,25},{25,17},{2,10},{10... | collective-permute-start | bytes 1769480 | tf_op jit(solution)/shard_map/ppermute | solution.py:342
  69.3 15.1 %collective-permute-start.26 = (bf16[192,1536]{1,0:T(8,128)(2,1)S(1)}, bf16[192,1536]{1,0:T(8,128)(2,1)S(1)}, u32[]{:S(2)}, u32[]{:S(2)}) collective-permute-start(bf16[192,1536]{1,0:T(8,128)(2,1)S(1)} %pad_maximum_fusion.7), channel_id=1, source_target_pairs={{0,16},{8,24},{16,0},{24,8},{1,17},{9,25},{17,1},{25,9},{2,18},{10... | collective-permute-start | bytes 1769480 | tf_op jit(solution)/shard_map/ppermute | solution.py:342
  70.1 41.3 %collective-permute-start.19 = (bf16[48,2304]{1,0:T(8,128)(2,1)S(1)}, bf16[48,2304]{1,0:T(8,128)(2,1)S(1)}, u32[]{:S(2)}, u32[]{:S(2)}) collective-permute-start(bf16[48,2304]{1,0:T(8,128)(2,1)S(1)} %pad_maximum_fusion.19), channel_id=1, source_target_pairs={{0,6},{1,7},{2,0},{3,1},{4,2},{5,3},{6,4},{7,5},{8,14},{9,15},{10,... | collective-permute-start | bytes 663560 | tf_op jit(solution)/shard_map/ppermute | solution.py:333
  70.9 41.0 %collective-permute-start.28 = (bf16[48,2304]{1,0:T(8,128)(2,1)S(1)}, bf16[48,2304]{1,0:T(8,128)(2,1)S(1)}, u32[]{:S(2)}, u32[]{:S(2)}) collective-permute-start(bf16[48,2304]{1,0:T(8,128)(2,1)S(1)} %pad_maximum_fusion.19), channel_id=1, source_target_pairs={{0,4},{1,5},{2,6},{3,7},{4,0},{5,1},{6,2},{7,3},{8,12},{9,13},{10,... | collective-permute-start | bytes 663560 | tf_op jit(solution)/shard_map/ppermute | solution.py:333
  70.9 41.1 %collective-permute-start.29 = (bf16[48,2304]{1,0:T(8,128)(2,1)S(1)}, bf16[48,2304]{1,0:T(8,128)(2,1)S(1)}, u32[]{:S(2)}, u32[]{:S(2)}) collective-permute-start(bf16[48,2304]{1,0:T(8,128)(2,1)S(1)} %pad_maximum_fusion.19), channel_id=1, source_target_pairs={{0,2},{1,3},{2,4},{3,5},{4,6},{5,7},{6,0},{7,1},{8,10},{9,11},{10,... | collective-permute-start | bytes 663560 | tf_op jit(solution)/shard_map/ppermute | solution.py:333
  83.1 27.2 %collective-permute-start.25 = (bf16[384,1536]{1,0:T(8,128)(2,1)S(1)}, bf16[384,1536]{1,0:T(8,128)(2,1)S(1)}, u32[]{:S(2)}, u32[]{:S(2)}) collective-permute-start(bf16[384,1536]{1,0:T(8,128)(2,1)S(1)} %constant_dynamic-update-slice_fusion.26.refs_1_), channel_id=1, source_target_pairs={{0,16},{8,24},{16,0},{24,8},{1,17},{9,25},{17,1},{25,9},{2,18},{10... | collective-permute-start | bytes 3538952 | tf_op jit(solution)/shard_map/ppermute | solution.py:342
  84.5 26.9 %collective-permute-start.27 = (bf16[384,1536]{1,0:T(8,128)(2,1)S(1)}, bf16[384,1536]{1,0:T(8,128)(2,1)S(1)}, u32[]{:S(2)}, u32[]{:S(2)}) collective-permute-start(bf16[384,1536]{1,0:T(8,128)(2,1)S(1)} %constant_dynamic-update-slice_fusion.31.refs_3_), channel_id=1, source_target_pairs={{0,8},{8,0},{16,24},{24,16},{1,9},{9,1},{17,25},{25,17},{2,10},{10... | collective-permute-start | bytes 3538952 | tf_op jit(solution)/shard_map/ppermute | solution.py:342
  112.4 23.4 %collective-permute-start.30 = (bf16[192,1152]{1,0:T(8,128)(2,1)S(1)}, bf16[192,1152]{1,0:T(8,128)(2,1)S(1)}, u32[]{:S(2)}, u32[]{:S(2)}) collective-permute-start(bf16[192,1152]{1,0:T(8,128)(2,1)S(1)} %pad_maximum_fusion.12), channel_id=1, source_target_pairs={{0,8},{8,0},{16,24},{24,16},{1,9},{9,1},{17,25},{25,17},{2,10},{10... | collective-permute-start | bytes 1327112 | tf_op jit(solution)/shard_map/ppermute | solution.py:342
  113.4 23.2 %collective-permute-start.36 = (bf16[192,1152]{1,0:T(8,128)(2,1)S(1)}, bf16[192,1152]{1,0:T(8,128)(2,1)}, u32[]{:S(2)}, u32[]{:S(2)}) collective-permute-start(bf16[192,1152]{1,0:T(8,128)(2,1)S(1)} %pad_maximum_fusion.13), channel_id=1, source_target_pairs={{0,16},{8,24},{16,0},{24,8},{1,17},{9,25},{17,1},{25,9},{2,18},{10... | collective-permute-start | bytes 1327112 | tf_op jit(solution)/shard_map/ppermute | solution.py:342
  135.9 21.8 %collective-permute-start.38 = (bf16[384,1152]{1,0:T(8,128)(2,1)S(1)}, bf16[384,1152]{1,0:T(8,128)(2,1)S(1)}, u32[]{:S(2)}, u32[]{:S(2)}) collective-permute-start(bf16[384,1152]{1,0:T(8,128)(2,1)S(1)} %constant_dynamic-update-slice_fusion.36.refs_1_), channel_id=1, source_target_pairs={{0,16},{8,24},{16,0},{24,8},{1,17},{9,25},{17,1},{25,9},{2,18},{10... | collective-permute-start | bytes 2654216 | tf_op jit(solution)/shard_map/ppermute | solution.py:342
  137.9 21.5 %collective-permute-start.40 = (bf16[384,1152]{1,0:T(8,128)(2,1)S(1)}, bf16[384,1152]{1,0:T(8,128)(2,1)S(1)}, u32[]{:S(2)}, u32[]{:S(2)}) collective-permute-start(bf16[384,1152]{1,0:T(8,128)(2,1)S(1)} %constant_dynamic-update-slice_fusion.41.refs_3_), channel_id=1, source_target_pairs={{0,8},{8,0},{16,24},{24,16},{1,9},{9,1},{17,25},{25,17},{2,10},{10... | collective-permute-start | bytes 2654216 | tf_op jit(solution)/shard_map/ppermute | solution.py:342
  139.5 20.0 %collective-permute-start.45 = (bf16[48,3072]{1,0:T(8,128)(2,1)S(1)}, bf16[48,3072]{1,0:T(8,128)(2,1)S(1)}, u32[]{:S(2)}, u32[]{:S(2)}) collective-permute-start(bf16[48,3072]{1,0:T(8,128)(2,1)S(1)} %pad_maximum_fusion.17), channel_id=1, source_target_pairs={{0,2},{1,3},{2,4},{3,5},{4,6},{5,7},{6,0},{7,1},{8,10},{9,11},{10,... | collective-permute-start | bytes 884744 | tf_op jit(solution)/shard_map/ppermute | solution.py:333
  139.6 23.1 %collective-permute-start.44 = (bf16[48,3072]{1,0:T(8,128)(2,1)S(1)}, bf16[48,3072]{1,0:T(8,128)(2,1)S(1)}, u32[]{:S(2)}, u32[]{:S(2)}) collective-permute-start(bf16[48,3072]{1,0:T(8,128)(2,1)S(1)} %pad_maximum_fusion.17), channel_id=1, source_target_pairs={{0,4},{1,5},{2,6},{3,7},{4,0},{5,1},{6,2},{7,3},{8,12},{9,13},{10,... | collective-permute-start | bytes 884744 | tf_op jit(solution)/shard_map/ppermute | solution.py:333
  141.1 21.6 %collective-permute-start.43 = (bf16[48,3072]{1,0:T(8,128)(2,1)S(1)}, bf16[48,3072]{1,0:T(8,128)(2,1)S(1)}, u32[]{:S(2)}, u32[]{:S(2)}) collective-permute-start(bf16[48,3072]{1,0:T(8,128)(2,1)S(1)} %pad_maximum_fusion.17), channel_id=1, source_target_pairs={{0,6},{1,7},{2,0},{3,1},{4,2},{5,3},{6,4},{7,5},{8,14},{9,15},{10,... | collective-permute-start | bytes 884744 | tf_op jit(solution)/shard_map/ppermute | solution.py:333
  165.6 16.4 %collective-permute-start.46 = (bf16[192,1536]{1,0:T(8,128)(2,1)S(1)}, bf16[192,1536]{1,0:T(8,128)(2,1)S(1)}, u32[]{:S(2)}, u32[]{:S(2)}) collective-permute-start(bf16[192,1536]{1,0:T(8,128)(2,1)S(1)} %pad_maximum_fusion.8), channel_id=1, source_target_pairs={{0,8},{8,0},{16,24},{24,16},{1,9},{9,1},{17,25},{25,17},{2,10},{10... | collective-permute-start | bytes 1769480 | tf_op jit(solution)/shard_map/ppermute | solution.py:342
  166.2 15.8 %collective-permute-start.47 = (bf16[192,1536]{1,0:T(8,128)(2,1)S(1)}, bf16[192,1536]{1,0:T(8,128)(2,1)S(1)}, u32[]{:S(2)}, u32[]{:S(2)}) collective-permute-start(bf16[192,1536]{1,0:T(8,128)(2,1)S(1)} %pad_maximum_fusion.9), channel_id=1, source_target_pairs={{0,16},{8,24},{16,0},{24,8},{1,17},{9,25},{17,1},{25,9},{2,18},{10... | collective-permute-start | bytes 1769480 | tf_op jit(solution)/shard_map/ppermute | solution.py:342
  182.0 62.9 %collective-permute-start.54 = (bf16[384,1536]{1,0:T(8,128)(2,1)S(1)}, bf16[384,1536]{1,0:T(8,128)(2,1)}, u32[]{:S(2)}, u32[]{:S(2)}) collective-permute-start(bf16[384,1536]{1,0:T(8,128)(2,1)S(1)} %constant_dynamic-update-slice_fusion.46.refs_1_), channel_id=1, source_target_pairs={{0,1},{1,0},{2,3},{3,2},{4,5},{5,4},{6,7},{7,6},{8,9},{9,8},{10,11... | collective-permute-start | bytes 3538952 | tf_op jit(solution)/shard_map/ppermute | solution.py:333
  183.0 61.9 %collective-permute-start.55 = (bf16[384,1536]{1,0:T(8,128)(2,1)}, bf16[384,1536]{1,0:T(8,128)(2,1)}, u32[]{:S(2)}, u32[]{:S(2)}) collective-permute-start(bf16[384,1536]{1,0:T(8,128)(2,1)} %constant_dynamic-update-slice_fusion.51.refs_3_), channel_id=1, source_target_pairs={{0,1},{1,0},{2,3},{3,2},{4,5},{5,4},{6,7},{7,6},{8,9},{9,8},{10,11... | collective-permute-start | bytes 3538952 | tf_op jit(solution)/shard_map/ppermute | solution.py:333
  184.6 19.6 %collective-permute-start.48 = (f32[8,1024]{1,0:T(8,128)S(1)}, f32[8,1024]{1,0:T(8,128)S(1)}, u32[]{:S(2)}, u32[]{:S(2)}) collective-permute-start(f32[8,1024]{1,0:T(8,128)S(1)} %shard_map.443), channel_id=1, source_target_pairs={{0,2},{1,3},{2,4},{3,5},{4,6},{5,7},{6,0},{7,1},{8,10},{9,11},{10,... | collective-permute-start | bytes 98312 | tf_op jit(solution)/shard_map/ppermute | solution.py:333
  191.6 15.1 %collective-permute-start.50 = (f32[8,1024]{1,0:T(8,128)S(1)}, f32[8,1024]{1,0:T(8,128)S(1)}, u32[]{:S(2)}, u32[]{:S(2)}) collective-permute-start(f32[8,1024]{1,0:T(8,128)S(1)} %shard_map.443), channel_id=1, source_target_pairs={{0,6},{1,7},{2,0},{3,1},{4,2},{5,3},{6,4},{7,5},{8,14},{9,15},{10,... | collective-permute-start | bytes 98312 | tf_op jit(solution)/shard_map/ppermute | solution.py:333
  204.2 27.4 %collective-permute-start.56 = (bf16[384,1536]{1,0:T(8,128)(2,1)S(1)}, bf16[384,1536]{1,0:T(8,128)(2,1)}, u32[]{:S(2)}, u32[]{:S(2)}) collective-permute-start(bf16[384,1536]{1,0:T(8,128)(2,1)S(1)} %constant_dynamic-update-slice_fusion.46.refs_1_), channel_id=1, source_target_pairs={{0,16},{8,24},{16,0},{24,8},{1,17},{9,25},{17,1},{25,9},{2,18},{10... | collective-permute-start | bytes 3538952 | tf_op jit(solution)/shard_map/ppermute | solution.py:342
  205.3 27.6 %collective-permute-start.58 = (bf16[384,1536]{1,0:T(8,128)(2,1)}, bf16[384,1536]{1,0:T(8,128)(2,1)}, u32[]{:S(2)}, u32[]{:S(2)}) collective-permute-start(bf16[384,1536]{1,0:T(8,128)(2,1)} %constant_dynamic-update-slice_fusion.51.refs_3_), channel_id=1, source_target_pairs={{0,8},{8,0},{16,24},{24,16},{1,9},{9,1},{17,25},{25,17},{2,10},{10... | collective-permute-start | bytes 3538952 | tf_op jit(solution)/shard_map/ppermute | solution.py:342
  271.3 17.1 %collective-permute-start.60 = (bf16[768,2304]{1,0:T(8,128)(2,1)S(1)}, bf16[768,2304]{1,0:T(8,128)(2,1)S(1)}, u32[]{:S(2)}, u32[]{:S(2)}) collective-permute-start(bf16[768,2304]{1,0:T(8,128)(2,1)S(1)} %pad_maximum_fusion.1), channel_id=1, source_target_pairs={{0,1},{1,0},{2,3},{3,2},{4,5},{5,4},{6,7},{7,6},{8,9},{9,8},{10,11... | collective-permute-start | bytes 10616840 | tf_op jit(solution)/shard_map/ppermute | solution.py:333
  301.4 29.5 %collective-permute-start.61 = (bf16[768,1920]{1,0:T(8,128)(2,1)S(1)}, bf16[768,1920]{1,0:T(8,128)(2,1)S(1)}, u32[]{:S(2)}, u32[]{:S(2)}) collective-permute-start(bf16[768,1920]{1,0:T(8,128)(2,1)S(1)} %pad_maximum_fusion.3), channel_id=1, source_target_pairs={{0,1},{1,0},{2,3},{3,2},{4,5},{5,4},{6,7},{7,6},{8,9},{9,8},{10,11... | collective-permute-start | bytes 8847368 | tf_op jit(solution)/shard_map/ppermute | solution.py:333
  305.3 22.0 %collective-permute-start.62 = (bf16[2,192,1152]{2,1,0:T(8,128)(2,1)S(1)}, bf16[2,192,1152]{2,1,0:T(8,128)(2,1)S(1)}, u32[]{:S(2)}, u32[]{:S(2)}) collective-permute-start(bf16[2,192,1152]{2,1,0:T(8,128)(2,1)S(1)} %get-tuple-element.315), channel_id=1, source_target_pairs={{0,16},{8,24},{16,0},{24,8},{1,17},{9,25},{17,1},{25,9},{2,18},{10... | collective-permute-start | bytes 2654216 | tf_op jit(solution)/shard_map/ppermute | solution.py:342
  306.2 21.7 %collective-permute-start.63 = (bf16[2,192,1152]{2,1,0:T(8,128)(2,1)S(1)}, bf16[2,192,1152]{2,1,0:T(8,128)(2,1)S(1)}, u32[]{:S(2)}, u32[]{:S(2)}) collective-permute-start(bf16[2,192,1152]{2,1,0:T(8,128)(2,1)S(1)} %fusion.24), channel_id=1, source_target_pairs={{0,8},{8,0},{16,24},{24,16},{1,9},{9,1},{17,25},{25,17},{2,10},{10... | collective-permute-start | bytes 2654216 | tf_op jit(solution)/shard_map/ppermute | solution.py:342
  328.1 23.8 %collective-permute-start.65 = (bf16[192,1152]{1,0:T(8,128)(2,1)S(1)}, bf16[192,1152]{1,0:T(8,128)(2,1)S(1)}, u32[]{:S(2)}, u32[]{:S(2)}) collective-permute-start(bf16[192,1152]{1,0:T(8,128)(2,1)S(1)} %get-tuple-element.325), channel_id=1, source_target_pairs={{0,16},{8,24},{16,0},{24,8},{1,17},{9,25},{17,1},{25,9},{2,18},{10... | collective-permute-start | bytes 1327112 | tf_op jit(solution)/shard_map/ppermute | solution.py:342
  329.5 26.3 %collective-permute-start.64 = (bf16[192,1152]{1,0:T(8,128)(2,1)S(1)}, bf16[192,1152]{1,0:T(8,128)(2,1)S(1)}, u32[]{:S(2)}, u32[]{:S(2)}) collective-permute-start(bf16[192,1152]{1,0:T(8,128)(2,1)S(1)} %get-tuple-element.323), channel_id=1, source_target_pairs={{0,8},{8,0},{16,24},{24,16},{1,9},{9,1},{17,25},{25,17},{2,10},{10... | collective-permute-start | bytes 1327112 | tf_op jit(solution)/shard_map/ppermute | solution.py:342
  333.0 36.0 %collective-permute-start.66 = (bf16[2,192,896]{2,1,0:T(8,128)(2,1)}, bf16[2,192,896]{2,1,0:T(8,128)(2,1)}, u32[]{:S(2)}, u32[]{:S(2)}) collective-permute-start(bf16[2,192,896]{2,1,0:T(8,128)(2,1)} %get-tuple-element.319), channel_id=1, source_target_pairs={{0,16},{8,24},{16,0},{24,8},{1,17},{9,25},{17,1},{25,9},{2,18},{10... | collective-permute-start | bytes 2064392 | tf_op jit(solution)/shard_map/ppermute | solution.py:342
  335.3 37.7 %collective-permute-start.67 = (bf16[2,192,1024]{2,1,0:T(8,128)(2,1)}, bf16[2,192,1024]{2,1,0:T(8,128)(2,1)}, u32[]{:S(2)}, u32[]{:S(2)}) collective-permute-start(bf16[2,192,1024]{2,1,0:T(8,128)(2,1)} %fusion.36), channel_id=1, source_target_pairs={{0,8},{8,0},{16,24},{24,16},{1,9},{9,1},{17,25},{25,17},{2,10},{10... | collective-permute-start | bytes 2359304 | tf_op jit(solution)/shard_map/ppermute | solution.py:342
  361.6 62.9 %collective-permute-start.74 = (bf16[768,1152]{0,1:T(8,128)(2,1)}, bf16[768,1152]{0,1:T(8,128)(2,1)}, u32[]{:S(2)}, u32[]{:S(2)}) collective-permute-start(bf16[768,1152]{0,1:T(8,128)(2,1)} %pad_maximum_fusion.5), channel_id=1, source_target_pairs={{0,1},{1,0},{2,3},{3,2},{4,5},{5,4},{6,7},{7,6},{8,9},{9,8},{10,11... | collective-permute-start | bytes 5308424 | tf_op jit(solution)/shard_map/ppermute | solution.py:333
  361.6 37.8 %collective-permute-start.91 = (bf16[48,2304]{1,0:T(8,128)(2,1)}, bf16[48,2304]{1,0:T(8,128)(2,1)}, u32[]{:S(2)}, u32[]{:S(2)}) collective-permute-start(bf16[48,2304]{1,0:T(8,128)(2,1)} %pad_maximum_fusion.22), channel_id=1, source_target_pairs={{0,6},{1,7},{2,0},{3,1},{4,2},{5,3},{6,4},{7,5},{8,14},{9,15},{10,... | collective-permute-start | bytes 663560 | tf_op jit(solution)/shard_map/ppermute | solution.py:333
  366.9 33.7 %collective-permute-start.90 = (bf16[48,2304]{1,0:T(8,128)(2,1)}, bf16[48,2304]{1,0:T(8,128)(2,1)}, u32[]{:S(2)}, u32[]{:S(2)}) collective-permute-start(bf16[48,2304]{1,0:T(8,128)(2,1)} %pad_maximum_fusion.21), channel_id=1, source_target_pairs={{0,4},{1,5},{2,6},{3,7},{4,0},{5,1},{6,2},{7,3},{8,12},{9,13},{10,... | collective-permute-start | bytes 663560 | tf_op jit(solution)/shard_map/ppermute | solution.py:333
  368.9 32.6 %collective-permute-start.89 = (bf16[48,2304]{1,0:T(8,128)(2,1)}, bf16[48,2304]{1,0:T(8,128)(2,1)}, u32[]{:S(2)}, u32[]{:S(2)}) collective-permute-start(bf16[48,2304]{1,0:T(8,128)(2,1)} %pad_maximum_fusion.20), channel_id=1, source_target_pairs={{0,2},{1,3},{2,4},{3,5},{4,6},{5,7},{6,0},{7,1},{8,10},{9,11},{10,... | collective-permute-start | bytes 663560 | tf_op jit(solution)/shard_map/ppermute | solution.py:333
  373.0 42.9 %collective-permute-start.83 = (bf16[192,896]{1,0:T(8,128)(2,1)}, bf16[192,896]{1,0:T(8,128)(2,1)}, u32[]{:S(2)}, u32[]{:S(2)}) collective-permute-start(bf16[192,896]{1,0:T(8,128)(2,1)} %get-tuple-element.329), channel_id=1, source_target_pairs={{0,8},{8,0},{16,24},{24,16},{1,9},{9,1},{17,25},{25,17},{2,10},{10... | collective-permute-start | bytes 1032200 | tf_op jit(solution)/shard_map/ppermute | solution.py:342
  399.4 18.3 %collective-permute-start.84 = (bf16[192,1024]{1,0:T(8,128)(2,1)}, bf16[192,1024]{1,0:T(8,128)(2,1)}, u32[]{:S(2)}, u32[]{:S(2)}) collective-permute-start(bf16[192,1024]{1,0:T(8,128)(2,1)} %get-tuple-element.327), channel_id=1, source_target_pairs={{0,16},{8,24},{16,0},{24,8},{1,17},{9,25},{17,1},{25,9},{2,18},{10... | collective-permute-start | bytes 1179656 | tf_op jit(solution)/shard_map/ppermute | solution.py:342
  420.2 15.8 %collective-permute-start.87 = (bf16[48,1920]{1,0:T(8,128)(2,1)}, bf16[48,1920]{1,0:T(8,128)(2,1)}, u32[]{:S(2)}, u32[]{:S(2)}) collective-permute-start(bf16[48,1920]{1,0:T(8,128)(2,1)} %pad_maximum_fusion.26), channel_id=1, source_target_pairs={{0,6},{1,7},{2,0},{3,1},{4,2},{5,3},{6,4},{7,5},{8,14},{9,15},{10,... | collective-permute-start | bytes 552968 | tf_op jit(solution)/shard_map/ppermute | solution.py:333
  423.0 15.9 %collective-permute-start.86 = (bf16[48,1920]{1,0:T(8,128)(2,1)}, bf16[48,1920]{1,0:T(8,128)(2,1)}, u32[]{:S(2)}, u32[]{:S(2)}) collective-permute-start(bf16[48,1920]{1,0:T(8,128)(2,1)} %pad_maximum_fusion.25), channel_id=1, source_target_pairs={{0,4},{1,5},{2,6},{3,7},{4,0},{5,1},{6,2},{7,3},{8,12},{9,13},{10,... | collective-permute-start | bytes 552968 | tf_op jit(solution)/shard_map/ppermute | solution.py:333
  423.7 17.3 %collective-permute-start.85 = (bf16[48,1920]{1,0:T(8,128)(2,1)}, bf16[48,1920]{1,0:T(8,128)(2,1)}, u32[]{:S(2)}, u32[]{:S(2)}) collective-permute-start(bf16[48,1920]{1,0:T(8,128)(2,1)} %pad_maximum_fusion.24), channel_id=1, source_target_pairs={{0,2},{1,3},{2,4},{3,5},{4,6},{5,7},{6,0},{7,1},{8,10},{9,11},{10,... | collective-permute-start | bytes 552968 | tf_op jit(solution)/shard_map/ppermute | solution.py:333
  428.6 36.1 %collective-permute-start.77 = (bf16[2,192,512]{2,1,0:T(8,128)(2,1)}, bf16[2,192,512]{2,1,0:T(8,128)(2,1)}, u32[]{:S(2)}, u32[]{:S(2)}) collective-permute-start(bf16[2,192,512]{2,1,0:T(8,128)(2,1)} %fusion.69), channel_id=1, source_target_pairs={{0,8},{8,0},{16,24},{24,16},{1,9},{9,1},{17,25},{25,17},{2,10},{10... | collective-permute-start | bytes 1179656 | tf_op jit(solution)/shard_map/ppermute | solution.py:342
  431.2 35.7 %collective-permute-start.75 = (bf16[2,192,640]{2,1,0:T(8,128)(2,1)}, bf16[2,192,640]{2,1,0:T(8,128)(2,1)S(1)}, u32[]{:S(2)}, u32[]{:S(2)}) collective-permute-start(bf16[2,192,640]{2,1,0:T(8,128)(2,1)} %get-tuple-element.321), channel_id=1, source_target_pairs={{0,16},{8,24},{16,0},{24,8},{1,17},{9,25},{17,1},{25,9},{2,18},{10... | collective-permute-start | bytes 1474568 | tf_op jit(solution)/shard_map/ppermute | solution.py:342
  443.0 20.7 %collective-permute-start.88 = (f32[24,1920]{1,0:T(8,128)}, f32[24,1920]{1,0:T(8,128)}, u32[]{:S(2)}, u32[]{:S(2)}) collective-permute-start(f32[24,1920]{1,0:T(8,128)} %dynamic-slice_bitcast_fusion.1), channel_id=1, source_target_pairs={{0,1},{1,0},{2,3},{3,2},{4,5},{5,4},{6,7},{7,6},{8,9},{9,8},{10,11... | collective-permute-start | bytes 552968 | tf_op jit(solution)/shard_map/ppermute | solution.py:333
  (228 other events, 2402.5 us)
